TPU v7x, 256 devices: a whole 4x4x8 slice. The times are simulated.
256 devices in a mesh: dom: 64 (over z, y, core), batch: 4 (over x).
Axes of the slice: x: 4, y: 4, z: 8, core: 2. Of those that a mesh axis runs over, the one named last changes fastest.
Arguments:
- signal: bfloat16 [32768, 4, 4, 256], P('dom', 'batch'), may hold values from -6 to 6
- cotangent: bfloat16 [32768, 4, 3, 256], P('dom', 'batch'), may hold values from -6 to 6
- conv_weight: bfloat16 [2, 2, 256, 256], replicated, may hold values from -0.25 to 0.25
- mix_weight: bfloat16 [3, 256, 256], replicated, may hold values from -0.21875 to 0.21875
- send_rows: int32 [4096, 2], P('dom'), may hold values from 0 to 511
- send_mask: int32 [4096, 2], P('dom'), may hold values 0 or 1
- tile_vals: bfloat16 [1024, 128, 128], P('dom'), may hold values from -0.26953125 to 0.26953125
- tile_row: int32 [1024], P('dom'), may hold values from 0 to 3
- tile_col: int32 [1024], P('dom'), may hold values from 0 to 5
- tile_mask: int32 [1024], P('dom'), may hold values 0 or 1
- hub_owner: int32 [8], replicated, may hold values from 0 to 63, as said below
- hub_rows: int32 [8, 16], replicated, may hold values from 0 to 511
Outputs:
- layer_out: bfloat16 [32768, 4, 3, 256], P('dom', 'batch')
- signal_grad: bfloat16 [32768, 4, 4, 256], P('dom', 'batch')
- conv_grad: float32 [2, 2, 256, 256], replicated
- mix_grad: float32 [3, 256, 256], replicated
Inputs may be any that keep to these rules, and one draw needn't show every extreme that they name: `hub_owner`: each owner slot names a different partition.
All inputs are finite; a program needn't handle non-finite values. No bound on the sum of `send_mask` or of `tile_mask` on one device may be relied on, other than what follows from the above.
Results may differ from a plain program's by a relative error of at most 0.0056.
Values may be sent and summed in bfloat16 or wider, within the bound.
No kernel may reach another device: no remote copies, remote signals or barrier semaphores. Data moves between devices by JAX's collectives and lax.ppermute only.
A program may use at most 128 MiB of HBM per device.

v0:
```python
import math

import jax
import jax.numpy as jnp
from jax import lax
from jax.sharding import PartitionSpec as P

highest = lax.Precision.HIGHEST


def from_root(block, axis, holder):
    block = jnp.where(lax.axis_index(axis) == holder, block, jnp.zeros_like(block))
    return lax.psum(block, axis)


def tile_apply(ext_rows, tile_block, row_ids, col_ids, tile_keep, row_tiles):
    block_rows = tile_block.shape[1]
    features = ext_rows.shape[1]
    chosen = ext_rows.reshape(-1, block_rows, features)[col_ids]
    product = jnp.einsum("tij,tjf->tif", tile_block, chosen, preferred_element_type=jnp.float32)
    product = product * tile_keep[:, None, None]
    onehot = (row_ids[None, :] == jnp.arange(row_tiles, dtype=jnp.int32)[:, None]).astype(
        jnp.float32
    )
    return jnp.einsum("rt,tif->rif", onehot, product, precision=highest).reshape(
        row_tiles * block_rows, features
    )


def tile_back(own_rows, tile_block, row_ids, col_ids, tile_keep, col_tiles):
    block_rows = tile_block.shape[1]
    features = own_rows.shape[1]
    chosen = own_rows.reshape(-1, block_rows, features)[row_ids]
    product = jnp.einsum("tji,tjf->tif", tile_block, chosen, preferred_element_type=jnp.float32)
    product = product * tile_keep[:, None, None]
    onehot = (col_ids[None, :] == jnp.arange(col_tiles, dtype=jnp.int32)[:, None]).astype(
        jnp.float32
    )
    return jnp.einsum("ct,tif->cif", onehot, product, precision=highest).reshape(
        col_tiles * block_rows, features
    )


def mm(left, right):
    return jnp.dot(left, right, preferred_element_type=jnp.float32)


def inner_sum(left, right):
    return lax.dot_general(
        left, right, (((0,), (0,)), ((), ())), preferred_element_type=jnp.float32
    )


def body(
    signal,
    cotangent,
    conv_weight,
    mix_weight,
    send_rows,
    send_mask,
    tile_vals,
    tile_row,
    tile_col,
    tile_mask,
    hub_owner,
    hub_rows,
):
    node_dev, b_dev, steps, chans = signal.shape
    out_steps = steps - 1
    block_rows = tile_vals.shape[1]
    features = b_dev * out_steps * chans
    halo_count = send_rows.shape[0] * send_rows.shape[1]
    hub_count = hub_rows.shape[0] * hub_rows.shape[1]
    ext_count = node_dev + halo_count + hub_count
    my_index = lax.axis_index("dom")
    flat_send = send_rows.reshape(-1)
    send_flag = send_mask.reshape(-1)
    keep_send = send_flag.astype(jnp.bfloat16)
    flat_hub = hub_rows.reshape(-1)
    mine = jnp.repeat(hub_owner, hub_rows.shape[1]) == my_index
    positions = jnp.arange(node_dev, dtype=jnp.int32)
    return_halo = ((positions[:, None] == flat_send[None, :]) & (send_flag[None, :] == 1)).astype(
        jnp.float32
    )
    return_hub = ((positions[:, None] == flat_hub[None, :]) & mine[None, :]).astype(jnp.float32)
    tile_keep = tile_mask.astype(jnp.float32)

    def spread(field):
        outgoing = field[flat_send] * keep_send[:, None]
        incoming = lax.all_to_all(outgoing, "dom", split_axis=0, concat_axis=0, tiled=True)
        panels = []
        for owner_slot in range(hub_rows.shape[0]):
            panel = field[hub_rows[owner_slot]]
            panels.append(from_root(panel, "dom", hub_owner[owner_slot]))
        hubs = jnp.concatenate(panels, 0)
        ext_rows = jnp.concatenate([field, incoming, hubs], 0)
        return tile_apply(
            ext_rows, tile_vals, tile_row, tile_col, tile_keep, node_dev // block_rows
        )

    def gather_back(field):
        ext_grad = tile_back(
            field, tile_vals, tile_row, tile_col, tile_keep, ext_count // block_rows
        )
        returned = lax.all_to_all(
            ext_grad[node_dev : node_dev + halo_count].astype(jnp.bfloat16),
            "dom",
            split_axis=0,
            concat_axis=0,
            tiled=True,
        ).astype(jnp.float32)
        summed = lax.psum(ext_grad[node_dev + halo_count :], "dom")
        local = ext_grad[:node_dev] + jnp.dot(return_halo, returned, precision=highest)
        return local + jnp.dot(return_hub, summed, precision=highest)

    earlier = signal[:, :, :-1, :].reshape(-1, chans)
    later = signal[:, :, 1:, :].reshape(-1, chans)
    filt = mm(earlier, conv_weight[0, 0]) + mm(later, conv_weight[0, 1])
    gate = mm(earlier, conv_weight[1, 0]) + mm(later, conv_weight[1, 1])
    tanh_filt = jnp.tanh(filt)
    sig_gate = jax.nn.sigmoid(gate)
    hidden = (tanh_filt * sig_gate).astype(jnp.bfloat16)
    hop_one = spread(hidden.reshape(node_dev, features)).astype(jnp.bfloat16)
    hop_two = spread(hop_one).astype(jnp.bfloat16)
    hop_one = hop_one.reshape(-1, chans)
    hop_two = hop_two.reshape(-1, chans)
    mixed = (
        later.astype(jnp.float32)
        + mm(hidden, mix_weight[0])
        + mm(hop_one, mix_weight[1])
        + mm(hop_two, mix_weight[2])
    )
    layer_out = mixed.astype(jnp.bfloat16).reshape(node_dev, b_dev, out_steps, chans)
    grad_out = cotangent.reshape(-1, chans)
    mix_part = jnp.stack(
        [inner_sum(hidden, grad_out), inner_sum(hop_one, grad_out), inner_sum(hop_two, grad_out)]
    )
    back_two = mm(grad_out, mix_weight[2].T).astype(jnp.bfloat16)
    back_one = mm(grad_out, mix_weight[1].T) + gather_back(
        back_two.reshape(node_dev, features)
    ).reshape(-1, chans)
    back_one = back_one.astype(jnp.bfloat16)
    grad_hidden = mm(grad_out, mix_weight[0].T) + gather_back(
        back_one.reshape(node_dev, features)
    ).reshape(-1, chans)
    grad_filt = (grad_hidden * sig_gate * (1.0 - tanh_filt * tanh_filt)).astype(jnp.bfloat16)
    grad_gate = (grad_hidden * tanh_filt * sig_gate * (1.0 - sig_gate)).astype(jnp.bfloat16)
    conv_part = jnp.stack(
        [
            jnp.stack([inner_sum(earlier, grad_filt), inner_sum(later, grad_filt)]),
            jnp.stack([inner_sum(earlier, grad_gate), inner_sum(later, grad_gate)]),
        ]
    )
    shape_four = (node_dev, b_dev, out_steps, chans)
    into_earlier = (
        mm(grad_filt, conv_weight[0, 0].T) + mm(grad_gate, conv_weight[1, 0].T)
    ).reshape(shape_four)
    into_later = (
        mm(grad_filt, conv_weight[0, 1].T)
        + mm(grad_gate, conv_weight[1, 1].T)
        + grad_out.astype(jnp.float32)
    ).reshape(shape_four)
    signal_grad = jnp.pad(into_earlier, ((0, 0), (0, 0), (0, 1), (0, 0))) + jnp.pad(
        into_later, ((0, 0), (0, 0), (1, 0), (0, 0))
    )
    conv_total, mix_total = lax.psum((conv_part, mix_part), ("dom", "batch"))
    factor = 1.0 / math.sqrt(
        node_dev * lax.axis_size("dom") * b_dev * lax.axis_size("batch") * out_steps
    )
    return (layer_out, signal_grad.astype(jnp.bfloat16), conv_total * factor, mix_total * factor)


def solution(mesh):
    placed = (
        P("dom", "batch", None, None),
        P("dom", "batch", None, None),
        P(),
        P(),
        P("dom", None),
        P("dom", None),
        P("dom", None, None),
        P("dom"),
        P("dom"),
        P("dom"),
        P(),
        P(),
    )
    return jax.shard_map(
        body,
        mesh=mesh,
        in_specs=placed,
        out_specs=(P("dom", "batch", None, None), P("dom", "batch", None, None), P(), P()),
        check_vma=False,
    )
```

profile of v0, /device:TPU:1, one launch (start us, length us, event | category | flops | bytes accessed | tf_op | source)
XLA Modules:
  0.0 1210.1 jit_solution(5882545146521414096)
XLA Ops:
  9.1 1.8 copy.30
  11.6 1.3 convolution_convert_fusion
  13.8 2.5 gather_fusion.20
  16.3 5.6 fusion.106
  21.9 6.9 copy.40
  28.8 4.6 fusion.2
  33.4 1.6 copy-done.1
  36.2 3.1 fusion.34
  40.0 13.3 %all-to-all-start.2 = ((bf16[64,2,768]{2,1,0:T(2,128)(2,1)}), bf16[64,2,768]{2,1,0:T(2,128)(2,1)}, u32[]{:S(2)}, u32[]{:S(2)}) async-start(bf16[64,2,768]{2,1,0:T(2,128)(2,1)} %convert_element_type.89), calls=%async_computation.2 | async-start | bytes 393216 | tf_op jit(solution)/shard_map/all_to_all | solution.py:105
  53.7 2.0 fusion.102
  55.7 2.5 reshape.367
  58.2 1.5 fusion.59
  59.8 1.5 fusion.52
  62.1 2.4 reshape.366
  64.7 3.1 fusion.17
  68.5 1.4 slice.211
  70.2 2.9 copy.31
  75.3 144.6 %all-reduce.11.cloned.1.call-done = f32[128,768]{1,0:T(8,128)} async-done(((f32[128,768]{1,0:T(8,128)}), f32[128,768]{1,0:T(8,128)}) %all-reduce.11.cloned.1.call-update) | async-done | bytes 393232 | tf_op jit(solution)/shard_map/psum | solution.py:112
  219.9 2.9 fusion.41
  223.8 3.4 fusion.25
  227.2 2.6 reshape.374
  229.8 2.8 fusion.23
  232.6 1.5 reshape_reshape.7
  234.1 2.5 gather_fusion.21
  236.5 5.6 fusion.107
  242.1 6.8 copy.41
  249.0 4.6 fusion
  253.6 1.6 copy-done.3
  256.4 3.1 fusion.33
  260.2 10.0 all-to-all-start.3
  273.6 1.4 slice-done
  275.0 1.5 copy.34
  276.4 160.1 %all-reduce.13.cloned.1.call-done = f32[128,768]{1,0:T(8,128)} async-done(((f32[128,768]{1,0:T(8,128)}), f32[128,768]{1,0:T(8,128)}) %all-reduce.13.cloned.1.call-update) | async-done | bytes 393232 | tf_op jit(solution)/shard_map/psum | solution.py:112
  436.5 2.9 fusion.39
  439.5 3.4 fusion.24
  442.9 2.6 reshape.375
  445.5 2.0 convolution_add_fusion.3
  448.2 1.9 multiply_convert_fusion
  454.6 1.5 fusion.57
  456.1 1.6 fusion.54
  464.9 1.7 gather_fusion
  466.6 1.7 gather.71
  468.3 1.8 broadcast_multiply_fusion.3
  470.1 9.8 all-to-all-start
  480.4 3.1 convolution_add_fusion.1
  483.5 1.6 fusion.16
  492.2 3.6 reshape.376
  495.8 3.6 reshape.377
  499.5 4.1 fusion.32
  505.7 173.9 %all-reduce.19.cloned.1.call-done = (bf16[16,768]{1,0:T(8,128)(2,1)}, bf16[16,768]{1,0:T(8,128)(2,1)}, bf16[16,768]{1,0:T(8,128)(2,1)}, bf16[16,768]{1,0:T(8,128...) async-done(((bf16[16,768]{1,0:T(8,128)(2,1)}, bf16[16,768]{1,0:T(8,128)(2,1)}, ...) | async-done | bytes 196624 | tf_op jit(solution)/shard_map/psum | solution.py:13
  685.6 2.5 gather_fusion.9
  688.0 5.6 fusion.104
  693.6 6.9 copy.38
  700.5 5.6 fusion.26
  718.2 9.0 all-to-all-start.1
  731.6 7.6 all-to-all-done.1
  739.3 172.8 %all-reduce.17.cloned.1.call-done = (bf16[16,768]{1,0:T(8,128)(2,1)}, bf16[16,768]{1,0:T(8,128)(2,1)}, bf16[16,768]{1,0:T(8,128)(2,1)}, bf16[16,768]{1,0:T(8,128...) async-done(((bf16[16,768]{1,0:T(8,128)(2,1)}, bf16[16,768]{1,0:T(8,128)(2,1)}, ...) | async-done | bytes 196624 | tf_op jit(solution)/shard_map/psum | solution.py:13
  918.1 2.5 gather_fusion.19
  920.5 5.6 fusion.105
  926.1 6.8 copy.39
  933.0 5.6 fusion.29
  945.0 254.7 %all-reduce.15.cloned.1.call-done = (f32[2,2,256,256]{2,3,1,0:T(8,128)}, f32[3,256,256]{2,1,0:T(8,128)}) async-done(((f32[2,2,256,256]{2,3,1,0:T(8,128)}, f32[3,256,256]{2,1,0:T(8,128)}), (f32[2,2,256,256]{2,3,1,0:T(8,128)}, f32[3,256,256]{2,1,0:T(8,128)})) %all-reduce.15.cloned.1.call-update) | async-done | bytes 1835024 | tf_op jit(solution)/shard_map/psum | solution.py:166
  1199.8 1.3 broadcast_multiply_fusion
  1201.1 1.3 copy.37
  (209 shorter events, 68.6 us)
Async XLA Ops:
  7.2 9.1 copy-start
  7.2 212.7 %all-reduce.11.cloned.1.call-start = ((), (), s32[]{:S(2)}) async-start(), calls=%async_computation.4 | async-start | bytes 786432 | tf_op jit(solution)/shard_map/psum | solution.py:112
  21.9 6.9 copy-start.41
  21.9 6.9 copy-start.37
  33.4 1.6 copy-start.1
  35.0 18.6 %copy-start.29 = (s32[8,16]{1,0:T(8,128)S(1)}, s32[8,16]{1,0:T(8,128)}, u32[]{:S(2)}) copy-start(s32[8,16]{1,0:T(8,128)} %param.23) | copy-start | bytes 1540
  35.0 18.7 %copy-start.8 = (bf16[512,1,4,256]{3,2,1,0:T(4,128)(2,1)S(1)}, bf16[512,1,4,256]{3,2,1,0:T(4,128)(2,1)}, u32[]{:S(2)}) copy-start(bf16[512,1,4,256]{3,2,1,0:T(4,128)(2,1)} %param.12) | copy-start | bytes 3145732
  40.0 182.8 %all-to-all-start.2 = ((bf16[64,2,768]{2,1,0:T(2,128)(2,1)}), bf16[64,2,768]{2,1,0:T(2,128)(2,1)}, u32[]{:S(2)}, u32[]{:S(2)}) async-start(bf16[64,2,768]{2,1,0:T(2,128)(2,1)} %convert_element_type.89), calls=%async_computation.2 | async-start | bytes 393216 | tf_op jit(solution)/shard_map/all_to_all | solution.py:105
  53.4 383.1 %all-reduce.13.cloned.1.call-start = ((), (), s32[]{:S(2)}) async-start(), calls=%async_computation.5 | async-start | bytes 786432 | tf_op jit(solution)/shard_map/psum | solution.py:112
  55.7 2.5 copy-start.16
  59.8 1.5 copy-start.28
  59.8 2.2 copy-start.39
  59.8 2.3 copy-start.40
  64.5 3.3 copy-start.4
  64.7 3.8 copy-start.2
  68.4 389.7 %copy-start.30 = (s32[1024]{0:T(1024)}, s32[1024]{0:T(1024)S(1)}, u32[]{:S(2)}) copy-start(s32[1024]{0:T(1024)S(1)} %get-tuple-element.59) | copy-start | bytes 12292
  68.4 390.9 %copy-start.32 = (s32[1024]{0:T(1024)}, s32[1024]{0:T(1024)S(1)}, u32[]{:S(2)}) copy-start(s32[1024]{0:T(1024)S(1)} %get-tuple-element.57) | copy-start | bytes 12292
  68.4 392.1 %copy-start.31 = (s32[1024]{0:T(1024)}, s32[1024]{0:T(1024)S(1)}, u32[]{:S(2)}) copy-start(s32[1024]{0:T(1024)S(1)} %get-tuple-element.58) | copy-start | bytes 12292
  75.3 386.4 %copy-start.34 = (s32[1024]{0:T(1024)}, s32[1024]{0:T(1024)S(1)}, u32[]{:S(2)}) copy-start(s32[1024]{0:T(1024)S(1)} %get-tuple-element.53) | copy-start | bytes 12292
  75.3 387.0 %copy-start.33 = (s32[1024]{0:T(1024)}, s32[1024]{0:T(1024)S(1)}, u32[]{:S(2)}) copy-start(s32[1024]{0:T(1024)S(1)} %get-tuple-element.54) | copy-start | bytes 12292
  253.6 1.6 copy-start.3
  260.2 179.2 %all-to-all-start.3 = ((bf16[64,2,768]{2,1,0:T(2,128)(2,1)}), bf16[64,2,768]{2,1,0:T(2,128)(2,1)S(1)}, u32[]{:S(2)}, u32[]{:S(2)}) async-start(bf16[64,2,768]{2,1,0:T(2,128)(2,1)} %convert_element_type.91), calls=%async_computation.3 | async-start | bytes 393216 | tf_op jit(solution)/shard_map/all_to_all | solution.py:105
  273.5 189.4 %copy-start.36 = (s32[1024]{0:T(1024)}, s32[1024]{0:T(1024)S(1)}, u32[]{:S(2)}) copy-start(s32[1024]{0:T(1024)S(1)} %get-tuple-element.55) | copy-start | bytes 12292
  273.5 189.9 %copy-start.35 = (s32[1024]{0:T(1024)}, s32[1024]{0:T(1024)S(1)}, u32[]{:S(2)}) copy-start(s32[1024]{0:T(1024)S(1)} %get-tuple-element.56) | copy-start | bytes 12292
  273.5 1.4 slice-start
  445.5 2.0 copy-start.5
  445.5 2.2 copy-start.17
  445.5 2.7 copy-start.19
  450.1 3.3 copy-start.12
  456.1 1.6 copy-start.9
  464.1 16.3 %copy-start.13 = (bf16[1536,256]{1,0:T(8,128)(2,1)S(1)}, bf16[1536,256]{1,0:T(8,128)(2,1)}, u32[]{:S(2)}) copy-start(bf16[1536,256]{1,0:T(8,128)(2,1)} %copy-done.12) | copy-start | bytes 2359300
  470.1 34.6 %all-to-all-start = ((bf16[64,2,768]{2,1,0:T(2,128)(2,1)}), bf16[64,2,768]{2,1,0:T(2,128)(2,1)}, u32[]{:S(2)}, u32[]{:S(2)}) async-start(bf16[64,2,768]{2,1,0:T(2,128)(2,1)} %broadcast_multiply_fusion.3), calls=%async_computation | async-start | bytes 393216 | tf_op jit(solution)/shard_map/all_to_all | solution.py:90
  479.9 199.7 %all-reduce.19.cloned.1.call-start = ((), (), s32[]{:S(2)}) async-start(), calls=%async_computation.8 | async-start | bytes 393216 | tf_op jit(solution)/shard_map/psum | solution.py:13
  480.4 3.1 copy-start.7
  483.5 1.6 copy-start.27
  483.5 2.2 copy-start.25
  483.5 2.8 copy-start.26
  485.1 5.9 copy-start.23
  485.1 5.9 copy-start.24
  499.5 4.1 copy-start.10
  693.6 6.9 copy-start.38
  718.2 21.0 %all-to-all-start.1 = ((bf16[64,2,768]{2,1,0:T(2,128)(2,1)}), bf16[64,2,768]{2,1,0:T(2,128)(2,1)S(1)}, u32[]{:S(2)}, u32[]{:S(2)}) async-start(bf16[64,2,768]{2,1,0:T(2,128)(2,1)} %broadcast_multiply_fusion.2), calls=%async_computation.1 | async-start | bytes 393216 | tf_op jit(solution)/shard_map/all_to_all | solution.py:90
  727.2 185.0 %all-reduce.17.cloned.1.call-start = ((), (), s32[]{:S(2)}) async-start(), calls=%async_computation.7 | async-start | bytes 393216 | tf_op jit(solution)/shard_map/psum | solution.py:13
  729.1 470.6 %all-reduce.15.cloned.1.call-start = ((), (), s32[]{:S(2)}) async-start(), calls=%async_computation.6 | async-start | bytes 3670016 | tf_op jit(solution)/shard_map/psum | solution.py:166
  729.3 1.1 copy-start.14
  938.7 1.0 copy-start.21
  939.0 1.0 copy-start.22
  940.0 1.4 copy-start.6
  940.0 1.7 copy-start.11
  940.0 1.7 copy-start.18
  941.8 1.1 copy-start.15
  1201.1 1.3 copy-start.20
Sparse Core Ops, SparseCore 0:
  36.4 183.4 all-reduce.10
  256.5 179.9 all-reduce.12
  499.6 180.0 all-reduce.18
  732.1 180.0 all-reduce.16
  941.1 258.6 all-reduce.14
where the time goes:
time: 1220 us; the launch traced here: 1210 us
  waiting for transfers between devices  914 us (75%)
  local copies, waits for them, and re-layouts  123 us (10%)
  matrix products  85.6 us (7%)
  starting transfers between devices  43.1 us (4%)
  other arithmetic  25 us (2%)
  between operations  19.7 us (2%)
    psum x2, waiting for transfers between devices, from_root(): return lax.psum(block, axis)  347 us
    psum x2, waiting for transfers between devices, gather_back(): summed = lax.psum(ext_grad[node_dev + halo_count:], 'dom')  305 us
    psum x1, waiting for transfers between devices, body(): conv_total, mix_total = lax.psum((conv_part, mix_part), ('dom', 'batch'))  255 us
  transfers between devices with their start and end apart: 9, of which 6 were waited for; matrix products, arithmetic and copies ran while one was open for 5% of the time, Pallas kernels for 0%

commit v1 on v0

v1 whole, which is shorter than its diff:
```python
import math

import jax
import jax.numpy as jnp
from jax import lax
from jax.experimental import pallas as pl
from jax.experimental.pallas import tpu as pltpu
from jax.sharding import PartitionSpec as P

BF = jnp.bfloat16
F32 = jnp.float32
I32 = jnp.int32
NODE = 512
EXT = 768
BLK = 128
C = 256
T1 = 3
HIST = 4
DOM = 64
BATCH = 4
LIMIT = 50 * 1024 * 1024


def nn(a, b):
    return jnp.dot(a, b, preferred_element_type=F32)


def nt(a, b):
    return lax.dot_general(a, b, (((1,), (1,)), ((), ())), preferred_element_type=F32)


def tn(a, b):
    return lax.dot_general(a, b, (((0,), (0,)), ((), ())), preferred_element_type=F32)


def iota(shape, dim):
    return lax.broadcasted_iota(I32, shape, dim)


def hot(mask):
    return jnp.where(mask, 1.0, 0.0).astype(BF)


def pick_rows(column, count):
    return hot(column == iota((column.shape[0], count), 1))


def put_rows(row, count):
    return hot(row == iota((count, row.shape[1]), 0))


def gates(early, late, conv):
    filt = nn(early, conv[0, 0]) + nn(late, conv[0, 1])
    gate = nn(early, conv[1, 0]) + nn(late, conv[1, 1])
    th = jnp.tanh(filt)
    sg = jax.nn.sigmoid(gate)
    return (th * sg).astype(BF), sg * (1.0 - th * th), th * sg * (1.0 - sg)


def start_kernel(
    trow, tcol, tmask, sig, cot, tiles, cols, a_ref, at_ref, eown, ehub, send, acc
):
    acc[...] = jnp.zeros_like(acc)

    def add(i, carry):
        at = trow[i] * 6 + tcol[i]
        acc[at] += tiles[i].astype(F32) * tmask[i].astype(F32)
        return carry

    lax.fori_loop(0, tiles.shape[0], add, 0)
    for r in range(4):
        for c in range(6):
            block = acc[r * 6 + c]
            a_ref[r * BLK : (r + 1) * BLK, c * BLK : (c + 1) * BLK] = block.astype(BF)
            at_ref[c * BLK : (c + 1) * BLK, r * BLK : (r + 1) * BLK] = block.T.astype(BF)
    pick_sig = pick_rows(cols[:, 0:1], NODE)
    pick_ext = pick_rows(cols[:, 1:2], EXT - NODE)
    for t in range(T1):
        ext = nn(at_ref[...], cot[t])
        eown[t] = ext[:NODE]
        ehub[t] = ext[NODE + BLK :]
        last = pick_rows(cols[:, 2 + t : 3 + t], NODE)
        out = (
            nn(pick_sig, sig[t])
            + nn(last, sig[HIST - 1])
            + nn(pick_ext, ext[NODE:].astype(BF))
        )
        send[:, t * C : (t + 1) * C] = out.astype(BF)


def own_kernel(sig, cot, conv, mix, a_ref, hid, fac_f, fac_g, hop, gw, mix0):
    total = jnp.zeros((C, C), F32)
    for t in range(T1):
        h, p, q = gates(sig[t], sig[t + 1], conv)
        hid[t] = h
        fac_f[t] = p
        fac_g[t] = q
        hop[t] = nn(a_ref[:, :NODE], h)
        gw[t] = nt(cot[t], mix[0])
        total += tn(h, cot[t])
    mix0[...] = total


def hub_blocks(recv, owner, with_last):
    row = iota((8, NODE), 0)
    m = iota((8, NODE), 1)
    which = row >> 2
    step = row & 3
    forward = jnp.zeros((8, C), F32)
    backward = jnp.zeros((8, C), F32)
    for c in range(T1):
        block = recv[:, c * C : (c + 1) * C]
        f = (step == c) & (m == owner * 8 + 2 + which)
        if with_last and c == 2:
            f = f | ((row == 3) & (m == owner * 8 + 6))
        if with_last and c == 0:
            f = f | ((row == 7) & (m == owner * 8 + 7))
        b = (step == c) & ((m & 7) == 2 + which) & ((m >> 3) != owner)
        forward += nn(hot(f), block)
        backward += nn(hot(b), block)
    return forward, backward


def hub_kernel(scal, recv, send):
    owner = scal[0]
    forward, backward = hub_blocks(recv, owner, True)
    at_owner = iota((DOM, 8, C), 0) == owner
    send[...] = jnp.where(at_owner, backward[None], forward[None]).astype(BF)


def middle_kernel(
    recv1, recv2, sig, cot, conv, mix, a_ref, at_ref, eown, ehub, hid, fac_f, fac_g,
    hop_part, gw, mix0, cols, rows, hubcol, hubrow, send, wsend, hop_out, gh_out, ehub2,
):
    halo = BLK
    r = iota((halo, NODE), 0)
    m = iota((halo, NODE), 1)
    base = (r >> 1) * 8
    odd = r & 1
    pick0 = hot(m == base + odd)
    pick3a = hot((odd == 0) & (m == base + 6))
    pick3b = hot((odd == 1) & (m == base + 6))
    own_node = hubcol[:, 0:1]
    own_pick = pick_rows(own_node, NODE)
    ext_sig = []
    for t in range(HIST):
        if t < T1:
            rows_halo = nn(pick0, recv1[:, t * C : (t + 1) * C])
        else:
            rows_halo = nn(pick3a, recv1[:, 0:C]) + nn(pick3b, recv1[:, C : 2 * C])
        hub_pick = hot((m == base + odd * 4 + t) & (own_node < 0))
        rows_hub = nn(hub_pick, recv2[...]) + nn(own_pick, sig[t])
        ext_sig.append(jnp.concatenate([rows_halo, rows_hub], 0).astype(BF))
    put_halo = put_rows(rows[0:1, :], NODE)
    put_hub_own = put_rows(hubrow[0:1, :], NODE)
    pick_sig = pick_rows(cols[:, 0:1], NODE)
    pick_ext = pick_rows(cols[:, 1:2], EXT - NODE)
    column = iota((NODE, NODE), 1)
    node = iota((NODE, NODE), 0)
    grads = [[jnp.zeros((C, C), F32) for _ in range(2)] for _ in range(2)]
    mix1 = jnp.zeros((C, C), F32)
    mix2 = jnp.zeros((C, C), F32)
    for t in range(T1):
        h, p, q = gates(ext_sig[t], ext_sig[t + 1], conv)
        hop = (hop_part[t] + nn(a_ref[:, NODE:], h)).astype(BF)
        hop_out[t] = hop
        put_hub = hot((rows[1:2, :] == node) & ((column & 3) == t))
        back = (
            eown[t]
            + nn(put_halo, recv1[:, t * C : (t + 1) * C])
            + nn(put_hub, recv2[...])
            + nn(put_hub_own, ehub[t].astype(BF))
        ).astype(BF)
        mix1 += tn(hop, cot[t])
        mix2 += tn(hop, back)
        ext = nn(at_ref[...], back)
        ehub2[t] = ext[NODE + BLK :]
        ext = ext.astype(BF)
        out = nn(pick_sig, hop) + nn(pick_ext, ext[NODE:])
        send[:, t * C : (t + 1) * C] = out.astype(BF)
        through = nt(ext, mix[2])
        gh = gw[t] + nt(back, mix[1]) + through[:NODE]
        gh_out[t] = gh
        far = through[NODE:]
        own = ((gh * fac_f[t]).astype(BF), (gh * fac_g[t]).astype(BF))
        other = ((far * p).astype(BF), (far * q).astype(BF))
        for k in range(2):
            for s in range(2):
                grads[k][s] += tn(sig[t + s], own[k]) + tn(ext_sig[t + s], other[k])
    parts = [grads[0][0], grads[0][1], grads[1][0], grads[1][1], mix0[...], mix1, mix2]
    for k, part in enumerate(parts):
        wsend[k * C : (k + 1) * C, :] = part.astype(BF)
    wsend[7 * C :, :] = jnp.zeros((C, C), BF)


def join_kernel(rows, parts, send):
    send[:, : T1 * C] = rows[...]
    total = parts[0].astype(F32)
    for b in range(1, BATCH):
        total += parts[b].astype(F32)
    send[:, T1 * C :] = total.astype(BF)


def hub_weight_kernel(scal, recv, send):
    owner = scal[0]
    forward, backward = hub_blocks(recv, owner, False)
    row = iota((8, NODE), 0)
    m = iota((8, NODE), 1)
    weights = nn(hot((m & 7) == row), recv[:, T1 * C :])
    at_owner = iota((DOM, 16, C), 0) == owner
    to_others = jnp.concatenate([forward, weights], 0)
    to_owner = jnp.concatenate([backward, weights], 0)
    send[...] = jnp.where(at_owner, to_owner[None], to_others[None]).astype(BF)


def end_kernel(
    recv3, recv4, sig, cot, conv, mix, a_ref, hid, fac_f, fac_g, hop_ref, gh_ref, ehub2,
    rows, rows4, hubcol, hubrow, layer, sgrad,
):
    halo = BLK
    r = iota((halo, NODE), 0)
    m = iota((halo, NODE), 1)
    pick0 = hot(m == (r >> 1) * 8 + (r & 1))
    r4 = iota((halo, 2 * NODE), 0)
    m4 = iota((halo, 2 * NODE), 1)
    base4 = (r4 >> 1) * 16 + (r4 & 1) * 4
    own_node = hubcol[:, 0:1]
    own_pick = pick_rows(own_node, NODE)
    put_halo = put_rows(rows[0:1, :], NODE)
    put_hub_own = put_rows(hubrow[0:1, :], NODE)
    column4 = iota((NODE, 2 * NODE), 1)
    node4 = iota((NODE, 2 * NODE), 0)
    for t in range(T1):
        block = recv3[:, t * C : (t + 1) * C]
        hop = hop_ref[t]
        hub_pick = hot((m4 == base4 + t) & (own_node < 0))
        rows_halo = nn(pick0, block).astype(BF)
        rows_hub = (nn(hub_pick, recv4[...]) + nn(own_pick, hop)).astype(BF)
        two = (
            nn(a_ref[:, :NODE], hop)
            + nn(a_ref[:, NODE : NODE + BLK], rows_halo)
            + nn(a_ref[:, NODE + BLK :], rows_hub)
        ).astype(BF)
        mixed = (
            sig[t + 1].astype(F32) + nn(hid[t], mix[0]) + nn(hop, mix[1]) + nn(two, mix[2])
        )
        layer[t] = mixed.astype(BF)
        put_hub = hot((rows4[0:1, :] == node4) & ((column4 & 3) == t))
        back = (
            nn(put_halo, block)
            + nn(put_hub, recv4[...])
            + nn(put_hub_own, ehub2[t].astype(BF))
        ).astype(BF)
        gh = gh_ref[t] + nt(back, mix[2])
        gf = (gh * fac_f[t]).astype(BF)
        gg = (gh * fac_g[t]).astype(BF)
        early = nt(gf, conv[0, 0]) + nt(gg, conv[1, 0])
        late = nt(gf, conv[0, 1]) + nt(gg, conv[1, 1]) + cot[t].astype(F32)
        if t == 0:
            sgrad[0] = early.astype(BF)
        else:
            sgrad[t] = (early + carried).astype(BF)
        carried = late
    sgrad[T1] = carried.astype(BF)


VM = pl.BlockSpec(memory_space=pltpu.VMEM)
SM = pl.BlockSpec(memory_space=pltpu.SMEM)


def call(kernel, outs, args, smem=0, scratch=(), flops=0):
    return pl.pallas_call(
        kernel,
        out_shape=[jax.ShapeDtypeStruct(s, d) for s, d in outs],
        in_specs=[SM] * smem + [VM] * (len(args) - smem),
        out_specs=[VM] * len(outs),
        scratch_shapes=list(scratch),
        compiler_params=pltpu.CompilerParams(vmem_limit_bytes=LIMIT),
        cost_estimate=pl.CostEstimate(flops=flops, bytes_accessed=8 << 20, transcendentals=0),
    )(*args)


def swap(x, axis):
    return lax.all_to_all(x, axis, split_axis=0, concat_axis=0, tiled=True)


def body(
    signal,
    cotangent,
    conv,
    mix,
    send_rows,
    send_mask,
    tile_vals,
    tile_row,
    tile_col,
    tile_mask,
    hub_owner,
    hub_rows,
):
    me = lax.axis_index("dom").astype(I32)
    sig = jnp.transpose(signal[:, 0], (1, 0, 2))
    cot = jnp.transpose(cotangent[:, 0], (1, 0, 2))

    part = jnp.arange(DOM, dtype=I32)
    none = jnp.full((DOM, 1), -1, I32)
    none2 = jnp.full((DOM, 2), -1, I32)
    used = jnp.where(send_mask == 1, send_rows, -1)
    mine = (jnp.repeat(hub_owner, 8) == me)[:, None]
    own_hub = jnp.where(mine, hub_rows.reshape(DOM, 2), -1)
    two = 2 * part[:, None] + jnp.arange(2, dtype=I32)[None]
    pick_sig = jnp.concatenate([used, own_hub, none2, none2], 1)
    pick_ext = jnp.concatenate([none2, jnp.where(mine, -1, BLK + two), two, none2], 1)
    six = jnp.full((DOM, 6), -1, I32)
    last0 = jnp.concatenate([six, used[:, 0:1], own_hub[:, 1:2]], 1)
    last1 = jnp.concatenate([six, used[:, 1:2], none], 1)
    last2 = jnp.concatenate([six, own_hub[:, 0:1], none], 1)
    cols = jnp.stack([pick_sig, pick_ext, last0, last1, last2], -1).reshape(NODE, 5)
    back_row = jnp.concatenate([none2, none2, used, none2], 1).reshape(1, NODE)
    hub_back = jnp.repeat(own_hub, 4, axis=1)
    rows = jnp.concatenate([back_row, hub_back.reshape(1, NODE)], 0)
    rows4 = jnp.concatenate([hub_back, jnp.full((DOM, 8), -1, I32)], 1).reshape(1, 2 * NODE)
    hubcol = own_hub.reshape(BLK, 1)
    hubrow = own_hub.reshape(1, BLK)
    scal = hub_owner[me // 8].reshape(1)

    field = (T1, NODE, C)
    a_mat, at_mat, eown, ehub, send1 = call(
        start_kernel,
        [((NODE, EXT), BF), ((EXT, NODE), BF), (field, F32), ((T1, BLK, C), F32), ((NODE, EXT), BF)],
        (tile_row, tile_col, tile_mask, sig, cot, tile_vals, cols),
        smem=3,
        scratch=[pltpu.VMEM((24, BLK, BLK), F32)],
        flops=2 << 30,
    )
    recv1 = swap(send1.reshape(DOM, 8, EXT), "dom").reshape(NODE, EXT)
    hid, fac_f, fac_g, hop_part, gw, mix0 = call(
        own_kernel,
        [(field, BF), (field, F32), (field, F32), (field, F32), (field, F32), ((C, C), F32)],
        (sig, cot, conv, mix, a_mat),
        flops=3 << 30,
    )
    (send2,) = call(hub_kernel, [((DOM, 8, C), BF)], (scal, recv1), smem=1, flops=1 << 28)
    recv2 = swap(send2, "dom").reshape(NODE, C)
    send3, wsend, hop, gh, ehub2 = call(
        middle_kernel,
        [
            ((NODE, EXT), BF),
            ((8 * C, C), BF),
            (field, BF),
            (field, F32),
            ((T1, BLK, C), F32),
        ],
        (recv1, recv2, sig, cot, conv, mix, a_mat, at_mat, eown, ehub, hid, fac_f, fac_g,
         hop_part, gw, mix0, cols, rows, hubcol, hubrow),
        flops=8 << 30,
    )
    wrecv = swap(wsend.reshape(BATCH, NODE, C), "batch")
    (send3w,) = call(join_kernel, [((NODE, 4 * C), BF)], (send3, wrecv), flops=1 << 28)
    recv3 = swap(send3w.reshape(DOM, 8, 4 * C), "dom").reshape(NODE, 4 * C)
    (send4,) = call(hub_weight_kernel, [((DOM, 16, C), BF)], (scal, recv3), smem=1, flops=1 << 28)
    recv4 = swap(send4, "dom")
    mine4 = recv4[:, 8:].reshape(NODE, C)
    whole = swap(jnp.broadcast_to(mine4[None], (BATCH, NODE, C)), "batch").reshape(8 * C, C)
    layer, sgrad = call(
        end_kernel,
        [(field, BF), ((HIST, NODE, C), BF)],
        (recv3, recv4.reshape(2 * NODE, C), sig, cot, conv, mix, a_mat, hid, fac_f, fac_g, hop,
         gh, ehub2, rows, rows4, hubcol, hubrow),
        flops=6 << 30,
    )
    factor = 1.0 / math.sqrt(NODE * DOM * BATCH * T1)
    whole = whole.astype(F32) * factor
    return (
        jnp.transpose(layer, (1, 0, 2))[:, None],
        jnp.transpose(sgrad, (1, 0, 2))[:, None],
        whole[: 4 * C].reshape(2, 2, C, C),
        whole[4 * C : 7 * C].reshape(3, C, C),
    )


def solution(mesh):
    placed = (
        P("dom", "batch", None, None),
        P("dom", "batch", None, None),
        P(),
        P(),
        P("dom", None),
        P("dom", None),
        P("dom", None, None),
        P("dom"),
        P("dom"),
        P("dom"),
        P(),
        P(),
    )
    return jax.shard_map(
        body,
        mesh=mesh,
        in_specs=placed,
        out_specs=(P("dom", "batch", None, None), P("dom", "batch", None, None), P(), P()),
        check_vma=False,
    )
```

time: 1220 us -> 188 us (0.15)
  waiting for transfers between devices: 914 us -> 26.6 us
  local copies, waits for them, and re-layouts: 123 us -> 17.8 us
  matrix products: 85.6 us -> 0 us
  blocking collectives: 0 us -> 76.5 us
  Pallas kernels: 0 us -> 38 us
  other arithmetic: 25 us -> 3.1 us
  starting transfers between devices: 43.1 us -> 24.1 us
  between operations: 19.7 us -> 0.99 us
    psum x5 -> x0, waiting for transfers between devices: 906 us -> none  [the longest x2 347 us: from_root(): return lax.psum(block, axis)]
    dot_general x33 -> x0, matrix products: 85.6 us -> none  [the longest x14 23.1 us: mm(): return jnp.dot(left, right, preferred_element_type=jnp.float32)]
    all_to_all x0 -> x3, blocking collectives: none -> 76.5 us  [swap(): return lax.all_to_all(x, axis, split_axis=0, concat_axis=0, tiled=True)]
    pallas_call x0 -> x7, Pallas kernels: none -> 38 us  [call(): pl.pallas_call(kernel, out_shape=[jax.ShapeDtypeStruct(s, d) for s, d in...]
    dot_general x4 -> x0, local copies, waits for them, and re-layouts: 27.4 us -> none  [the longest x2 13.7 us: tile_back(): jnp.einsum('tji,tjf->tif', tile_block, chosen, preferred_element_type=jnp...]
    gather x24 -> x0, local copies, waits for them, and re-layouts: 26.7 us -> none  [the longest x16 12.5 us: spread(): panel = field[hub_rows[owner_slot]]]
    all_to_all x4 -> x3, waiting for transfers between devices: 7.63 us -> 26.6 us  [swap(): return lax.all_to_all(x, axis, split_axis=0, concat_axis=0, tiled=True)]
    all_to_all x4 -> x3, starting transfers between devices: 42.1 us -> 24.1 us  [swap(): return lax.all_to_all(x, axis, split_axis=0, concat_axis=0, tiled=True)]
  transfers between devices with their start and end apart: 9 -> 3, of which waited for: 6 -> 2; matrix products, arithmetic and copies ran while one was open for 5% -> 2% of each run, Pallas kernels for 0% -> 9%
where the time goes in v1:
time: 188 us; the launch traced here: 187 us
  blocking collectives  76.5 us (41%)
  Pallas kernels  38 us (20%)
  waiting for transfers between devices  26.6 us (14%)
  starting transfers between devices  24.1 us (13%)
  local copies, waits for them, and re-layouts  17.8 us (9%)
  other arithmetic  3.1 us (2%)
    all_to_all x3, blocking collectives, swap(): return lax.all_to_all(x, axis, split_axis=0, concat_axis=0, tiled=True)  76.5 us
    pallas_call x7, Pallas kernels, call(): pl.pallas_call(kernel, out_shape=[jax.ShapeDtypeStruct(s, d) for s, d in...  38 us
    all_to_all x3, waiting for transfers between devices, swap(): return lax.all_to_all(x, axis, split_axis=0, concat_axis=0, tiled=True)  26.6 us
    all_to_all x3, starting transfers between devices, swap(): return lax.all_to_all(x, axis, split_axis=0, concat_axis=0, tiled=True)  24.1 us
    unnamed x47, local copies, waits for them, and re-layouts  10.8 us
  transfers between devices with their start and end apart: 3, of which 2 were waited for; matrix products, arithmetic and copies ran while one was open for 2% of the time, Pallas kernels for 9%

profile of v1, /device:TPU:1, one launch (start us, length us, event | category | flops | bytes accessed | tf_op | source)
XLA Modules:
  0.0 187.0 jit_solution(7268471827598881060)
XLA Ops:
  0.7 0.7 broadcast_compare_fusion
  1.4 0.1 broadcast_in_dim.61
  1.5 0.1 eq.24
  1.6 0.8 reshape.122
  2.3 0.1 copy.81
  2.4 0.1 copy.83
  2.5 0.7 compare_select_fusion
  3.2 0.1 copy.82
  3.3 0.1 copy.86
  3.4 0.1 copy.88
  3.5 0.0 copy-start.8
  3.5 0.0 copy-start.9
  3.6 0.1 copy.85
  3.7 0.1 copy.87
  3.8 0.1 pad.11.clone
  3.8 0.1 add_add_fusion.1
  3.9 0.1 stack.20
  4.0 0.1 stack.21
  4.1 0.1 stack.22
  4.2 0.1 copy.84
  4.3 0.1 stack.19
  4.4 0.1 pad.5.clone
  4.5 0.1 add_add_fusion.2
  4.6 0.1 stack.18
  4.7 0.1 copy.89.cols
  4.9 1.1 copy.107
  6.0 4.6 %shard_map.147 = (bf16[512,768]{1,0:T(8,128)(2,1)S(1)}, bf16[768,512]{1,0:T(8,128)(2,1)S(1)}, f32[3,512,256]{2,1,0:T(8,128)}, f32[3,128,256]{2,1,0:T(8,128)S(1)}, bf16[512,768]{1,0:T(8,128)(2,1)}) custom-call(s32[16]{0:T(128)S(1)} %copy-done.7, s32[16]{0:T(128)S(1)} %copy-done.8, s32[16]{0:T(128)S(1)} %copy-done.9, bf16[4,512,256]{2,1,0:T(8,128)(2,1)} %bitcast.40, ...), custom_call_target="tpu_custom_call" | custom-call | flops 2147483648 | bytes 8388608 | tf_op jit(solution)/shard_map/pallas_call | solution.py:272
  10.6 0.9 copy-done.10
  11.5 0.9 copy-done.13
  12.4 0.7 copy-done.14
  13.1 13.3 %all-to-all-start = ((bf16[64,8,768]{2,1,0:T(8,128)(2,1)}), bf16[64,8,768]{2,1,0:T(8,128)(2,1)S(1)}, u32[]{:S(2)}, u32[]{:S(2)}) async-start(bf16[64,8,768]{2,1,0:T(8,128)(2,1)} %bitcast.4), calls=%async_computation | async-start | bytes 1572864 | tf_op jit(solution)/shard_map/all_to_all | solution.py:284
  26.4 0.1 reshape.137
  26.5 0.1 broadcast_in_dim.62.clone
  26.6 0.1 broadcast_in_dim.74
  26.7 0.1 broadcast_in_dim.68
  26.9 0.1 reshape.128
  26.9 0.6 dynamic_slice.3.scal
  27.5 0.1 reshape.126
  27.6 0.1 broadcast_in_dim.65.clone
  27.7 0.1 reshape_reshape.3
  27.9 21.3 %all-to-all-done = bf16[64,8,768]{2,1,0:T(8,128)(2,1)S(1)} async-done(((bf16[64,8,768]{2,1,0:T(8,128)(2,1)}), bf16[64,8,768]{2,1,0:T(8,128)(2,1)S(1)}, u32[]{:S(2)}, u32[]{:S(2)}) %all-to-all-start) | async-done | bytes 786464 | tf_op jit(solution)/shard_map/all_to_all | solution.py:284
  49.2 1.6 shard_map.148
  50.8 6.2 %all-to-all-start.1 = ((bf16[64,8,256]{2,1,0:T(8,128)(2,1)}), bf16[64,8,256]{2,1,0:T(8,128)(2,1)S(1)}, u32[]{:S(2)}, u32[]{:S(2)}) async-start(bf16[64,8,256]{2,1,0:T(8,128)(2,1)} %shard_map.148), calls=%async_computation.1 | async-start | bytes 524288 | tf_op jit(solution)/shard_map/all_to_all | solution.py:284
  57.1 1.1 copy-done.11
  58.3 5.8 %shard_map.149 = (bf16[3,512,256]{2,1,0:T(8,128)(2,1)S(1)}, f32[3,512,256]{2,1,0:T(8,128)}, f32[3,512,256]{2,1,0:T(8,128)}, f32[3,512,256]{2,1,0:T(8,128)}, f32[...) custom-call(bf16[4,512,256]{2,1,0:T(8,128)(2,1)} %bitcast.41, bf16[3,512,256]{2,1,0:T(8,128)(2,1)S(1)} %bitcast.37, ...), custom_call_target="tpu_custom_call" | custom-call | flops 3221225472 | bytes 8388608 | tf_op jit(solution)/shard_map/pallas_call | solution.py:272
  64.1 0.9 copy-done.16
  65.0 5.3 %all-to-all-done.1 = bf16[64,8,256]{2,1,0:T(8,128)(2,1)S(1)} async-done(((bf16[64,8,256]{2,1,0:T(8,128)(2,1)}), bf16[64,8,256]{2,1,0:T(8,128)(2,1)S(1)}, u32[]{:S(2)}, u32[]{:S(2)}) %all-to-all-start.1) | async-done | bytes 262176 | tf_op jit(solution)/shard_map/all_to_all | solution.py:284
  70.2 1.0 copy-done.15
  71.2 13.7 %shard_map.150 = (bf16[512,768]{1,0:T(8,128)(2,1)S(1)}, bf16[2048,256]{1,0:T(8,128)(2,1)}, bf16[3,512,256]{2,1,0:T(8,128)(2,1)}, f32[3,512,256]{2,1,0:T(8,128)}, f32[3,128,256]{2,1,0:T(8,128)S(1)}) custom-call(bf16[512,768]{1,0:T(8,128)(2,1)} %bitcast.32, bf16[512,256]{1,0:T(8,128)(2,1)S(1)} %bitcast.34, bf16[4,512,256]{2,1,0:T(8,128)(2,1)} %bitcast.42, ...), custom_call_target="tpu_custom_call" | custom-call | flops 8589934592 | bytes 8388608 | tf_op jit(solution)/shard_map/pallas_call | solution.py:272
  84.9 18.7 %all_to_all.30.parts = bf16[4,512,256]{2,1,0:T(8,128)(2,1)S(1)} all-to-all(bf16[4,512,256]{2,1,0:T(8,128)(2,1)} %bitcast.46), channel_id=1, replica_groups=mesh['dom'=64,'batch'=4] {'batch'}, dimensions={0} | all-to-all | bytes 2097152 | tf_op jit(solution)/shard_map/all_to_all | solution.py:284
  103.6 0.2 shard_map.151
  103.8 33.9 %all_to_all.31 = bf16[64,8,1024]{2,1,0:T(8,128)(2,1)S(1)} all-to-all(bf16[64,8,1024]{2,1,0:T(8,128)(2,1)S(1)} %bitcast.30), channel_id=1, replica_groups=mesh['dom'=64,'batch'=4] {'dom'}, dimensions={0} | all-to-all | bytes 2097152 | tf_op jit(solution)/shard_map/all_to_all | solution.py:284
  137.7 1.0 shard_map.152
  138.7 24.0 %all_to_all.32 = bf16[64,16,256]{2,1,0:T(8,128)(2,1)S(1)} all-to-all(bf16[64,16,256]{2,1,0:T(8,128)(2,1)S(1)} %shard_map.152), channel_id=1, replica_groups=mesh['dom'=64,'batch'=4] {'dom'}, dimensions={0} | all-to-all | bytes 1048576 | tf_op jit(solution)/shard_map/all_to_all | solution.py:284
  162.7 1.1 broadcast_in_dim.73
  163.8 4.6 %all-to-all-start.5 = ((bf16[4,512,256]{2,1,0:T(8,128)(2,1)}), bf16[4,512,256]{2,1,0:T(8,128)(2,1)}, u32[]{:S(2)}, u32[]{:S(2)}) async-start(bf16[4,512,256]{2,1,0:T(8,128)(2,1)} %broadcast_in_dim.73), calls=%async_computation.5 | async-start | bytes 2097152 | tf_op jit(solution)/shard_map/all_to_all | solution.py:284
  168.4 0.1 copy.105
  168.5 0.1 reshape.134.rows4
  168.6 1.0 copy-done.18
  169.6 11.1 %shard_map.153 = (bf16[3,512,256]{2,1,0:T(8,128)(2,1)}, bf16[4,512,256]{2,1,0:T(8,128)(2,1)}) custom-call(bf16[512,1024]{1,0:T(8,128)(2,1)} %bitcast.29, bf16[1024,256]{1,0:T(8,128)(2,1)S(1)} %bitcast.33, bf16[4,512,256]{2,1,0:T(8,128)(2,1)} %bitcast.43, bf16[3,512,256]{2,1,0:T(8,128)(2,1)S(1)} %bitcast.38, bf16[2,2,256,256]{3,2,1,0:T(8,128)(2,1)S(1)} %copy-done.5, ...), custom_call_target="tpu_custom_call" | custom-call | flops 6442450944 | bytes 8388608 | tf_op jit(solution)/shard_map/pallas_call | solution.py:272
  180.6 3.0 %copy.99 = bf16[512,1,4,256]{3,2,1,0:T(4,128)(2,1)} copy(bf16[512,1,4,256]{3,0,2,1:T(8,128)(2,1)} %bitcast.45) | data formatting | bytes 2097152
  183.6 1.4 convert_multiply_fusion
  185.1 1.0 slice.30
  186.1 0.9 slice.31
  (53 shorter events, 0.2 us)
Async XLA Ops:
  0.6 4.3 %copy-start.19 = (bf16[512,1,4,256]{3,2,1,0:T(4,128)(2,1)S(1)}, bf16[512,1,4,256]{3,2,1,0:T(4,128)(2,1)}, u32[]{:S(2)}) copy-start(bf16[512,1,4,256]{3,2,1,0:T(4,128)(2,1)} %param.12) | copy-start | bytes 3145732
  3.5 2.5 %copy-start.4 = (bf16[16,128,128]{2,1,0:T(8,128)(2,1)S(1)}, bf16[16,128,128]{2,1,0:T(8,128)(2,1)}, u32[]{:S(2)}) copy-start(bf16[16,128,128]{2,1,0:T(8,128)(2,1)} %tiles.1) | copy-start | bytes 1572868
  3.5 2.5 %copy-start.7 = (s32[16]{0:T(128)S(1)}, s32[16]{0:T(128)}, u32[]{:S(2)}) copy-start(s32[16]{0:T(128)} %trow.1) | copy-start | bytes 196
  3.5 2.5 %copy-start.8 = (s32[16]{0:T(128)S(1)}, s32[16]{0:T(128)}, u32[]{:S(2)}) copy-start(s32[16]{0:T(128)} %tcol.1) | copy-start | bytes 196
  3.5 2.5 %copy-start.9 = (s32[16]{0:T(128)S(1)}, s32[16]{0:T(128)}, u32[]{:S(2)}) copy-start(s32[16]{0:T(128)} %tmask.1) | copy-start | bytes 196
  10.6 0.9 copy-start.10
  11.5 0.9 copy-start.13
  12.4 0.7 copy-start.14
  13.1 13.3 %copy-start.20 = (s32[8,16]{1,0:T(8,128)S(1)}, s32[8,16]{1,0:T(8,128)}, u32[]{:S(2)}) copy-start(s32[8,16]{1,0:T(8,128)} %param.23) | copy-start | bytes 1540
  13.1 13.8 %copy-start.21 = (s32[8]{0:T(128)S(1)}, s32[8]{0:T(128)}, u32[]{:S(2)}) copy-start(s32[8]{0:T(128)} %param.22) | copy-start | bytes 100
  13.1 44.0 %copy-start.2 = (bf16[512,1,3,256]{3,0,2,1:T(8,128)(2,1)S(1)}, bf16[512,1,3,256]{3,0,2,1:T(8,128)(2,1)}, u32[]{:S(2)}) copy-start(bf16[512,1,3,256]{3,0,2,1:T(8,128)(2,1)} %param.13) | copy-start | bytes 2359300
  13.1 44.0 %copy-start.5 = (bf16[2,2,256,256]{3,2,1,0:T(8,128)(2,1)S(1)}, bf16[2,2,256,256]{3,2,1,0:T(8,128)(2,1)}, u32[]{:S(2)}) copy-start(bf16[2,2,256,256]{3,2,1,0:T(8,128)(2,1)} %conv.5) | copy-start | bytes 1572868
  13.1 44.0 %copy-start.6 = (bf16[3,256,256]{2,1,0:T(8,128)(2,1)S(1)}, bf16[3,256,256]{2,1,0:T(8,128)(2,1)}, u32[]{:S(2)}) copy-start(bf16[3,256,256]{2,1,0:T(8,128)(2,1)} %mix.5) | copy-start | bytes 1179652
  13.1 36.1 %all-to-all-start = ((bf16[64,8,768]{2,1,0:T(8,128)(2,1)}), bf16[64,8,768]{2,1,0:T(8,128)(2,1)S(1)}, u32[]{:S(2)}, u32[]{:S(2)}) async-start(bf16[64,8,768]{2,1,0:T(8,128)(2,1)} %bitcast.4), calls=%async_computation | async-start | bytes 1572864 | tf_op jit(solution)/shard_map/all_to_all | solution.py:284
  49.2 14.9 %copy-start.1 = (bf16[64,8,768]{2,1,0:T(8,128)(2,1)}, bf16[64,8,768]{2,1,0:T(8,128)(2,1)S(1)}, u32[]{:S(2)}) copy-start(bf16[64,8,768]{2,1,0:T(8,128)(2,1)S(1)} %all-to-all-done) | copy-start | bytes 2359300
  50.8 19.4 %all-to-all-start.1 = ((bf16[64,8,256]{2,1,0:T(8,128)(2,1)}), bf16[64,8,256]{2,1,0:T(8,128)(2,1)S(1)}, u32[]{:S(2)}, u32[]{:S(2)}) async-start(bf16[64,8,256]{2,1,0:T(8,128)(2,1)} %shard_map.148), calls=%async_computation.1 | async-start | bytes 524288 | tf_op jit(solution)/shard_map/all_to_all | solution.py:284
  57.1 1.1 copy-start.11
  64.1 0.9 copy-start.16
  70.2 1.0 copy-start.15
  84.9 18.9 %copy-start.17 = (f32[3,128,256]{2,1,0:T(8,128)}, f32[3,128,256]{2,1,0:T(8,128)S(1)}, u32[]{:S(2)}) copy-start(f32[3,128,256]{2,1,0:T(8,128)S(1)} %get-tuple-element.37.ehub2) | copy-start | bytes 1179652
  137.7 25.0 %copy-start = (bf16[64,8,1024]{2,1,0:T(8,128)(2,1)}, bf16[64,8,1024]{2,1,0:T(8,128)(2,1)S(1)}, u32[]{:S(2)}) copy-start(bf16[64,8,1024]{2,1,0:T(8,128)(2,1)S(1)} %all_to_all.31) | copy-start | bytes 3145732
  162.7 5.9 %copy-start.3 = (bf16[512,1,3,256]{3,0,2,1:T(8,128)(2,1)S(1)}, bf16[512,1,3,256]{3,0,2,1:T(8,128)(2,1)}, u32[]{:S(2)}) copy-start(bf16[512,1,3,256]{3,0,2,1:T(8,128)(2,1)} %param.13) | copy-start | bytes 2359300
  163.8 4.8 %copy-start.12 = (bf16[512,768]{1,0:T(8,128)(2,1)S(1)}, bf16[512,768]{1,0:T(8,128)(2,1)}, u32[]{:S(2)}) copy-start(bf16[512,768]{1,0:T(8,128)(2,1)} %copy-done.10) | copy-start | bytes 2359300
  163.8 19.9 %all-to-all-start.5 = ((bf16[4,512,256]{2,1,0:T(8,128)(2,1)}), bf16[4,512,256]{2,1,0:T(8,128)(2,1)}, u32[]{:S(2)}, u32[]{:S(2)}) async-start(bf16[4,512,256]{2,1,0:T(8,128)(2,1)} %broadcast_in_dim.73), calls=%async_computation.5 | async-start | bytes 2097152 | tf_op jit(solution)/shard_map/all_to_all | solution.py:284
  168.6 1.0 copy-start.18

commit v2 on v1

v2 whole, which is shorter than its diff:
```python
import math

import jax
import jax.numpy as jnp
from jax import lax
from jax.experimental import pallas as pl
from jax.experimental.pallas import tpu as pltpu
from jax.sharding import PartitionSpec as P

BF = jnp.bfloat16
F32 = jnp.float32
I32 = jnp.int32
NODE = 512
EXT = 768
BLK = 128
C = 256
T1 = 3
HIST = 4
DOM = 64
BATCH = 4
OWNERS = 8
HUB_PER = 16
TILES = 16


def nn(a, b):
    return jnp.dot(a, b, preferred_element_type=F32)


def nt(a, b):
    return lax.dot_general(a, b, (((1,), (1,)), ((), ())), preferred_element_type=F32)


def tn(a, b):
    return lax.dot_general(a, b, (((0,), (0,)), ((), ())), preferred_element_type=F32)


def iota(shape, dim):
    return lax.broadcasted_iota(I32, shape, dim)


def hot(mask):
    return jnp.where(mask, 1.0, 0.0).astype(BF)


def pick_rows(column, count):
    return hot(column == iota((column.shape[0], count), 1))


def put_rows(row, count):
    return hot(row == iota((count, row.shape[1]), 0))


def gates(early, late, conv):
    filt = nn(early, conv[0, 0]) + nn(late, conv[0, 1])
    gate = nn(early, conv[1, 0]) + nn(late, conv[1, 1])
    th = jnp.tanh(filt)
    sg = jax.nn.sigmoid(gate)
    return (th * sg).astype(BF), sg * (1.0 - th * th), th * sg * (1.0 - sg)


def call(kernel, outs, args, mib=60, smem=0, scratch=(), flops=0):
    vmem = pl.BlockSpec(memory_space=pltpu.VMEM)
    return pl.pallas_call(
        kernel,
        out_shape=[jax.ShapeDtypeStruct(s, d) for s, d in outs],
        in_specs=[pl.BlockSpec(memory_space=pltpu.SMEM)] * smem + [vmem] * (len(args) - smem),
        out_specs=[vmem] * len(outs),
        scratch_shapes=list(scratch),
        compiler_params=pltpu.CompilerParams(vmem_limit_bytes=mib << 20),
        cost_estimate=pl.CostEstimate(flops=flops, bytes_accessed=8 << 20, transcendentals=0),
    )(*args)


def high_low(x):
    return (x >> 4).astype(F32).astype(BF), (x & 15).astype(F32).astype(BF)


def start_kernel(
    trow, tcol, tmask, me, owners, tiles, used_rows, used_mask, hubs, cot, sig,
    a_out, a_hub, at_out, cols_out, rows_out, send, acc,
):
    slot = jnp.int32(-1)
    for o in range(OWNERS):
        slot = jnp.where(owners[o] == me[0], o, slot)
    used = jnp.where(used_mask[...] == 1, used_rows[...] + 1, 0)
    held = jnp.where(iota((OWNERS, HUB_PER), 0) == slot, hubs[...] + 1, 0)
    held = jnp.broadcast_to(jnp.sum(held, 0, keepdims=True), (8, HUB_PER))
    held_high, held_low = high_low(held)
    j16 = iota((HUB_PER, DOM), 0)
    q16 = iota((HUB_PER, DOM), 1)
    line = iota((8, DOM), 0)
    values = jnp.where(line == 0, used[0:1], jnp.where(line == 1, used[1:2], 0))
    for i in range(2):
        lay = hot((j16 == 2 * (q16 & 7) + i) & ((q16 >> 3) == slot))
        wide = (16.0 * nn(held_high, lay) + nn(held_low, lay)).astype(I32)
        values = jnp.where(line == 2 + i, wide, values)
    high, low = high_low(values)

    def down(count, shift):
        pick = hot((iota((count, DOM), 0) >> shift) == iota((count, DOM), 1))
        return (16.0 * nt(pick, high) + nt(pick, low)).astype(I32) - 1

    def along(count, shift):
        pick = hot((iota((DOM, count), 1) >> shift) == iota((DOM, count), 0))
        return (16.0 * nn(high, pick) + nn(low, pick)).astype(I32) - 1

    by_row = down(NODE, 3)
    m = iota((NODE, 1), 0)
    j = m & 7
    first, second, hub0, hub1 = [by_row[:, k : k + 1] for k in range(4)]
    pick_sig = jnp.where(j == 0, first, jnp.where(j == 1, second, -1))
    pick_sig = jnp.where(j == 2, hub0, jnp.where(j == 3, hub1, pick_sig))
    two = 2 * (m >> 3) + (j & 1)
    not_mine = (m >> 6) != slot
    pick_ext = jnp.where((j >> 1) == 2, two, -1)
    pick_ext = jnp.where(((j >> 1) == 1) & not_mine, BLK + two, pick_ext)
    last = [
        jnp.where(j == 6, first, jnp.where(j == 7, hub1, -1)),
        jnp.where(j == 6, second, -1),
        jnp.where(j == 6, hub0, -1),
    ]
    by_hub = down(BLK, 1)
    odd = (iota((BLK, 1), 0) & 1) == 1
    hub_col = jnp.where(odd, by_hub[:, 3:4], by_hub[:, 2:3])
    lane = iota((NODE, BLK), 1)
    hub_wide = jnp.concatenate([hub_col, jnp.full((NODE - BLK, 1), -1, I32)], 0)
    cols_out[...] = jnp.where(
        lane == 0, pick_sig, jnp.where(lane == 1, pick_ext, jnp.where(lane == 2, hub_wide, -1))
    )
    flat = along(NODE, 3)
    mr = iota((1, NODE), 1)
    jr = mr & 7
    back_row = jnp.where(jr == 4, flat[0:1], jnp.where(jr == 5, flat[1:2], -1))
    hub_back = jnp.where(((mr >> 2) & 1) == 0, flat[2:3], flat[3:4])
    flat_hub = along(BLK, 1)
    odd = (iota((1, BLK), 1) & 1) == 1
    hub_row = jnp.where(odd, flat_hub[3:4], flat_hub[2:3])
    hub_row = jnp.concatenate([hub_row, jnp.full((1, NODE - BLK), -1, I32)], 1)
    line = iota((8, NODE), 0)
    rows_out[...] = jnp.where(
        line == 0, back_row, jnp.where(line == 1, hub_back, jnp.where(line == 2, hub_row, -1))
    )

    acc[...] = jnp.zeros_like(acc)
    tile = tiles

    def add(i, carry):
        at = trow[i] * 6 + tcol[i]
        acc[at] += tile[i].astype(F32) * tmask[i].astype(F32)
        return carry

    lax.fori_loop(0, TILES, add, 0)
    for r in range(4):
        for c in range(6):
            block = acc[r * 6 + c]
            a_out[r * BLK : (r + 1) * BLK, c * BLK : (c + 1) * BLK] = block.astype(BF)
            at_out[c * BLK : (c + 1) * BLK, r * BLK : (r + 1) * BLK] = block.T.astype(BF)
    a_hub[...] = a_out[:, NODE + BLK :]
    from_sig = pick_rows(pick_sig, NODE)
    from_ext = pick_rows(pick_ext, EXT - NODE)
    for t in range(T1):
        ext = nn(at_out[NODE:, :], cot[t]).astype(BF)
        out = (
            nn(from_ext, ext)
            + nn(from_sig, sig[t])
            + nn(pick_rows(last[t], NODE), sig[HIST - 1])
        )
        send[:, t * C : (t + 1) * C] = out.astype(BF)


def own_kernel(conv, sig, cot, hid, fac_f, fac_g, mix0):
    total = jnp.zeros((C, C), F32)
    weights = conv
    for t in range(T1):
        h, p, q = gates(sig[t], sig[t + 1], weights)
        hid[t] = h
        fac_f[t] = p
        fac_g[t] = q
        total += tn(h, cot[t])
    mix0[...] = total


def hub_blocks(recv, owner, with_last):
    row = iota((8, NODE), 0)
    m = iota((8, NODE), 1)
    which = row >> 2
    step = row & 3
    forward = jnp.zeros((8, C), F32)
    backward = jnp.zeros((8, C), F32)
    for c in range(T1):
        block = recv[:, c * C : (c + 1) * C]
        f = (step == c) & (m == owner * 8 + 2 + which)
        if with_last and c == 2:
            f = f | ((row == 3) & (m == owner * 8 + 6))
        if with_last and c == 0:
            f = f | ((row == 7) & (m == owner * 8 + 7))
        b = (step == c) & ((m & 7) == 2 + which) & ((m >> 3) != owner)
        forward += nn(hot(f), block)
        backward += nn(hot(b), block)
    return forward, backward


def hub_kernel(me, owners, recv, send):
    owner = owners[me[0] >> 3]
    forward, backward = hub_blocks(recv, owner, True)
    at_owner = iota((DOM, 8, C), 0) == owner
    send[...] = jnp.where(at_owner, backward[None], forward[None]).astype(BF)


def halo_kernel(
    recv, conv, cols, rows, at_mat, a_mat, hid, cot, sig, back, hop, sig_x, hub_sig
):
    r = iota((BLK, NODE), 0)
    m = iota((BLK, NODE), 1)
    base = (r >> 1) * 8
    odd = r & 1
    pick0 = hot(m == base + odd)
    pick3a = hot((odd == 0) & (m == base + 6))
    pick3b = hot((odd == 1) & (m == base + 6))
    blocks = [recv[:, t * C : (t + 1) * C] for t in range(T1)]
    weights = conv
    far = [nn(pick0, block).astype(BF) for block in blocks]
    far.append((nn(pick3a, blocks[0]) + nn(pick3b, blocks[1])).astype(BF))
    for t in range(HIST):
        sig_x[t] = far[t]
    hid_x = [gates(far[t], far[t + 1], weights)[0] for t in range(T1)]
    put_halo = put_rows(rows[0:1, :], NODE)
    put_hub_own = put_rows(rows[2:3, 0:BLK], NODE)
    for t in range(T1):
        hub = nn(at_mat[NODE + BLK :, :], cot[t]).astype(BF)
        back[t] = (
            nn(at_mat[:NODE, :], cot[t]) + nn(put_halo, blocks[t]) + nn(put_hub_own, hub)
        )
        hop[t] = nn(a_mat[:, :NODE], hid[t]) + nn(a_mat[:, NODE : NODE + BLK], hid_x[t])
    own_pick = pick_rows(cols[0:BLK, 2:3], NODE)
    for t in range(HIST):
        hub_sig[t] = nn(own_pick, sig[t]).astype(BF)


def rows_kernel(
    recv, cols, rows, conv, hub_sig, a_hub, hop_part, back_part, at_mat,
    send, back_out, hop_out, ext_out, ext_hub, sig_x,
):
    r = iota((BLK, NODE), 0)
    m = iota((BLK, NODE), 1)
    base = (r >> 1) * 8 + (r & 1) * 4
    own_node = cols[0:BLK, 2:3]
    hubs = recv[...]
    far = []
    for t in range(HIST):
        hub_pick = hot((m == base + t) & (own_node < 0))
        far.append((nn(hub_pick, hubs) + hub_sig[t].astype(F32)).astype(BF))
        sig_x[t] = far[t]
    pick_sig = pick_rows(cols[:, 0:1], NODE)
    pick_ext = pick_rows(cols[:, 1:2], EXT - NODE)
    column = iota((NODE, NODE), 1)
    node = iota((NODE, NODE), 0)
    weights = conv
    for t in range(T1):
        h = gates(far[t], far[t + 1], weights)[0]
        hop = (hop_part[t] + nn(a_hub[...], h)).astype(BF)
        hop_out[t] = hop
        put_hub = hot((rows[1:2, :] == node) & ((column & 3) == t))
        back = (back_part[t] + nn(put_hub, hubs)).astype(BF)
        back_out[t] = back
        ext = nn(at_mat[...], back).astype(BF)
        out = nn(pick_sig, hop) + nn(pick_ext, ext[NODE:])
        send[:, t * C : (t + 1) * C] = out.astype(BF)
        ext_out[t] = ext
        ext_hub[t] = ext[NODE + BLK :]


def weight_kernel(
    core, conv, mix, hop, cot, back, ext, sig, sig_h, sig_u, fac_f, fac_g, mix0,
    keep, give, gh_out,
):
    grads = [[jnp.zeros((C, C), F32) for _ in range(2)] for _ in range(2)]
    mix1 = jnp.zeros((C, C), F32)
    mix2 = jnp.zeros((C, C), F32)
    weights = conv
    far_sig = [None] * HIST

    def far_at(t):
        if far_sig[t] is None:
            far_sig[t] = jnp.concatenate([sig_h[t], sig_u[t]], 0)
        return far_sig[t]

    for t in range(T1):
        mix1 += tn(hop[t], cot[t])
        mix2 += tn(hop[t], back[t])
        through = nt(ext[t], mix[2])
        gh = nt(cot[t], mix[0]) + nt(back[t], mix[1]) + through[:NODE]
        gh_out[t] = gh
        _, p, q = gates(far_at(t), far_at(t + 1), weights)
        own = ((gh * fac_f[t]).astype(BF), (gh * fac_g[t]).astype(BF))
        far = ((through[NODE:] * p).astype(BF), (through[NODE:] * q).astype(BF))
        for s in range(2):
            for k in range(2):
                grads[k][s] += tn(sig[t + s], own[k]) + tn(far_at(t + s), far[k])
    low = [grads[0][0], grads[0][1], grads[1][0], grads[1][1]]
    high = [mix0[...], mix1, mix2, jnp.zeros((C, C), F32)]
    first = core[0] == 0
    for k in range(4):
        stay = jnp.where(first, low[k], high[k])
        away = jnp.where(first, high[k], low[k])
        for s in range(2):
            at = (2 * k + s) * C
            give[at : at + C, :] = away[:, s * BLK : (s + 1) * BLK]
            keep[at : at + C, :] = stay[:, s * BLK : (s + 1) * BLK]


def pair_kernel(batch, keep, got, *outs):
    mine, other = keep, got
    for k in range(BATCH):
        at = pl.ds(pl.multiple_of(((batch[0] + k) & (BATCH - 1)) * NODE, NODE), NODE)
        outs[k][...] = (mine[at, :] + other[at, :]).astype(BF)


def second_hub_kernel(me, owners, recv, part0, part1, part2, part3, send):
    owner = owners[me[0] >> 3]
    forward, backward = hub_blocks(recv, owner, False)
    total = part0[...].astype(F32) + part1[...].astype(F32)
    total += part2[...].astype(F32) + part3[...].astype(F32)
    at_owner = iota((DOM, 8, C), 0) == owner
    send[:, :, 0:C] = jnp.where(at_owner, backward[None], forward[None]).astype(BF)
    send[:, :, C:] = total.astype(BF).reshape(DOM, 8, BLK)


def spread_kernel(recv, send):
    even = jnp.zeros((8, BLK), F32)
    odd = jnp.zeros((8, BLK), F32)
    for p in range(0, DOM, 2):
        even += recv[p, :, C:].astype(F32)
        odd += recv[p + 1, :, C:].astype(F32)
    is_odd = (iota((DOM, 8, BLK), 0) & 1) == 1
    send[...] = jnp.where(is_odd, odd[None], even[None]).astype(BF)


def near_kernel(
    recv, cols, rows, a_mat, mix, hop_ref, hid, sig, ext_hub, gh_ref, mixed, two, gh_out, hop_hub
):
    r = iota((BLK, NODE), 0)
    m = iota((BLK, NODE), 1)
    pick0 = hot(m == (r >> 1) * 8 + (r & 1))
    own_pick = pick_rows(cols[0:BLK, 2:3], NODE)
    put_halo = put_rows(rows[0:1, :], NODE)
    put_hub_own = put_rows(rows[2:3, 0:BLK], NODE)
    for t in range(T1):
        block = recv[:, t * C : (t + 1) * C]
        hop = hop_ref[t]
        rows_halo = nn(pick0, block).astype(BF)
        two[t] = nn(a_mat[:, :NODE], hop) + nn(a_mat[:, NODE : NODE + BLK], rows_halo)
        hop_hub[t] = nn(own_pick, hop).astype(BF)
        mixed[t] = sig[t + 1].astype(F32) + nn(hid[t], mix[0]) + nn(hop, mix[1])
        back = (nn(put_halo, block) + nn(put_hub_own, ext_hub[t])).astype(BF)
        gh_out[t] = gh_ref[t] + nt(back, mix[2])


def end_kernel(
    recv, cols, rows, a_hub, mix, conv, hop_hub, mixed, two_ref, gh_ref, fac_f, fac_g, cot,
    layer, sgrad,
):
    r = iota((BLK, NODE), 0)
    m = iota((BLK, NODE), 1)
    base = (r >> 1) * 8 + (r & 1) * 4
    own_node = cols[0:BLK, 2:3]
    column = iota((NODE, NODE), 1)
    node = iota((NODE, NODE), 0)
    hubs = recv[:, 0:C]
    for t in range(T1):
        hub_pick = hot((m == base + t) & (own_node < 0))
        rows_hub = (nn(hub_pick, hubs) + hop_hub[t].astype(F32)).astype(BF)
        two = (two_ref[t] + nn(a_hub[...], rows_hub)).astype(BF)
        layer[t] = (mixed[t] + nn(two, mix[2])).astype(BF)
        put_hub = hot((rows[1:2, :] == node) & ((column & 3) == t))
        gh = gh_ref[t] + nt(nn(put_hub, hubs).astype(BF), mix[2])
        gf = (gh * fac_f[t]).astype(BF)
        gg = (gh * fac_g[t]).astype(BF)
        early = nt(gf, conv[0, 0]) + nt(gg, conv[1, 0])
        late = nt(gf, conv[0, 1]) + nt(gg, conv[1, 1]) + cot[t].astype(F32)
        if t == 0:
            sgrad[0] = early.astype(BF)
        else:
            sgrad[t] = (early + carried).astype(BF)
        carried = late
    sgrad[T1] = carried.astype(BF)


def scale_kernel(core, batch, *refs):
    mine, other = refs[0:BATCH], refs[BATCH : 2 * BATCH]
    conv_grad, mix_grad = refs[2 * BATCH :]
    factor = 1.0 / math.sqrt(NODE * DOM * BATCH * T1)
    first = core[0] == 0
    for k in range(BATCH):
        block = (batch[0] + BATCH - k) & (BATCH - 1)
        for s in range(2):
            one = mine[k][s * C : (s + 1) * C, :].astype(F32) * factor
            two = other[k][s * C : (s + 1) * C, :].astype(F32) * factor
            lanes = slice(s * BLK, (s + 1) * BLK)
            conv_grad[block, :, lanes] = jnp.where(first, one, two)

            @pl.when(block < 3)
            def _():
                mix_grad[block, :, lanes] = jnp.where(first, two, one)


def swap(x, axis):
    return lax.all_to_all(x, axis, split_axis=0, concat_axis=0, tiled=True)


def body(
    signal,
    cotangent,
    conv,
    mix,
    send_rows,
    send_mask,
    tile_vals,
    tile_row,
    tile_col,
    tile_mask,
    hub_owner,
    hub_rows,
):
    me = lax.axis_index("dom").astype(I32)
    core = (me & 1).reshape(1)
    me = me.reshape(1)
    batch = lax.axis_index("batch").astype(I32).reshape(1)
    sig = jnp.transpose(signal[:, 0], (1, 0, 2))
    cot = jnp.transpose(cotangent[:, 0], (1, 0, 2))

    field = (T1, NODE, C)
    edge = (T1, BLK, C)
    edge4 = (HIST, BLK, C)
    half = (8 * C, BLK)
    chunk = (NODE, BLK)
    a_mat, a_hub, at_mat, cols, rows, send1 = call(
        start_kernel,
        [((NODE, EXT), BF), ((NODE, BLK), BF), ((EXT, NODE), BF), ((NODE, BLK), I32),
         ((8, NODE), I32), ((NODE, EXT), BF)],
        (tile_row, tile_col, tile_mask, me, hub_owner, tile_vals, send_rows.T, send_mask.T,
         hub_rows, cot, sig),
        smem=5,
        scratch=[pltpu.VMEM((24, BLK, BLK), F32)],
        flops=2 << 30,
    )
    recv1 = swap(send1.reshape(DOM, 8, EXT), "dom").reshape(NODE, EXT)
    hid, fac_f, fac_g, mix0 = call(
        own_kernel,
        [(field, BF), (field, F32), (field, F32), ((C, C), F32)],
        (conv, sig, cot),
        flops=8 << 30,
    )
    (send2,) = call(
        hub_kernel, [((DOM, 8, C), BF)], (me, hub_owner, recv1), 8, smem=2, flops=1 << 28
    )
    recv2 = swap(send2, "dom").reshape(NODE, C)
    back_part, hop_part, sig_h, hub_sig = call(
        halo_kernel,
        [(field, F32), (field, F32), (edge4, BF), (edge4, BF)],
        (recv1, conv, cols, rows, at_mat, a_mat, hid, cot, sig),
        flops=8 << 30,
    )
    send3, back, hop, ext, ext_hub, sig_u = call(
        rows_kernel,
        [((NODE, EXT), BF), (field, BF), (field, BF), ((T1, EXT, C), BF), (edge, BF),
         (edge4, BF)],
        (recv2, cols, rows, conv, hub_sig, a_hub, hop_part, back_part, at_mat),
        flops=4 << 30,
    )
    recv3 = swap(send3.reshape(DOM, 8, EXT), "dom").reshape(NODE, EXT)
    keep, give, gh = call(
        weight_kernel,
        [(half, F32), (half, F32), (field, F32)],
        (core, conv, mix, hop, cot, back, ext, sig, sig_h, sig_u, fac_f, fac_g, mix0),
        smem=1,
        flops=8 << 30,
    )
    pairs = [(i, i ^ 1) for i in range(DOM)]
    rounds = [[(i, (i + k) % BATCH) for i in range(BATCH)] for k in range(BATCH)]
    got = lax.ppermute(give, "dom", pairs)
    parts = call(
        pair_kernel, [(chunk, BF)] * BATCH, (batch, keep, got), 8, smem=1, flops=1 << 26
    )
    parts = [parts[0]] + [
        lax.ppermute(parts[k], "batch", rounds[k]) for k in range(1, BATCH)
    ]
    (send4,) = call(
        second_hub_kernel,
        [((DOM, 8, C + BLK), BF)],
        (me, hub_owner, recv3, *parts),
        8,
        smem=2,
        flops=1 << 28,
    )
    recv4 = swap(send4, "dom")
    mixed, two, gh, hop_hub = call(
        near_kernel,
        [(field, F32), (field, F32), (field, F32), (edge, BF)],
        (recv3, cols, rows, a_mat, mix, hop, hid, sig, ext_hub, gh),
        flops=8 << 30,
    )
    recv4, mixed, two, gh, hop_hub = lax.optimization_barrier((recv4, mixed, two, gh, hop_hub))
    (send5,) = call(spread_kernel, [((DOM, 8, BLK), BF)], (recv4,), 6, flops=1 << 26)
    recv5 = swap(send5, "dom").reshape(chunk)
    layer, sgrad = call(
        end_kernel,
        [(field, BF), ((HIST, NODE, C), BF)],
        (recv4.reshape(NODE, C + BLK), cols, rows, a_hub, mix, conv, hop_hub, mixed, two, gh,
         fac_f, fac_g, cot),
        flops=12 << 30,
    )
    layer = jnp.transpose(layer, (1, 0, 2))[:, None]
    sgrad = jnp.transpose(sgrad, (1, 0, 2))[:, None]
    recv5, layer, sgrad = lax.optimization_barrier((recv5, layer, sgrad))
    mine = [recv5] + [lax.ppermute(recv5, "batch", rounds[k]) for k in range(1, BATCH)]
    other = [lax.ppermute(one, "dom", pairs) for one in mine]
    conv_grad, mix_grad = call(
        scale_kernel,
        [((4, C, C), F32), ((3, C, C), F32)],
        (core, batch, *mine, *other),
        10,
        smem=2,
        flops=1 << 20,
    )
    return layer, sgrad, conv_grad.reshape(2, 2, C, C), mix_grad


def solution(mesh):
    placed = (
        P("dom", "batch", None, None),
        P("dom", "batch", None, None),
        P(),
        P(),
        P("dom", None),
        P("dom", None),
        P("dom", None, None),
        P("dom"),
        P("dom"),
        P("dom"),
        P(),
        P(),
    )
    return jax.shard_map(
        body,
        mesh=mesh,
        in_specs=placed,
        out_specs=(P("dom", "batch", None, None), P("dom", "batch", None, None), P(), P()),
        check_vma=False,
    )
```

time: 188 us -> 164 us (0.87)
  blocking collectives: 76.5 us -> 0 us
  starting transfers between devices: 24.1 us -> 54.7 us
  Pallas kernels: 38 us -> 57.1 us
  waiting for transfers between devices: 26.6 us -> 43.2 us
  local copies, waits for them, and re-layouts: 17.8 us -> 7.28 us
  other arithmetic: 3.1 us -> 0 us
    all_to_all x3 -> x0, blocking collectives: 76.5 us -> none  [swap(): return lax.all_to_all(x, axis, split_axis=0, concat_axis=0, tiled=True)]
    pallas_call x7 -> x12, Pallas kernels: 38 us -> 57.1 us  [call(): pl.pallas_call(kernel, out_shape=[jax.ShapeDtypeStruct(s, d) for s, d in...]
    all_to_all x3 -> x5, starting transfers between devices: 24.1 us -> 40.8 us  [swap(): return lax.all_to_all(x, axis, split_axis=0, concat_axis=0, tiled=True)]
    ppermute x0 -> x11, starting transfers between devices: none -> 13.9 us  [the longest x3 4.89 us: body(): lax.ppermute(parts[k], 'batch', rounds[k])]
    ppermute x0 -> x11, waiting for transfers between devices: none -> 9.34 us  [the longest x3 4.9 us: body(): lax.ppermute(parts[k], 'batch', rounds[k])]
    all_to_all x3 -> x5, waiting for transfers between devices: 26.6 us -> 33.8 us  [swap(): return lax.all_to_all(x, axis, split_axis=0, concat_axis=0, tiled=True)]
    unnamed x47 -> x14, local copies, waits for them, and re-layouts: 10.8 us -> 7.28 us
    slice x8 -> x0, local copies, waits for them, and re-layouts: 2.37 us -> none  [the longest x1 1.04 us: body(): whole[:4 * C].reshape(2, 2, C, C)]
  transfers between devices with their start and end apart: 3 -> 16, of which waited for: 2 -> 9; matrix products, arithmetic and copies ran while one was open for 2% -> 2% of each run, Pallas kernels for 9% -> 23%
where the time goes in v2:
time: 164 us; the launch traced here: 163 us
  Pallas kernels  57.1 us (35%)
  starting transfers between devices  54.7 us (33%)
  waiting for transfers between devices  43.2 us (26%)
  local copies, waits for them, and re-layouts  7.28 us (4%)
    pallas_call x12, Pallas kernels, call(): pl.pallas_call(kernel, out_shape=[jax.ShapeDtypeStruct(s, d) for s, d in...  57.1 us
    all_to_all x5, starting transfers between devices, swap(): return lax.all_to_all(x, axis, split_axis=0, concat_axis=0, tiled=True)  40.8 us
    all_to_all x5, waiting for transfers between devices, swap(): return lax.all_to_all(x, axis, split_axis=0, concat_axis=0, tiled=True)  33.8 us
    unnamed x14, local copies, waits for them, and re-layouts  7.28 us
    ppermute x3, waiting for transfers between devices, body(): lax.ppermute(parts[k], 'batch', rounds[k])  4.9 us
    ppermute x3, starting transfers between devices, body(): lax.ppermute(parts[k], 'batch', rounds[k])  4.89 us
    ppermute x3, starting transfers between devices, body(): lax.ppermute(recv5, 'batch', rounds[k])  4.45 us
    ppermute x4, starting transfers between devices, body(): other = [lax.ppermute(one, 'dom', pairs) for one in mine]  4.12 us
  transfers between devices with their start and end apart: 16, of which 9 were waited for; matrix products, arithmetic and copies ran while one was open for 2% of the time, Pallas kernels for 23%

profile of v2, /device:TPU:1, one launch (start us, length us, event | category | flops | bytes accessed | tf_op | source)
XLA Modules:
  0.0 163.0 jit_solution(4145623614072921113)
XLA Ops:
  0.6 2.3 %copy.19 = bf16[512,1,4,256]{3,0,2,1:T(8,128)(2,1)} copy(bf16[512,1,4,256]{3,2,1,0:T(4,128)(2,1)} %param.12) | data formatting | bytes 2097152 | tf_op args[0]
  3.0 5.7 %shard_map.147 = (bf16[512,768]{1,0:T(8,128)(2,1)}, bf16[512,128]{1,0:T(8,128)(2,1)}, bf16[768,512]{1,0:T(8,128)(2,1)}, s32[512,128]{1,0:T(8,128)}, s32[8,512]{1,0:T(8,128)}, /*index=5*/bf16[512,768]{1,0:T(8,128)(2,1)}) custom-call(s32[16]{0:T(128)} %trow.1, s32[16]{0:T(128)} %tcol.1, s32[16]{0:T(128)} %tmask.1, s32[1]{0:T(128)} %bitcast.me, s32[8]{0:T(128)} %owners.5, ...), custom_call_target="tpu_custom_call" | custom-call | flops 2147483648 | bytes 8388608 | tf_op jit(solution)/shard_map/pallas_call | solution.py:64
  8.7 13.2 %all-to-all-start = ((bf16[64,8,768]{2,1,0:T(8,128)(2,1)}), bf16[64,8,768]{2,1,0:T(8,128)(2,1)S(1)}, u32[]{:S(2)}, u32[]{:S(2)}) async-start(bf16[64,8,768]{2,1,0:T(8,128)(2,1)} %bitcast.44), calls=%async_computation | async-start | bytes 1572864 | tf_op jit(solution)/shard_map/all_to_all | solution.py:409
  21.9 0.0 copy-start.4
  21.9 5.2 %shard_map.149 = (bf16[3,512,256]{2,1,0:T(8,128)(2,1)}, f32[3,512,256]{2,1,0:T(8,128)}, f32[3,512,256]{2,1,0:T(8,128)}, f32[256,256]{1,0:T(8,128)}) custom-call(bf16[2,2,256,256]{3,2,1,0:T(8,128)(2,1)} %conv.9, bf16[4,512,256]{2,1,0:T(8,128)(2,1)} %bitcast.38, bf16[3,512,256]{2,1,0:T(8,128)(2,1)} %bitcast.48), custom_call_target="tpu_custom_call" | custom-call | flops 8589934592 | bytes 8388608 | tf_op jit(solution)/shard_map/pallas_call | solution.py:64
  27.1 17.5 %all-to-all-done = bf16[64,8,768]{2,1,0:T(8,128)(2,1)S(1)} async-done(((bf16[64,8,768]{2,1,0:T(8,128)(2,1)}), bf16[64,8,768]{2,1,0:T(8,128)(2,1)S(1)}, u32[]{:S(2)}, u32[]{:S(2)}) %all-to-all-start) | async-done | bytes 786464 | tf_op jit(solution)/shard_map/all_to_all | solution.py:409
  44.6 0.0 copy-start.1
  44.6 0.0 copy-done.4
  44.6 1.6 shard_map.148
  46.2 6.2 %all-to-all-start.1 = ((bf16[64,8,256]{2,1,0:T(8,128)(2,1)}), bf16[64,8,256]{2,1,0:T(8,128)(2,1)S(1)}, u32[]{:S(2)}, u32[]{:S(2)}) async-start(bf16[64,8,256]{2,1,0:T(8,128)(2,1)} %shard_map.148), calls=%async_computation.1 | async-start | bytes 524288 | tf_op jit(solution)/shard_map/all_to_all | solution.py:409
  52.5 0.0 copy-done.1
  52.5 6.7 %shard_map.150 = (f32[3,512,256]{2,1,0:T(8,128)}, f32[3,512,256]{2,1,0:T(8,128)}, bf16[4,128,256]{2,1,0:T(8,128)(2,1)}, bf16[4,128,256]{2,1,0:T(8,128)(2,1)}) custom-call(bf16[512,768]{1,0:T(8,128)(2,1)} %bitcast.30, bf16[2,2,256,256]{3,2,1,0:T(8,128)(2,1)} %conv.9, s32[512,128]{1,0:T(8,128)} %get-tuple-element.48.cols, s32[8,512]{1,0:T(8,128)} %get-tuple-element.49.rows, ...), custom_call_target="tpu_custom_call" | custom-call | flops 8589934592 | bytes 8388608 | tf_op jit(solution)/shard_map/pallas_call | solution.py:64
  59.2 6.5 %all-to-all-done.1 = bf16[64,8,256]{2,1,0:T(8,128)(2,1)S(1)} async-done(((bf16[64,8,256]{2,1,0:T(8,128)(2,1)}), bf16[64,8,256]{2,1,0:T(8,128)(2,1)S(1)}, u32[]{:S(2)}, u32[]{:S(2)}) %all-to-all-start.1) | async-done | bytes 262176 | tf_op jit(solution)/shard_map/all_to_all | solution.py:409
  65.6 0.0 copy-start.5
  65.6 0.7 copy-done.5
  66.3 7.9 %shard_map.151 = (bf16[512,768]{1,0:T(8,128)(2,1)}, bf16[3,512,256]{2,1,0:T(8,128)(2,1)}, bf16[3,512,256]{2,1,0:T(8,128)(2,1)}, bf16[3,768,256]{2,1,0:T(8,128)(2...) custom-call(bf16[512,256]{1,0:T(8,128)(2,1)} %bitcast.45, s32[512,128]{1,0:T(8,128)} %get-tuple-element.48.cols, ...), custom_call_target="tpu_custom_call" | custom-call | flops 4294967296 | bytes 8388608 | tf_op jit(solution)/shard_map/pallas_call | solution.py:64
  74.3 4.7 %all-to-all-start.2 = ((bf16[64,8,768]{2,1,0:T(8,128)(2,1)}), bf16[64,8,768]{2,1,0:T(8,128)(2,1)S(1)}, u32[]{:S(2)}, u32[]{:S(2)}) async-start(bf16[64,8,768]{2,1,0:T(8,128)(2,1)} %bitcast.43), calls=%async_computation.2 | async-start | bytes 1572864 | tf_op jit(solution)/shard_map/all_to_all | solution.py:409
  79.0 9.5 %shard_map.152 = (f32[2048,128]{1,0:T(8,128)}, f32[2048,128]{1,0:T(8,128)}, f32[3,512,256]{2,1,0:T(8,128)}) custom-call(s32[1]{0:T(128)} %bitcast.15.core, bf16[2,2,256,256]{3,2,1,0:T(8,128)(2,1)} %conv.9, bf16[3,256,256]{2,1,0:T(8,128)(2,1)} %mix.5, bf16[3,512,256]{2,1,0:T(8,128)(2,1)} %get-tuple-element.58.hop.hop_ref, bf16[3,512,256]{2,1,0:T(8,128)(2,1)} %bitcast.50, ...), custom_call_target="tpu_custom_call" | custom-call | flops 8589934592 | bytes 8388608 | tf_op jit(solution)/shard_map/pallas_call | solution.py:64
  88.5 0.5 collective-permute-start
  88.9 2.5 %collective-permute-done.got = f32[2048,128]{1,0:T(8,128)S(1)} collective-permute-done((f32[2048,128]{1,0:T(8,128)}, f32[2048,128]{1,0:T(8,128)S(1)}, u32[]{:S(2)}, u32[]{:S(2)}) %collective-permute-start) | collective-permute-done | bytes 1048608 | tf_op jit(solution)/shard_map/ppermute | solution.py:482
  91.4 0.0 copy-start.3
  91.4 1.2 copy-done.3
  92.7 0.2 shard_map.153
  92.9 1.3 collective-permute-start.1
  94.1 2.5 %collective-permute-start.2 = (bf16[512,128]{1,0:T(8,128)(2,1)S(1)}, bf16[512,128]{1,0:T(8,128)(2,1)S(1)}, u32[]{:S(2)}, u32[]{:S(2)}) collective-permute-start(bf16[512,128]{1,0:T(8,128)(2,1)S(1)} %get-tuple-element.70), channel_id=1, source_target_pairs={{0,2},{1,3},{2,0},{3,1},{4,6},{5,7},{6,4},{7,5},{8,10},{9,11},{10,... | collective-permute-start | bytes 393224 | tf_op jit(solution)/shard_map/ppermute | solution.py:487
  96.6 1.2 collective-permute-start.3
  97.7 1.1 collective-permute-done.1.part1
  98.8 3.8 %collective-permute-done.2.part2 = bf16[512,128]{1,0:T(8,128)(2,1)S(1)} collective-permute-done((bf16[512,128]{1,0:T(8,128)(2,1)S(1)}, bf16[512,128]{1,0:T(8,128)(2,1)S(1)}, u32[]{:S(2)}, u32[]{:S(2)}) %collective-permute-start.2) | collective-permute-done | bytes 131104 | tf_op jit(solution)/shard_map/ppermute | solution.py:487
  102.6 0.0 collective-permute-done.3.part3
  102.6 0.0 all-to-all-done.2
  102.7 0.0 copy-start
  102.7 1.7 %shard_map.154 = bf16[64,8,384]{2,1,0:T(8,128)(2,1)} custom-call(s32[1]{0:T(128)} %bitcast.me, s32[8]{0:T(128)S(1)} %copy-done.4, bf16[512,768]{1,0:T(8,128)(2,1)S(1)} %bitcast.27, bf16[512,128]{1,0:T(8,128)(2,1)S(1)} %get-tuple-element.68.part0, bf16[512,128]{1,0:T(8,128)(2,1)S(1)} %collective-permute-done.1.part1, ...), custom_call_target="tpu_custom_call" | custom-call | flops 268435456 | bytes 8388608 | tf_op jit(solution)/shard_map/pallas_call | solution.py:64
  104.4 11.1 %all-to-all-start.3 = ((bf16[64,8,384]{2,1,0:T(8,128)(2,1)}), bf16[64,8,384]{2,1,0:T(8,128)(2,1)S(1)}, u32[]{:S(2)}, u32[]{:S(2)}) async-start(bf16[64,8,384]{2,1,0:T(8,128)(2,1)} %shard_map.154), calls=%async_computation.3 | async-start | bytes 786432 | tf_op jit(solution)/shard_map/all_to_all | solution.py:409
  115.4 0.0 copy-done
  115.4 8.0 %shard_map.155 = (f32[3,512,256]{2,1,0:T(8,128)}, f32[3,512,256]{2,1,0:T(8,128)}, f32[3,512,256]{2,1,0:T(8,128)}, bf16[3,128,256]{2,1,0:T(8,128)(2,1)}) custom-call(bf16[512,768]{1,0:T(8,128)(2,1)} %bitcast.28, s32[512,128]{1,0:T(8,128)} %get-tuple-element.48.cols, s32[8,512]{1,0:T(8,128)} %get-tuple-element.49.rows, ...), custom_call_target="tpu_custom_call" | custom-call | flops 8589934592 | bytes 8388608 | tf_op jit(solution)/shard_map/pallas_call | solution.py:64
  123.5 7.0 %all-to-all-done.3.recv = bf16[64,8,384]{2,1,0:T(8,128)(2,1)S(1)} async-done(((bf16[64,8,384]{2,1,0:T(8,128)(2,1)}), bf16[64,8,384]{2,1,0:T(8,128)(2,1)S(1)}, u32[]{:S(2)}, u32[]{:S(2)}) %all-to-all-start.3) | async-done | bytes 393248 | tf_op jit(solution)/shard_map/all_to_all | solution.py:409
  130.5 0.0 copy-start.2
  130.5 0.8 shard_map.156
  131.2 5.6 %all-to-all-start.4 = ((bf16[64,8,128]{2,1,0:T(8,128)(2,1)}), bf16[64,8,128]{2,1,0:T(8,128)(2,1)S(1)}, u32[]{:S(2)}, u32[]{:S(2)}) async-start(bf16[64,8,128]{2,1,0:T(8,128)(2,1)} %shard_map.156), calls=%async_computation.4 | async-start | bytes 262144 | tf_op jit(solution)/shard_map/all_to_all | solution.py:409
  136.8 0.0 copy-done.2
  136.9 8.3 %shard_map.157 = (bf16[3,512,256]{2,1,0:T(8,128)(2,1)}, bf16[4,512,256]{2,1,0:T(8,128)(2,1)}) custom-call(bf16[512,384]{1,0:T(8,128)(2,1)} %bitcast.31, s32[512,128]{1,0:T(8,128)} %get-tuple-element.48.cols, s32[8,512]{1,0:T(8,128)} %get-tuple-element.49.rows, bf16[512,128]{1,0:T(8,128)(2,1)} %get-tuple-element.54.a_hub, bf16[3,256,256]{2,1,0:T(8,128)(2,1)} %mix.5, ...), custom_call_target="tpu_custom_call" | custom-call | flops 12884901888 | bytes 8388608 | tf_op jit(solution)/shard_map/pallas_call | solution.py:64
  145.2 2.8 %all-to-all-done.4 = bf16[64,8,128]{2,1,0:T(8,128)(2,1)S(1)} async-done(((bf16[64,8,128]{2,1,0:T(8,128)(2,1)}), bf16[64,8,128]{2,1,0:T(8,128)(2,1)S(1)}, u32[]{:S(2)}, u32[]{:S(2)}) %all-to-all-start.4) | async-done | bytes 131104 | tf_op jit(solution)/shard_map/all_to_all | solution.py:409
  148.0 1.1 collective-permute-start.4
  149.0 2.1 %collective-permute-start.5 = (bf16[512,128]{1,0:T(8,128)(2,1)S(1)}, bf16[512,128]{1,0:T(8,128)(2,1)S(1)}, u32[]{:S(2)}, u32[]{:S(2)}) collective-permute-start(bf16[512,128]{1,0:T(8,128)(2,1)S(1)} %bitcast.33), channel_id=1, source_target_pairs={{0,2},{1,3},{2,0},{3,1},{4,6},{5,7},{6,4},{7,5},{8,10},{9,11},{10,... | collective-permute-start | bytes 393224 | tf_op jit(solution)/shard_map/ppermute | solution.py:517
  151.1 1.3 collective-permute-start.6
  152.4 1.2 collective-permute-start.7
  153.6 0.2 collective-permute-done.4.refs_1_
  153.8 1.6 collective-permute-start.8
  155.4 1.7 %collective-permute-done.5.refs_2_ = bf16[512,128]{1,0:T(8,128)(2,1)S(1)} collective-permute-done((bf16[512,128]{1,0:T(8,128)(2,1)S(1)}, bf16[512,128]{1,0:T(8,128)(2,1)S(1)}, u32[]{:S(2)}, u32[]{:S(2)}) %collective-permute-start.5) | collective-permute-done | bytes 131104 | tf_op jit(solution)/shard_map/ppermute | solution.py:517
  157.1 1.2 collective-permute-start.9
  158.4 0.0 collective-permute-done.6.refs_3_
  158.4 0.1 collective-permute-start.10
  158.5 3.0 %copy.17 = bf16[512,1,4,256]{3,2,1,0:T(4,128)(2,1)} copy(bf16[512,1,4,256]{3,0,2,1:T(8,128)(2,1)} %bitcast.42) | data formatting | bytes 2097152
  161.5 0.0 collective-permute-done.7.refs_4_
  161.5 0.0 collective-permute-done.8.refs_5_
  161.5 0.0 collective-permute-done.9.refs_6_
  161.5 0.0 collective-permute-done.10.refs_7_
  161.5 1.5 shard_map.158
Async XLA Ops:
  8.7 35.9 %all-to-all-start = ((bf16[64,8,768]{2,1,0:T(8,128)(2,1)}), bf16[64,8,768]{2,1,0:T(8,128)(2,1)S(1)}, u32[]{:S(2)}, u32[]{:S(2)}) async-start(bf16[64,8,768]{2,1,0:T(8,128)(2,1)} %bitcast.44), calls=%async_computation | async-start | bytes 1572864 | tf_op jit(solution)/shard_map/all_to_all | solution.py:409
  21.9 22.8 %copy-start.4 = (s32[8]{0:T(128)S(1)}, s32[8]{0:T(128)}, u32[]{:S(2)}) copy-start(s32[8]{0:T(128)} %owners.5) | copy-start | bytes 100
  44.6 7.9 %copy-start.1 = (bf16[64,8,768]{2,1,0:T(8,128)(2,1)}, bf16[64,8,768]{2,1,0:T(8,128)(2,1)S(1)}, u32[]{:S(2)}) copy-start(bf16[64,8,768]{2,1,0:T(8,128)(2,1)S(1)} %all-to-all-done) | copy-start | bytes 2359300
  46.2 19.4 %all-to-all-start.1 = ((bf16[64,8,256]{2,1,0:T(8,128)(2,1)}), bf16[64,8,256]{2,1,0:T(8,128)(2,1)S(1)}, u32[]{:S(2)}, u32[]{:S(2)}) async-start(bf16[64,8,256]{2,1,0:T(8,128)(2,1)} %shard_map.148), calls=%async_computation.1 | async-start | bytes 524288 | tf_op jit(solution)/shard_map/all_to_all | solution.py:409
  65.6 0.7 copy-start.5
  74.3 28.4 %all-to-all-start.2 = ((bf16[64,8,768]{2,1,0:T(8,128)(2,1)}), bf16[64,8,768]{2,1,0:T(8,128)(2,1)S(1)}, u32[]{:S(2)}, u32[]{:S(2)}) async-start(bf16[64,8,768]{2,1,0:T(8,128)(2,1)} %bitcast.43), calls=%async_computation.2 | async-start | bytes 1572864 | tf_op jit(solution)/shard_map/all_to_all | solution.py:409
  88.5 3.0 %collective-permute-start = (f32[2048,128]{1,0:T(8,128)}, f32[2048,128]{1,0:T(8,128)S(1)}, u32[]{:S(2)}, u32[]{:S(2)}) collective-permute-start(f32[2048,128]{1,0:T(8,128)} %get-tuple-element.67), channel_id=1, source_target_pairs={{0,4},{4,0},{8,12},{12,8},{16,20},{20,16},{24,28},{28,24},{32,36},... | collective-permute-start | bytes 3145736 | tf_op jit(solution)/shard_map/ppermute | solution.py:482
  91.4 1.2 copy-start.3
  92.9 6.0 %collective-permute-start.1 = (bf16[512,128]{1,0:T(8,128)(2,1)S(1)}, bf16[512,128]{1,0:T(8,128)(2,1)S(1)}, u32[]{:S(2)}, u32[]{:S(2)}) collective-permute-start(bf16[512,128]{1,0:T(8,128)(2,1)S(1)} %get-tuple-element.69), channel_id=1, source_target_pairs={{0,1},{1,2},{2,3},{3,0},{4,5},{5,6},{6,7},{7,4},{8,9},{9,10},{10,1... | collective-permute-start | bytes 393224 | tf_op jit(solution)/shard_map/ppermute | solution.py:487
  94.1 8.5 %collective-permute-start.2 = (bf16[512,128]{1,0:T(8,128)(2,1)S(1)}, bf16[512,128]{1,0:T(8,128)(2,1)S(1)}, u32[]{:S(2)}, u32[]{:S(2)}) collective-permute-start(bf16[512,128]{1,0:T(8,128)(2,1)S(1)} %get-tuple-element.70), channel_id=1, source_target_pairs={{0,2},{1,3},{2,0},{3,1},{4,6},{5,7},{6,4},{7,5},{8,10},{9,11},{10,... | collective-permute-start | bytes 393224 | tf_op jit(solution)/shard_map/ppermute | solution.py:487
  96.6 6.1 %collective-permute-start.3 = (bf16[512,128]{1,0:T(8,128)(2,1)S(1)}, bf16[512,128]{1,0:T(8,128)(2,1)S(1)}, u32[]{:S(2)}, u32[]{:S(2)}) collective-permute-start(bf16[512,128]{1,0:T(8,128)(2,1)S(1)} %get-tuple-element.71), channel_id=1, source_target_pairs={{0,3},{1,0},{2,1},{3,2},{4,7},{5,4},{6,5},{7,6},{8,11},{9,8},{10,9... | collective-permute-start | bytes 393224 | tf_op jit(solution)/shard_map/ppermute | solution.py:487
  102.7 12.8 %copy-start = (bf16[64,8,768]{2,1,0:T(8,128)(2,1)}, bf16[64,8,768]{2,1,0:T(8,128)(2,1)S(1)}, u32[]{:S(2)}) copy-start(bf16[64,8,768]{2,1,0:T(8,128)(2,1)S(1)} %all-to-all-done.2) | copy-start | bytes 2359300
  104.4 26.1 %all-to-all-start.3 = ((bf16[64,8,384]{2,1,0:T(8,128)(2,1)}), bf16[64,8,384]{2,1,0:T(8,128)(2,1)S(1)}, u32[]{:S(2)}, u32[]{:S(2)}) async-start(bf16[64,8,384]{2,1,0:T(8,128)(2,1)} %shard_map.154), calls=%async_computation.3 | async-start | bytes 786432 | tf_op jit(solution)/shard_map/all_to_all | solution.py:409
  130.5 6.4 %copy-start.2 = (bf16[64,8,384]{2,1,0:T(8,128)(2,1)}, bf16[64,8,384]{2,1,0:T(8,128)(2,1)S(1)}, u32[]{:S(2)}) copy-start(bf16[64,8,384]{2,1,0:T(8,128)(2,1)S(1)} %all-to-all-done.3.recv) | copy-start | bytes 1179652
  131.2 16.7 %all-to-all-start.4 = ((bf16[64,8,128]{2,1,0:T(8,128)(2,1)}), bf16[64,8,128]{2,1,0:T(8,128)(2,1)S(1)}, u32[]{:S(2)}, u32[]{:S(2)}) async-start(bf16[64,8,128]{2,1,0:T(8,128)(2,1)} %shard_map.156), calls=%async_computation.4 | async-start | bytes 262144 | tf_op jit(solution)/shard_map/all_to_all | solution.py:409
  148.0 5.9 %collective-permute-start.4 = (bf16[512,128]{1,0:T(8,128)(2,1)S(1)}, bf16[512,128]{1,0:T(8,128)(2,1)S(1)}, u32[]{:S(2)}, u32[]{:S(2)}) collective-permute-start(bf16[512,128]{1,0:T(8,128)(2,1)S(1)} %bitcast.32), channel_id=1, source_target_pairs={{0,1},{1,2},{2,3},{3,0},{4,5},{5,6},{6,7},{7,4},{8,9},{9,10},{10,1... | collective-permute-start | bytes 393224 | tf_op jit(solution)/shard_map/ppermute | solution.py:517
  149.0 8.1 %collective-permute-start.5 = (bf16[512,128]{1,0:T(8,128)(2,1)S(1)}, bf16[512,128]{1,0:T(8,128)(2,1)S(1)}, u32[]{:S(2)}, u32[]{:S(2)}) collective-permute-start(bf16[512,128]{1,0:T(8,128)(2,1)S(1)} %bitcast.33), channel_id=1, source_target_pairs={{0,2},{1,3},{2,0},{3,1},{4,6},{5,7},{6,4},{7,5},{8,10},{9,11},{10,... | collective-permute-start | bytes 393224 | tf_op jit(solution)/shard_map/ppermute | solution.py:517
  151.1 7.3 %collective-permute-start.6 = (bf16[512,128]{1,0:T(8,128)(2,1)S(1)}, bf16[512,128]{1,0:T(8,128)(2,1)S(1)}, u32[]{:S(2)}, u32[]{:S(2)}) collective-permute-start(bf16[512,128]{1,0:T(8,128)(2,1)S(1)} %bitcast.34), channel_id=1, source_target_pairs={{0,3},{1,0},{2,1},{3,2},{4,7},{5,4},{6,5},{7,6},{8,11},{9,8},{10,9... | collective-permute-start | bytes 393224 | tf_op jit(solution)/shard_map/ppermute | solution.py:517
  152.4 9.1 %collective-permute-start.7 = (bf16[512,128]{1,0:T(8,128)(2,1)S(1)}, bf16[512,128]{1,0:T(8,128)(2,1)S(1)}, u32[]{:S(2)}, u32[]{:S(2)}) collective-permute-start(bf16[512,128]{1,0:T(8,128)(2,1)S(1)} %bitcast.35), channel_id=1, source_target_pairs={{0,4},{4,0},{8,12},{12,8},{16,20},{20,16},{24,28},{28,24},{32,36},... | collective-permute-start | bytes 393224 | tf_op jit(solution)/shard_map/ppermute | solution.py:518
  153.8 7.6 %collective-permute-start.8 = (bf16[512,128]{1,0:T(8,128)(2,1)S(1)}, bf16[512,128]{1,0:T(8,128)(2,1)S(1)}, u32[]{:S(2)}, u32[]{:S(2)}) collective-permute-start(bf16[512,128]{1,0:T(8,128)(2,1)S(1)} %collective-permute-done.4.refs_1_), channel_id=1, source_target_pairs={{0,4},{4,0},{8,12},{12,8},{16,20},{20,16},{24,28},{28,24},{32,36},... | collective-permute-start | bytes 393224 | tf_op jit(solution)/shard_map/ppermute | solution.py:518
  157.1 4.3 %collective-permute-start.9 = (bf16[512,128]{1,0:T(8,128)(2,1)S(1)}, bf16[512,128]{1,0:T(8,128)(2,1)S(1)}, u32[]{:S(2)}, u32[]{:S(2)}) collective-permute-start(bf16[512,128]{1,0:T(8,128)(2,1)S(1)} %collective-permute-done.5.refs_2_), channel_id=1, source_target_pairs={{0,4},{4,0},{8,12},{12,8},{16,20},{20,16},{24,28},{28,24},{32,36},... | collective-permute-start | bytes 393224 | tf_op jit(solution)/shard_map/ppermute | solution.py:518
  158.4 3.1 %collective-permute-start.10 = (bf16[512,128]{1,0:T(8,128)(2,1)S(1)}, bf16[512,128]{1,0:T(8,128)(2,1)S(1)}, u32[]{:S(2)}, u32[]{:S(2)}) collective-permute-start(bf16[512,128]{1,0:T(8,128)(2,1)S(1)} %collective-permute-done.6.refs_3_), channel_id=1, source_target_pairs={{0,4},{4,0},{8,12},{12,8},{16,20},{20,16},{24,28},{28,24},{32,36},... | collective-permute-start | bytes 393224 | tf_op jit(solution)/shard_map/ppermute | solution.py:518

commit v3 on v2

--- a/solution.py
+++ b/solution.py
@@ -72,17 +72,67 @@
     )(*args)
 
 
+def stepped(kernel, outs, args, kinds, out_kinds, smem=0, scratch=(), flops=0):
+    def spec(shape, kind):
+        if kind == "all":
+            return pl.BlockSpec(shape, lambda t: (0,) * len(shape))
+        if kind == "lanes":
+            return pl.BlockSpec((shape[0], C), lambda t: (0, t))
+        ahead = 1 if kind == "next" else 0
+        return pl.BlockSpec((1,) + shape[1:], lambda t: (t + ahead,) + (0,) * (len(shape) - 1))
+
+    return pl.pallas_call(
+        kernel,
+        grid=(T1,),
+        out_shape=[jax.ShapeDtypeStruct(s, d) for s, d in outs],
+        in_specs=[pl.BlockSpec(memory_space=pltpu.SMEM)] * smem
+        + [spec(x.shape, k) for x, k in zip(args[smem:], kinds)],
+        out_specs=[spec(s, k) for (s, d), k in zip(outs, out_kinds)],
+        scratch_shapes=list(scratch),
+        compiler_params=pltpu.CompilerParams(vmem_limit_bytes=60 << 20),
+        cost_estimate=pl.CostEstimate(flops=flops, bytes_accessed=8 << 20, transcendentals=0),
+    )(*args)
+
+
 def high_low(x):
     return (x >> 4).astype(F32).astype(BF), (x & 15).astype(F32).astype(BF)
 
 
-def start_kernel(
-    trow, tcol, tmask, me, owners, tiles, used_rows, used_mask, hubs, cot, sig,
-    a_out, a_hub, at_out, cols_out, rows_out, send, acc,
-):
+def add_tiles(acc, trow, tcol, tmask, tiles, low):
+    acc[...] = jnp.zeros_like(acc)
+
+    def add(i, carry):
+        @pl.when((tmask[i] == 1) & (tcol[i] >= low))
+        def _():
+            acc[(tcol[i] - low) * 4 + trow[i]] += tiles[i].astype(F32)
+
+        return carry
+
+    lax.fori_loop(0, TILES, add, 0)
+
+
+def slot_of(me, owners):
     slot = jnp.int32(-1)
     for o in range(OWNERS):
         slot = jnp.where(owners[o] == me[0], o, slot)
+    return slot
+
+
+def own_hub_block(me, owners, rows, recv):
+    at = pl.multiple_of(jnp.maximum(slot_of(me, owners), 0) * DOM, DOM)
+    return recv[pl.ds(at, DOM), 0:C], rows[3:4, 0:DOM]
+
+
+def put_step(target, t):
+    at = iota((NODE, DOM), 1)
+    return hot((target == iota((NODE, DOM), 0)) & ((at & 3) == t))
+
+
+def start_kernel(
+    trow, tcol, tmask, me, owners, tiles, used_rows, used_mask, hubs, cot, sig,
+    cols_out, rows_out, send, acc, far,
+):
+    slot = slot_of(me, owners)
     used = jnp.where(used_mask[...] == 1, used_rows[...] + 1, 0)
     held = jnp.where(iota((OWNERS, HUB_PER), 0) == slot, hubs[...] + 1, 0)
     held = jnp.broadcast_to(jnp.sum(held, 0, keepdims=True), (8, HUB_PER))
@@ -132,35 +182,28 @@
     mr = iota((1, NODE), 1)
     jr = mr & 7
     back_row = jnp.where(jr == 4, flat[0:1], jnp.where(jr == 5, flat[1:2], -1))
-    hub_back = jnp.where(((mr >> 2) & 1) == 0, flat[2:3], flat[3:4])
     flat_hub = along(BLK, 1)
     odd = (iota((1, BLK), 1) & 1) == 1
     hub_row = jnp.where(odd, flat_hub[3:4], flat_hub[2:3])
     hub_row = jnp.concatenate([hub_row, jnp.full((1, NODE - BLK), -1, I32)], 1)
+    j16 = iota((HUB_PER, NODE), 0)
+    at = iota((HUB_PER, NODE), 1)
+    lay = hot((j16 == 2 * (at >> 3) + ((at >> 2) & 1)) & (at < DOM))
+    hub_mine = (16.0 * nn(held_high, lay) + nn(held_low, lay)).astype(I32)[0:1] - 1
     line = iota((8, NODE), 0)
     rows_out[...] = jnp.where(
-        line == 0, back_row, jnp.where(line == 1, hub_back, jnp.where(line == 2, hub_row, -1))
-    )
-
-    acc[...] = jnp.zeros_like(acc)
-    tile = tiles
-
-    def add(i, carry):
-        at = trow[i] * 6 + tcol[i]
-        acc[at] += tile[i].astype(F32) * tmask[i].astype(F32)
-        return carry
-
-    lax.fori_loop(0, TILES, add, 0)
+        line == 0, back_row, jnp.where(line == 2, hub_row, jnp.where(line == 3, hub_mine, -1))
+    )
+
+    add_tiles(acc, trow, tcol, tmask, tiles, 4)
     for r in range(4):
-        for c in range(6):
-            block = acc[r * 6 + c]
-            a_out[r * BLK : (r + 1) * BLK, c * BLK : (c + 1) * BLK] = block.astype(BF)
-            at_out[c * BLK : (c + 1) * BLK, r * BLK : (r + 1) * BLK] = block.T.astype(BF)
-    a_hub[...] = a_out[:, NODE + BLK :]
+        for c in range(2):
+            block = acc[c * 4 + r]
+            far[c * BLK : (c + 1) * BLK, r * BLK : (r + 1) * BLK] = block.T.astype(BF)
     from_sig = pick_rows(pick_sig, NODE)
     from_ext = pick_rows(pick_ext, EXT - NODE)
     for t in range(T1):
-        ext = nn(at_out[NODE:, :], cot[t]).astype(BF)
+        ext = nn(far[...], cot[t]).astype(BF)
         out = (
             nn(from_ext, ext)
             + nn(from_sig, sig[t])
@@ -169,7 +212,16 @@
         send[:, t * C : (t + 1) * C] = out.astype(BF)
 
 
-def own_kernel(conv, sig, cot, hid, fac_f, fac_g, mix0):
+def own_kernel(
+    trow, tcol, tmask, tiles, conv, sig, cot, a_out, a_hub, at_out, hid, fac_f, fac_g, mix0, acc
+):
+    add_tiles(acc, trow, tcol, tmask, tiles, 0)
+    for r in range(4):
+        for c in range(6):
+            block = acc[c * 4 + r]
+            a_out[r * BLK : (r + 1) * BLK, c * BLK : (c + 1) * BLK] = block.astype(BF)
+            at_out[c * BLK : (c + 1) * BLK, r * BLK : (r + 1) * BLK] = block.T.astype(BF)
+    a_hub[...] = a_out[:, NODE + BLK :]
     total = jnp.zeros((C, C), F32)
     weights = conv
     for t in range(T1):
@@ -239,75 +291,76 @@
 
 
 def rows_kernel(
-    recv, cols, rows, conv, hub_sig, a_hub, hop_part, back_part, at_mat,
-    send, back_out, hop_out, ext_out, ext_hub, sig_x,
-):
+    me, owners, recv, cols, rows, conv, hub0, hub1, a_hub, hop_part, back_part, at_mat,
+    send, back_out, hop_out, ext_out, ext_hub, sig_x, pick_sig, pick_ext,
+):
+    t = pl.program_id(0)
+
+    @pl.when(t == 0)
+    def _():
+        pick_sig[...] = pick_rows(cols[:, 0:1], NODE)
+        pick_ext[...] = pick_rows(cols[:, 1:2], EXT - NODE)
+
     r = iota((BLK, NODE), 0)
     m = iota((BLK, NODE), 1)
     base = (r >> 1) * 8 + (r & 1) * 4
     own_node = cols[0:BLK, 2:3]
     hubs = recv[...]
     far = []
-    for t in range(HIST):
-        hub_pick = hot((m == base + t) & (own_node < 0))
-        far.append((nn(hub_pick, hubs) + hub_sig[t].astype(F32)).astype(BF))
-        sig_x[t] = far[t]
-    pick_sig = pick_rows(cols[:, 0:1], NODE)
-    pick_ext = pick_rows(cols[:, 1:2], EXT - NODE)
-    column = iota((NODE, NODE), 1)
-    node = iota((NODE, NODE), 0)
-    weights = conv
-    for t in range(T1):
-        h = gates(far[t], far[t + 1], weights)[0]
-        hop = (hop_part[t] + nn(a_hub[...], h)).astype(BF)
-        hop_out[t] = hop
-        put_hub = hot((rows[1:2, :] == node) & ((column & 3) == t))
-        back = (back_part[t] + nn(put_hub, hubs)).astype(BF)
-        back_out[t] = back
-        ext = nn(at_mat[...], back).astype(BF)
-        out = nn(pick_sig, hop) + nn(pick_ext, ext[NODE:])
-        send[:, t * C : (t + 1) * C] = out.astype(BF)
-        ext_out[t] = ext
-        ext_hub[t] = ext[NODE + BLK :]
+    for s, hub_sig in ((0, hub0), (1, hub1)):
+        hub_pick = hot((m == base + (t + s)) & (own_node < 0))
+        far.append((nn(hub_pick, hubs) + hub_sig[0].astype(F32)).astype(BF))
+        sig_x[t + s] = far[s]
+    mine, target = own_hub_block(me, owners, rows, recv)
+    h = gates(far[0], far[1], conv)[0]
+    hop = (hop_part[0] + nn(a_hub[...], h)).astype(BF)
+    hop_out[0] = hop
+    back = (back_part[0] + nn(put_step(target, t), mine)).astype(BF)
+    back_out[0] = back
+    ext = nn(at_mat[...], back).astype(BF)
+    out = nn(pick_sig[...], hop) + nn(pick_ext[...], ext[NODE:])
+    send[...] = out.astype(BF)
+    ext_out[0] = ext
+    ext_hub[0] = ext[NODE + BLK :]
 
 
 def weight_kernel(
-    core, conv, mix, hop, cot, back, ext, sig, sig_h, sig_u, fac_f, fac_g, mix0,
-    keep, give, gh_out,
-):
-    grads = [[jnp.zeros((C, C), F32) for _ in range(2)] for _ in range(2)]
-    mix1 = jnp.zeros((C, C), F32)
-    mix2 = jnp.zeros((C, C), F32)
-    weights = conv
-    far_sig = [None] * HIST
-
-    def far_at(t):
-        if far_sig[t] is None:
-            far_sig[t] = jnp.concatenate([sig_h[t], sig_u[t]], 0)
-        return far_sig[t]
-
-    for t in range(T1):
-        mix1 += tn(hop[t], cot[t])
-        mix2 += tn(hop[t], back[t])
-        through = nt(ext[t], mix[2])
-        gh = nt(cot[t], mix[0]) + nt(back[t], mix[1]) + through[:NODE]
-        gh_out[t] = gh
-        _, p, q = gates(far_at(t), far_at(t + 1), weights)
-        own = ((gh * fac_f[t]).astype(BF), (gh * fac_g[t]).astype(BF))
-        far = ((through[NODE:] * p).astype(BF), (through[NODE:] * q).astype(BF))
-        for s in range(2):
-            for k in range(2):
-                grads[k][s] += tn(sig[t + s], own[k]) + tn(far_at(t + s), far[k])
-    low = [grads[0][0], grads[0][1], grads[1][0], grads[1][1]]
-    high = [mix0[...], mix1, mix2, jnp.zeros((C, C), F32)]
-    first = core[0] == 0
-    for k in range(4):
-        stay = jnp.where(first, low[k], high[k])
-        away = jnp.where(first, high[k], low[k])
-        for s in range(2):
-            at = (2 * k + s) * C
-            give[at : at + C, :] = away[:, s * BLK : (s + 1) * BLK]
-            keep[at : at + C, :] = stay[:, s * BLK : (s + 1) * BLK]
+    core, conv, mix, hop, cot, back, ext, sig0, sig1, halo0, halo1, hub0, hub1, fac_f, fac_g,
+    mix0, keep, give, acc,
+):
+    t = pl.program_id(0)
+
+    @pl.when(t == 0)
+    def _():
+        acc[...] = jnp.zeros_like(acc)
+
+    acc[4] += tn(hop[0], cot[0])
+    acc[5] += tn(hop[0], back[0])
+    through = nt(ext[0], mix[2])
+    gh = nt(cot[0], mix[0]) + nt(back[0], mix[1]) + through[:NODE]
+    far_sig = (
+        jnp.concatenate([halo0[0], hub0[0]], 0),
+        jnp.concatenate([halo1[0], hub1[0]], 0),
+    )
+    _, p, q = gates(far_sig[0], far_sig[1], conv)
+    own = ((gh * fac_f[0]).astype(BF), (gh * fac_g[0]).astype(BF))
+    far = ((through[NODE:] * p).astype(BF), (through[NODE:] * q).astype(BF))
+    for s, sig in ((0, sig0), (1, sig1)):
+        for k in range(2):
+            acc[2 * k + s] += tn(sig[0], own[k]) + tn(far_sig[s], far[k])
+
+    @pl.when(t == T1 - 1)
+    def _():
+        first = core[0] == 0
+        for k in range(4):
+            low = acc[k]
+            high = (mix0[...], acc[4], acc[5], jnp.zeros((C, C), F32))[k]
+            stay = jnp.where(first, low, high)
+            away = jnp.where(first, high, low)
+            for s in range(2):
+                at = (2 * k + s) * C
+                give[at : at + C, :] = away[:, s * BLK : (s + 1) * BLK]
+                keep[at : at + C, :] = stay[:, s * BLK : (s + 1) * BLK]
 
 
 def pair_kernel(batch, keep, got, *outs):
@@ -338,7 +391,8 @@
 
 
 def near_kernel(
-    recv, cols, rows, a_mat, mix, hop_ref, hid, sig, ext_hub, gh_ref, mixed, two, gh_out, hop_hub
+    recv, cols, rows, a_mat, mix, hop_ref, hid, sig, ext_hub, ext, back_ref, cot,
+    mixed, two, gh_out, hop_hub,
 ):
     r = iota((BLK, NODE), 0)
     m = iota((BLK, NODE), 1)
@@ -354,27 +408,17 @@
         hop_hub[t] = nn(own_pick, hop).astype(BF)
         mixed[t] = sig[t + 1].astype(F32) + nn(hid[t], mix[0]) + nn(hop, mix[1])
         back = (nn(put_halo, block) + nn(put_hub_own, ext_hub[t])).astype(BF)
-        gh_out[t] = gh_ref[t] + nt(back, mix[2])
-
-
-def end_kernel(
-    recv, cols, rows, a_hub, mix, conv, hop_hub, mixed, two_ref, gh_ref, fac_f, fac_g, cot,
-    layer, sgrad,
-):
-    r = iota((BLK, NODE), 0)
-    m = iota((BLK, NODE), 1)
-    base = (r >> 1) * 8 + (r & 1) * 4
-    own_node = cols[0:BLK, 2:3]
-    column = iota((NODE, NODE), 1)
-    node = iota((NODE, NODE), 0)
-    hubs = recv[:, 0:C]
+        own = nt(cot[t], mix[0]) + nt(back_ref[t], mix[1]) + nt(ext[t, 0:NODE, :], mix[2])
+        gh_out[t] = own + nt(back, mix[2])
+
+
+def signal_kernel(
+    me, owners, recv, rows, mix, conv, gh_ref, fac_f, fac_g, cot, sgrad
+):
+    mine, target = own_hub_block(me, owners, rows, recv)
     for t in range(T1):
-        hub_pick = hot((m == base + t) & (own_node < 0))
-        rows_hub = (nn(hub_pick, hubs) + hop_hub[t].astype(F32)).astype(BF)
-        two = (two_ref[t] + nn(a_hub[...], rows_hub)).astype(BF)
-        layer[t] = (mixed[t] + nn(two, mix[2])).astype(BF)
-        put_hub = hot((rows[1:2, :] == node) & ((column & 3) == t))
-        gh = gh_ref[t] + nt(nn(put_hub, hubs).astype(BF), mix[2])
+        back = nn(put_step(target, t), mine).astype(BF)
+        gh = gh_ref[t] + nt(back, mix[2])
         gf = (gh * fac_f[t]).astype(BF)
         gg = (gh * fac_g[t]).astype(BF)
         early = nt(gf, conv[0, 0]) + nt(gg, conv[1, 0])
@@ -385,6 +429,24 @@
             sgrad[t] = (early + carried).astype(BF)
         carried = late
     sgrad[T1] = carried.astype(BF)
+
+
+def layer_kernel(recv, cols, a_hub, mix, hop_hub, mixed, two_ref, layer):
+    r = iota((BLK, NODE), 0)
+    m = iota((BLK, NODE), 1)
+    base = (r >> 1) * 8 + (r & 1) * 4
+    own_node = cols[0:BLK, 2:3]
+    hubs = recv[:, 0:C]
+    for t in range(T1):
+        hub_pick = hot((m == base + t) & (own_node < 0))
+        rows_hub = (nn(hub_pick, hubs) + hop_hub[t].astype(F32)).astype(BF)
+        two = (two_ref[t] + nn(a_hub[...], rows_hub)).astype(BF)
+        layer[t] = (mixed[t] + nn(two, mix[2])).astype(BF)
+
+
+def tie_kernel(chunk, kept, chunk_out, kept_out):
+    del kept, kept_out
+    chunk_out[...] = chunk[...]
 
 
 def scale_kernel(core, batch, *refs):
@@ -435,21 +497,23 @@
     edge4 = (HIST, BLK, C)
     half = (8 * C, BLK)
     chunk = (NODE, BLK)
-    a_mat, a_hub, at_mat, cols, rows, send1 = call(
+    cols, rows, send1 = call(
         start_kernel,
-        [((NODE, EXT), BF), ((NODE, BLK), BF), ((EXT, NODE), BF), ((NODE, BLK), I32),
-         ((8, NODE), I32), ((NODE, EXT), BF)],
+        [((NODE, BLK), I32), ((8, NODE), I32), ((NODE, EXT), BF)],
         (tile_row, tile_col, tile_mask, me, hub_owner, tile_vals, send_rows.T, send_mask.T,
          hub_rows, cot, sig),
         smem=5,
+        scratch=[pltpu.VMEM((8, BLK, BLK), F32), pltpu.VMEM((EXT - NODE, NODE), BF)],
+        flops=2 << 30,
+    )
+    recv1 = swap(send1.reshape(DOM, 8, EXT), "dom").reshape(NODE, EXT)
+    a_mat, a_hub, at_mat, hid, fac_f, fac_g, mix0 = call(
+        own_kernel,
+        [((NODE, EXT), BF), ((NODE, BLK), BF), ((EXT, NODE), BF), (field, BF), (field, F32),
+         (field, F32), ((C, C), F32)],
+        (tile_row, tile_col, tile_mask, tile_vals, conv, sig, cot),
+        smem=3,
         scratch=[pltpu.VMEM((24, BLK, BLK), F32)],
-        flops=2 << 30,
-    )
-    recv1 = swap(send1.reshape(DOM, 8, EXT), "dom").reshape(NODE, EXT)
-    hid, fac_f, fac_g, mix0 = call(
-        own_kernel,
-        [(field, BF), (field, F32), (field, F32), ((C, C), F32)],
-        (conv, sig, cot),
         flops=8 << 30,
     )
     (send2,) = call(
@@ -462,19 +526,29 @@
         (recv1, conv, cols, rows, at_mat, a_mat, hid, cot, sig),
         flops=8 << 30,
     )
-    send3, back, hop, ext, ext_hub, sig_u = call(
+    send3, back, hop, ext, ext_hub, sig_u = stepped(
         rows_kernel,
         [((NODE, EXT), BF), (field, BF), (field, BF), ((T1, EXT, C), BF), (edge, BF),
          (edge4, BF)],
-        (recv2, cols, rows, conv, hub_sig, a_hub, hop_part, back_part, at_mat),
+        (me, hub_owner, recv2, cols, rows, conv, hub_sig, hub_sig, a_hub, hop_part, back_part,
+         at_mat),
+        ("all", "all", "all", "all", "this", "next", "all", "this", "this", "all"),
+        ("lanes", "this", "this", "this", "this", "all"),
+        smem=2,
+        scratch=[pltpu.VMEM((NODE, NODE), BF), pltpu.VMEM((NODE, EXT - NODE), BF)],
         flops=4 << 30,
     )
     recv3 = swap(send3.reshape(DOM, 8, EXT), "dom").reshape(NODE, EXT)
-    keep, give, gh = call(
+    keep, give = stepped(
         weight_kernel,
-        [(half, F32), (half, F32), (field, F32)],
-        (core, conv, mix, hop, cot, back, ext, sig, sig_h, sig_u, fac_f, fac_g, mix0),
+        [(half, F32), (half, F32)],
+        (core, conv, mix, hop, cot, back, ext, sig, sig, sig_h, sig_h, sig_u, sig_u, fac_f, fac_g,
+         mix0),
+        ("all", "all", "this", "this", "this", "this", "this", "next", "this", "next", "this",
+         "next", "this", "this", "all"),
+        ("all", "all"),
         smem=1,
+        scratch=[pltpu.VMEM((6, C, C), F32)],
         flops=8 << 30,
     )
     pairs = [(i, i ^ 1) for i in range(DOM)]
@@ -498,23 +572,38 @@
     mixed, two, gh, hop_hub = call(
         near_kernel,
         [(field, F32), (field, F32), (field, F32), (edge, BF)],
-        (recv3, cols, rows, a_mat, mix, hop, hid, sig, ext_hub, gh),
+        (recv3, cols, rows, a_mat, mix, hop, hid, sig, ext_hub, ext, back, cot),
         flops=8 << 30,
     )
     recv4, mixed, two, gh, hop_hub = lax.optimization_barrier((recv4, mixed, two, gh, hop_hub))
     (send5,) = call(spread_kernel, [((DOM, 8, BLK), BF)], (recv4,), 6, flops=1 << 26)
     recv5 = swap(send5, "dom").reshape(chunk)
-    layer, sgrad = call(
-        end_kernel,
-        [(field, BF), ((HIST, NODE, C), BF)],
-        (recv4.reshape(NODE, C + BLK), cols, rows, a_hub, mix, conv, hop_hub, mixed, two, gh,
-         fac_f, fac_g, cot),
-        flops=12 << 30,
-    )
-    layer = jnp.transpose(layer, (1, 0, 2))[:, None]
-    sgrad = jnp.transpose(sgrad, (1, 0, 2))[:, None]
-    recv5, layer, sgrad = lax.optimization_barrier((recv5, layer, sgrad))
+    recv4 = recv4.reshape(NODE, C + BLK)
+    (sgrad,) = call(
+        signal_kernel,
+        [((HIST, NODE, C), BF)],
+        (me, hub_owner, recv4, rows, mix, conv, gh, fac_f, fac_g, cot),
+        smem=2,
+        flops=8 << 30,
+    )
+    sgrad = jnp.transpose(sgrad, (1, 0, 2))
+    vmem, keep_place = (pl.BlockSpec(memory_space=m) for m in (pltpu.VMEM, pl.ANY))
+    recv5, sgrad = pl.pallas_call(
+        tie_kernel,
+        out_shape=[jax.ShapeDtypeStruct(x.shape, x.dtype) for x in (recv5, sgrad)],
+        in_specs=[vmem, keep_place],
+        out_specs=[vmem, keep_place],
+        input_output_aliases={1: 1},
+        compiler_params=pltpu.CompilerParams(vmem_limit_bytes=4 << 20),
+    )(recv5, sgrad)
     mine = [recv5] + [lax.ppermute(recv5, "batch", rounds[k]) for k in range(1, BATCH)]
+    (layer,) = call(
+        layer_kernel,
+        [(field, BF)],
+        (recv4, cols, a_hub, mix, hop_hub, mixed, two),
+        flops=4 << 30,
+    )
+    mine, layer = lax.optimization_barrier((mine, layer))
     other = [lax.ppermute(one, "dom", pairs) for one in mine]
     conv_grad, mix_grad = call(
         scale_kernel,
@@ -524,7 +613,8 @@
         smem=2,
         flops=1 << 20,
     )
-    return layer, sgrad, conv_grad.reshape(2, 2, C, C), mix_grad
+    layer = jnp.transpose(layer, (1, 0, 2))[:, None]
+    return layer, sgrad[:, None], conv_grad.reshape(2, 2, C, C), mix_grad
 
 
 def solution(mesh):

time: 164 us -> 162 us (0.988)
  waiting for transfers between devices: 43.2 us -> 41.2 us
  starting transfers between devices: 54.7 us -> 52.8 us
  Pallas kernels: 57.1 us -> 58.9 us
    pallas_call x0 -> x3, Pallas kernels: none -> 16.5 us  [the longest x2 16.5 us: stepped(): pl.pallas_call(kernel, grid=(T1,), out_shape=[jax.ShapeDtypeStruct(s, d)...]
    pallas_call x12 -> x11, Pallas kernels: 57.1 us -> 42.4 us  [call(): pl.pallas_call(kernel, out_shape=[jax.ShapeDtypeStruct(s, d) for s, d in...]
    pallas_call x0 -> x1, local copies, waits for them, and re-layouts: none -> 3 us  [call(): pl.pallas_call(kernel, out_shape=[jax.ShapeDtypeStruct(s, d) for s, d in...]
    unnamed x14 -> x15, local copies, waits for them, and re-layouts: 7.28 us -> 4.29 us
    ppermute x4, starting transfers between devices: 4.12 us -> 1.84 us  [body(): other = [lax.ppermute(one, 'dom', pairs) for one in mine]]
    ppermute x3, waiting for transfers between devices: 1.93 us -> 0.26 us  [body(): lax.ppermute(recv5, 'batch', rounds[k])]
  transfers between devices with their start and end apart: 16 -> 16, of which waited for: 9 -> 12; matrix products, arithmetic and copies ran while one was open for 2% -> 2% of each run, Pallas kernels for 23% -> 25%
where the time goes in v3:
time: 162 us; the launch traced here: 161 us
  Pallas kernels  58.9 us (36%)
  starting transfers between devices  52.8 us (33%)
  waiting for transfers between devices  41.2 us (25%)
  local copies, waits for them, and re-layouts  7.29 us (4%)
    pallas_call x11, Pallas kernels, call(): pl.pallas_call(kernel, out_shape=[jax.ShapeDtypeStruct(s, d) for s, d in...  42.4 us
    all_to_all x5, starting transfers between devices, swap(): return lax.all_to_all(x, axis, split_axis=0, concat_axis=0, tiled=True)  40.6 us
    all_to_all x5, waiting for transfers between devices, swap(): return lax.all_to_all(x, axis, split_axis=0, concat_axis=0, tiled=True)  32.2 us
    pallas_call x2, Pallas kernels, stepped(): pl.pallas_call(kernel, grid=(T1,), out_shape=[jax.ShapeDtypeStruct(s, d)...  16.5 us
    ppermute x3, waiting for transfers between devices, body(): lax.ppermute(parts[k], 'batch', rounds[k])  4.9 us
    ppermute x3, starting transfers between devices, body(): lax.ppermute(parts[k], 'batch', rounds[k])  4.89 us
    ppermute x3, starting transfers between devices, body(): lax.ppermute(recv5, 'batch', rounds[k])  4.75 us
    unnamed x15, local copies, waits for them, and re-layouts  4.29 us
  transfers between devices with their start and end apart: 16, of which 12 were waited for; matrix products, arithmetic and copies ran while one was open for 2% of the time, Pallas kernels for 25%

profile of v3, /device:TPU:1, one launch (start us, length us, event | category | flops | bytes accessed | tf_op | source)
XLA Modules:
  0.0 160.9 jit_solution(3362158617143901085)
XLA Ops:
  0.6 2.3 %copy.23 = bf16[512,1,4,256]{3,0,2,1:T(8,128)(2,1)} copy(bf16[512,1,4,256]{3,2,1,0:T(4,128)(2,1)} %param.12) | data formatting | bytes 2097152 | tf_op args[0]
  3.0 5.3 %shard_map.147 = (s32[512,128]{1,0:T(8,128)}, s32[8,512]{1,0:T(8,128)}, bf16[512,768]{1,0:T(8,128)(2,1)}) custom-call(s32[16]{0:T(128)} %trow.3, s32[16]{0:T(128)} %tcol.3, s32[16]{0:T(128)} %tmask.3, s32[1]{0:T(128)} %bitcast.me, s32[8]{0:T(128)} %owners.9, bf16[16,128,128]{2,1,0:T(8,128)(2,1)} %tiles.3, s32[2,64]{1,0:T(2,128)} %bitcast.55, ...), custom_call_target="tpu_custom_call" | custom-call | flops 2147483648 | bytes 8388608 | tf_op jit(solution)/shard_map/pallas_call | solution.py:64
  8.3 13.2 %all-to-all-start = ((bf16[64,8,768]{2,1,0:T(8,128)(2,1)}), bf16[64,8,768]{2,1,0:T(8,128)(2,1)S(1)}, u32[]{:S(2)}, u32[]{:S(2)}) async-start(bf16[64,8,768]{2,1,0:T(8,128)(2,1)} %bitcast.46), calls=%async_computation | async-start | bytes 1572864 | tf_op jit(solution)/shard_map/all_to_all | solution.py:471
  21.4 0.0 copy-start.4
  21.4 6.4 %shard_map.149 = (bf16[512,768]{1,0:T(8,128)(2,1)}, bf16[512,128]{1,0:T(8,128)(2,1)}, bf16[768,512]{1,0:T(8,128)(2,1)}, bf16[3,512,256]{2,1,0:T(8,128)(2,1)}, f3...) custom-call(s32[16]{0:T(128)} %trow.3, s32[16]{0:T(128)} %tcol.3, s32[16]{0:T(128)} %tmask.3, ...), custom_call_target="tpu_custom_call" | custom-call | flops 8589934592 | bytes 8388608 | tf_op jit(solution)/shard_map/pallas_call | solution.py:64
  27.9 16.3 %all-to-all-done = bf16[64,8,768]{2,1,0:T(8,128)(2,1)S(1)} async-done(((bf16[64,8,768]{2,1,0:T(8,128)(2,1)}), bf16[64,8,768]{2,1,0:T(8,128)(2,1)S(1)}, u32[]{:S(2)}, u32[]{:S(2)}) %all-to-all-start) | async-done | bytes 786464 | tf_op jit(solution)/shard_map/all_to_all | solution.py:471
  44.2 0.0 copy-start.1
  44.2 0.0 copy-done.4
  44.2 1.6 %shard_map.148 = bf16[64,8,256]{2,1,0:T(8,128)(2,1)} custom-call(s32[1]{0:T(128)} %bitcast.me, s32[8]{0:T(128)S(1)} %copy-done.4, bf16[512,768]{1,0:T(8,128)(2,1)S(1)} %bitcast.32), custom_call_target="tpu_custom_call" | custom-call | flops 268435456 | bytes 8388608 | tf_op jit(solution)/shard_map/pallas_call | solution.py:64
  45.8 6.2 %all-to-all-start.1 = ((bf16[64,8,256]{2,1,0:T(8,128)(2,1)}), bf16[64,8,256]{2,1,0:T(8,128)(2,1)S(1)}, u32[]{:S(2)}, u32[]{:S(2)}) async-start(bf16[64,8,256]{2,1,0:T(8,128)(2,1)} %shard_map.148), calls=%async_computation.1 | async-start | bytes 524288 | tf_op jit(solution)/shard_map/all_to_all | solution.py:471
  52.1 0.0 copy-done.1
  52.1 6.7 %shard_map.150 = (f32[3,512,256]{2,1,0:T(8,128)}, f32[3,512,256]{2,1,0:T(8,128)}, bf16[4,128,256]{2,1,0:T(8,128)(2,1)}, bf16[4,128,256]{2,1,0:T(8,128)(2,1)}) custom-call(bf16[512,768]{1,0:T(8,128)(2,1)} %bitcast.33, bf16[2,2,256,256]{3,2,1,0:T(8,128)(2,1)} %conv.9, s32[512,128]{1,0:T(8,128)} %get-tuple-element.49.cols, s32[8,512]{1,0:T(8,128)} %get-tuple-element.50.rows, ...), custom_call_target="tpu_custom_call" | custom-call | flops 8589934592 | bytes 8388608 | tf_op jit(solution)/shard_map/pallas_call | solution.py:64
  58.8 6.5 %all-to-all-done.1 = bf16[64,8,256]{2,1,0:T(8,128)(2,1)S(1)} async-done(((bf16[64,8,256]{2,1,0:T(8,128)(2,1)}), bf16[64,8,256]{2,1,0:T(8,128)(2,1)S(1)}, u32[]{:S(2)}, u32[]{:S(2)}) %all-to-all-start.1) | async-done | bytes 262176 | tf_op jit(solution)/shard_map/all_to_all | solution.py:471
  65.2 0.0 copy-start.6
  65.2 0.7 copy-done.6
  65.9 8.0 %shard_map.151 = (bf16[512,768]{1,0:T(8,128)(2,1)}, bf16[3,512,256]{2,1,0:T(8,128)(2,1)}, bf16[3,512,256]{2,1,0:T(8,128)(2,1)}, bf16[3,768,256]{2,1,0:T(8,128)(2...) custom-call(s32[1]{0:T(128)} %bitcast.me, s32[8]{0:T(128)} %owners.9, bf16[512,256]{1,0:T(8,128)(2,1)} %bitcast.47, ...), custom_call_target="tpu_custom_call" | custom-call | flops 4294967296 | bytes 8388608 | tf_op jit(solution)/shard_map/pallas_call | solution.py:84
  73.9 4.7 %all-to-all-start.2 = ((bf16[64,8,768]{2,1,0:T(8,128)(2,1)}), bf16[64,8,768]{2,1,0:T(8,128)(2,1)S(1)}, u32[]{:S(2)}, u32[]{:S(2)}) async-start(bf16[64,8,768]{2,1,0:T(8,128)(2,1)} %bitcast.45), calls=%async_computation.2 | async-start | bytes 1572864 | tf_op jit(solution)/shard_map/all_to_all | solution.py:471
  78.6 8.5 %shard_map.152 = (f32[2048,128]{1,0:T(8,128)}, f32[2048,128]{1,0:T(8,128)}) custom-call(s32[1]{0:T(128)} %bitcast.15.core, bf16[2,2,256,256]{3,2,1,0:T(8,128)(2,1)} %conv.9, bf16[3,256,256]{2,1,0:T(8,128)(2,1)} %mix.7, bf16[3,512,256]{2,1,0:T(8,128)(2,1)} %get-tuple-element.59.hop.hop_ref, bf16[3,512,256]{2,1,0:T(8,128)(2,1)} %bitcast.52, ...), custom_call_target="tpu_custom_call" | custom-call | flops 8589934592 | bytes 8388608 | tf_op jit(solution)/shard_map/pallas_call | solution.py:84
  87.1 0.0 copy-start.5
  87.2 0.7 collective-permute-start
  87.9 2.5 %collective-permute-done.got = f32[2048,128]{1,0:T(8,128)S(1)} collective-permute-done((f32[2048,128]{1,0:T(8,128)}, f32[2048,128]{1,0:T(8,128)S(1)}, u32[]{:S(2)}, u32[]{:S(2)}) %collective-permute-start) | collective-permute-done | bytes 1048608 | tf_op jit(solution)/shard_map/ppermute | solution.py:556
  90.4 0.0 copy-start.3
  90.4 1.2 copy-done.3
  91.6 0.2 shard_map.153
  91.8 1.3 collective-permute-start.1
  93.1 2.4 %collective-permute-start.2 = (bf16[512,128]{1,0:T(8,128)(2,1)S(1)}, bf16[512,128]{1,0:T(8,128)(2,1)S(1)}, u32[]{:S(2)}, u32[]{:S(2)}) collective-permute-start(bf16[512,128]{1,0:T(8,128)(2,1)S(1)} %get-tuple-element.71), channel_id=1, source_target_pairs={{0,2},{1,3},{2,0},{3,1},{4,6},{5,7},{6,4},{7,5},{8,10},{9,11},{10,... | collective-permute-start | bytes 393224 | tf_op jit(solution)/shard_map/ppermute | solution.py:561
  95.5 1.2 collective-permute-start.3
  96.7 1.1 collective-permute-done.1.part1
  97.8 3.8 %collective-permute-done.2.part2 = bf16[512,128]{1,0:T(8,128)(2,1)S(1)} collective-permute-done((bf16[512,128]{1,0:T(8,128)(2,1)S(1)}, bf16[512,128]{1,0:T(8,128)(2,1)S(1)}, u32[]{:S(2)}, u32[]{:S(2)}) %collective-permute-start.2) | collective-permute-done | bytes 131104 | tf_op jit(solution)/shard_map/ppermute | solution.py:561
  101.6 0.0 collective-permute-done.3.part3
  101.6 0.0 all-to-all-done.2
  101.6 0.0 copy-start
  101.6 0.0 copy-done.5
  101.6 1.7 %shard_map.154 = bf16[64,8,384]{2,1,0:T(8,128)(2,1)} custom-call(s32[1]{0:T(128)} %bitcast.me, s32[8]{0:T(128)S(1)} %copy-done.5, bf16[512,768]{1,0:T(8,128)(2,1)S(1)} %bitcast.30, bf16[512,128]{1,0:T(8,128)(2,1)S(1)} %get-tuple-element.69.part0, bf16[512,128]{1,0:T(8,128)(2,1)S(1)} %collective-permute-done.1.part1, ...), custom_call_target="tpu_custom_call" | custom-call | flops 268435456 | bytes 8388608 | tf_op jit(solution)/shard_map/pallas_call | solution.py:64
  103.3 10.9 %all-to-all-start.3 = ((bf16[64,8,384]{2,1,0:T(8,128)(2,1)}), bf16[64,8,384]{2,1,0:T(8,128)(2,1)S(1)}, u32[]{:S(2)}, u32[]{:S(2)}) async-start(bf16[64,8,384]{2,1,0:T(8,128)(2,1)} %shard_map.154), calls=%async_computation.3 | async-start | bytes 786432 | tf_op jit(solution)/shard_map/all_to_all | solution.py:471
  114.2 0.0 copy-done
  114.2 8.1 %shard_map.155 = (f32[3,512,256]{2,1,0:T(8,128)}, f32[3,512,256]{2,1,0:T(8,128)}, f32[3,512,256]{2,1,0:T(8,128)}, bf16[3,128,256]{2,1,0:T(8,128)(2,1)}) custom-call(bf16[512,768]{1,0:T(8,128)(2,1)} %bitcast.31, s32[512,128]{1,0:T(8,128)} %get-tuple-element.49.cols, s32[8,512]{1,0:T(8,128)} %get-tuple-element.50.rows, ...), custom_call_target="tpu_custom_call" | custom-call | flops 8589934592 | bytes 8388608 | tf_op jit(solution)/shard_map/pallas_call | solution.py:64
  122.3 7.0 %all-to-all-done.3.recv = bf16[64,8,384]{2,1,0:T(8,128)(2,1)S(1)} async-done(((bf16[64,8,384]{2,1,0:T(8,128)(2,1)}), bf16[64,8,384]{2,1,0:T(8,128)(2,1)S(1)}, u32[]{:S(2)}, u32[]{:S(2)}) %all-to-all-start.3) | async-done | bytes 393248 | tf_op jit(solution)/shard_map/all_to_all | solution.py:471
  129.2 0.0 copy-start.2
  129.2 0.8 shard_map.156
  130.0 5.6 %all-to-all-start.4 = ((bf16[64,8,128]{2,1,0:T(8,128)(2,1)}), bf16[64,8,128]{2,1,0:T(8,128)(2,1)S(1)}, u32[]{:S(2)}, u32[]{:S(2)}) async-start(bf16[64,8,128]{2,1,0:T(8,128)(2,1)} %shard_map.156), calls=%async_computation.4 | async-start | bytes 262144 | tf_op jit(solution)/shard_map/all_to_all | solution.py:471
  135.6 0.0 copy-done.2
  135.6 5.7 %shard_map.157 = bf16[4,512,256]{2,1,0:T(8,128)(2,1)} custom-call(s32[1]{0:T(128)} %bitcast.me, s32[8]{0:T(128)} %owners.9, bf16[512,384]{1,0:T(8,128)(2,1)} %bitcast.34, s32[8,512]{1,0:T(8,128)} %get-tuple-element.50.rows, bf16[3,256,256]{2,1,0:T(8,128)(2,1)} %mix.7, bf16[2,2,256,256]{3,2,1,0:T(8,128)(2,1)} %conv.9, ...), custom_call_target="tpu_custom_call" | custom-call | flops 8589934592 | bytes 8388608 | tf_op jit(solution)/shard_map/pallas_call | solution.py:64
  141.3 3.0 %copy.22 = bf16[4,512,256]{2,0,1:T(4,128)(2,1)} copy(bf16[4,512,256]{2,1,0:T(8,128)(2,1)} %shard_map.157) | data formatting | bytes 2097152 | tf_op jit(solution)/shard_map/pallas_call | solution.py:64
  144.3 2.4 %all-to-all-done.4 = bf16[64,8,128]{2,1,0:T(8,128)(2,1)S(1)} async-done(((bf16[64,8,128]{2,1,0:T(8,128)(2,1)}), bf16[64,8,128]{2,1,0:T(8,128)(2,1)S(1)}, u32[]{:S(2)}, u32[]{:S(2)}) %all-to-all-start.4) | async-done | bytes 131104 | tf_op jit(solution)/shard_map/all_to_all | solution.py:471
  146.7 1.3 collective-permute-start.4
  148.1 2.1 %collective-permute-start.5 = (bf16[512,128]{1,0:T(8,128)(2,1)S(1)}, bf16[512,128]{1,0:T(8,128)(2,1)S(1)}, u32[]{:S(2)}, u32[]{:S(2)}) collective-permute-start(bf16[512,128]{1,0:T(8,128)(2,1)S(1)} %get-tuple-element.86.refs_0_), channel_id=1, source_target_pairs={{0,2},{1,3},{2,0},{3,1},{4,6},{5,7},{6,4},{7,5},{8,10},{9,11},{10,... | collective-permute-start | bytes 393224 | tf_op jit(solution)/shard_map/ppermute | solution.py:599
  150.2 1.3 collective-permute-start.6
  151.5 4.5 %shard_map.159 = bf16[3,512,256]{2,1,0:T(8,128)(2,1)} custom-call(bf16[512,384]{1,0:T(8,128)(2,1)} %bitcast.35, s32[512,128]{1,0:T(8,128)} %get-tuple-element.49.cols, bf16[512,128]{1,0:T(8,128)(2,1)} %get-tuple-element.55.a_hub, bf16[3,256,256]{2,1,0:T(8,128)(2,1)} %mix.7, bf16[3,128,256]{2,1,0:T(8,128)(2,1)} %get-tuple-element.81.hop_hub, ...), custom_call_target="tpu_custom_call" | custom-call | flops 4294967296 | bytes 8388608 | tf_op jit(solution)/shard_map/pallas_call | solution.py:64
  156.0 0.0 collective-permute-done.4.refs_1_
  156.0 0.3 collective-permute-done.5.refs_2_
  156.2 0.0 collective-permute-done.6.refs_3_
  156.2 1.3 collective-permute-start.7
  157.5 0.0 collective-permute-start.8
  157.5 0.5 collective-permute-start.9
  158.0 0.0 collective-permute-start.10
  158.1 0.5 collective-permute-done.7.refs_4_
  158.5 0.4 collective-permute-done.8.refs_5_
  158.9 0.2 collective-permute-done.9.refs_6_
  159.1 0.3 collective-permute-done.10.refs_7_
  159.4 1.5 shard_map.160
  (1 shorter events, 0.0 us)
Async XLA Ops:
  8.3 35.9 %all-to-all-start = ((bf16[64,8,768]{2,1,0:T(8,128)(2,1)}), bf16[64,8,768]{2,1,0:T(8,128)(2,1)S(1)}, u32[]{:S(2)}, u32[]{:S(2)}) async-start(bf16[64,8,768]{2,1,0:T(8,128)(2,1)} %bitcast.46), calls=%async_computation | async-start | bytes 1572864 | tf_op jit(solution)/shard_map/all_to_all | solution.py:471
  21.4 22.8 %copy-start.4 = (s32[8]{0:T(128)S(1)}, s32[8]{0:T(128)}, u32[]{:S(2)}) copy-start(s32[8]{0:T(128)} %owners.9) | copy-start | bytes 100
  44.2 7.9 %copy-start.1 = (bf16[64,8,768]{2,1,0:T(8,128)(2,1)}, bf16[64,8,768]{2,1,0:T(8,128)(2,1)S(1)}, u32[]{:S(2)}) copy-start(bf16[64,8,768]{2,1,0:T(8,128)(2,1)S(1)} %all-to-all-done) | copy-start | bytes 2359300
  45.8 19.4 %all-to-all-start.1 = ((bf16[64,8,256]{2,1,0:T(8,128)(2,1)}), bf16[64,8,256]{2,1,0:T(8,128)(2,1)S(1)}, u32[]{:S(2)}, u32[]{:S(2)}) async-start(bf16[64,8,256]{2,1,0:T(8,128)(2,1)} %shard_map.148), calls=%async_computation.1 | async-start | bytes 524288 | tf_op jit(solution)/shard_map/all_to_all | solution.py:471
  65.2 0.7 copy-start.6
  73.9 27.7 %all-to-all-start.2 = ((bf16[64,8,768]{2,1,0:T(8,128)(2,1)}), bf16[64,8,768]{2,1,0:T(8,128)(2,1)S(1)}, u32[]{:S(2)}, u32[]{:S(2)}) async-start(bf16[64,8,768]{2,1,0:T(8,128)(2,1)} %bitcast.45), calls=%async_computation.2 | async-start | bytes 1572864 | tf_op jit(solution)/shard_map/all_to_all | solution.py:471
  87.1 14.4 %copy-start.5 = (s32[8]{0:T(128)S(1)}, s32[8]{0:T(128)}, u32[]{:S(2)}) copy-start(s32[8]{0:T(128)} %owners.9) | copy-start | bytes 100
  87.2 3.2 %collective-permute-start = (f32[2048,128]{1,0:T(8,128)}, f32[2048,128]{1,0:T(8,128)S(1)}, u32[]{:S(2)}, u32[]{:S(2)}) collective-permute-start(f32[2048,128]{1,0:T(8,128)} %get-tuple-element.68), channel_id=1, source_target_pairs={{0,4},{4,0},{8,12},{12,8},{16,20},{20,16},{24,28},{28,24},{32,36},... | collective-permute-start | bytes 3145736 | tf_op jit(solution)/shard_map/ppermute | solution.py:556
  90.4 1.2 copy-start.3
  91.8 6.0 %collective-permute-start.1 = (bf16[512,128]{1,0:T(8,128)(2,1)S(1)}, bf16[512,128]{1,0:T(8,128)(2,1)S(1)}, u32[]{:S(2)}, u32[]{:S(2)}) collective-permute-start(bf16[512,128]{1,0:T(8,128)(2,1)S(1)} %get-tuple-element.70), channel_id=1, source_target_pairs={{0,1},{1,2},{2,3},{3,0},{4,5},{5,6},{6,7},{7,4},{8,9},{9,10},{10,1... | collective-permute-start | bytes 393224 | tf_op jit(solution)/shard_map/ppermute | solution.py:561
  93.1 8.5 %collective-permute-start.2 = (bf16[512,128]{1,0:T(8,128)(2,1)S(1)}, bf16[512,128]{1,0:T(8,128)(2,1)S(1)}, u32[]{:S(2)}, u32[]{:S(2)}) collective-permute-start(bf16[512,128]{1,0:T(8,128)(2,1)S(1)} %get-tuple-element.71), channel_id=1, source_target_pairs={{0,2},{1,3},{2,0},{3,1},{4,6},{5,7},{6,4},{7,5},{8,10},{9,11},{10,... | collective-permute-start | bytes 393224 | tf_op jit(solution)/shard_map/ppermute | solution.py:561
  95.5 6.1 %collective-permute-start.3 = (bf16[512,128]{1,0:T(8,128)(2,1)S(1)}, bf16[512,128]{1,0:T(8,128)(2,1)S(1)}, u32[]{:S(2)}, u32[]{:S(2)}) collective-permute-start(bf16[512,128]{1,0:T(8,128)(2,1)S(1)} %get-tuple-element.72), channel_id=1, source_target_pairs={{0,3},{1,0},{2,1},{3,2},{4,7},{5,4},{6,5},{7,6},{8,11},{9,8},{10,9... | collective-permute-start | bytes 393224 | tf_op jit(solution)/shard_map/ppermute | solution.py:561
  101.6 12.6 %copy-start = (bf16[64,8,768]{2,1,0:T(8,128)(2,1)}, bf16[64,8,768]{2,1,0:T(8,128)(2,1)S(1)}, u32[]{:S(2)}) copy-start(bf16[64,8,768]{2,1,0:T(8,128)(2,1)S(1)} %all-to-all-done.2) | copy-start | bytes 2359300
  103.3 26.0 %all-to-all-start.3 = ((bf16[64,8,384]{2,1,0:T(8,128)(2,1)}), bf16[64,8,384]{2,1,0:T(8,128)(2,1)S(1)}, u32[]{:S(2)}, u32[]{:S(2)}) async-start(bf16[64,8,384]{2,1,0:T(8,128)(2,1)} %shard_map.154), calls=%async_computation.3 | async-start | bytes 786432 | tf_op jit(solution)/shard_map/all_to_all | solution.py:471
  129.2 6.4 %copy-start.2 = (bf16[64,8,384]{2,1,0:T(8,128)(2,1)}, bf16[64,8,384]{2,1,0:T(8,128)(2,1)S(1)}, u32[]{:S(2)}) copy-start(bf16[64,8,384]{2,1,0:T(8,128)(2,1)S(1)} %all-to-all-done.3.recv) | copy-start | bytes 1179652
  130.0 16.7 %all-to-all-start.4 = ((bf16[64,8,128]{2,1,0:T(8,128)(2,1)}), bf16[64,8,128]{2,1,0:T(8,128)(2,1)S(1)}, u32[]{:S(2)}, u32[]{:S(2)}) async-start(bf16[64,8,128]{2,1,0:T(8,128)(2,1)} %shard_map.156), calls=%async_computation.4 | async-start | bytes 262144 | tf_op jit(solution)/shard_map/all_to_all | solution.py:471
  146.7 9.2 %collective-permute-start.4 = (bf16[512,128]{1,0:T(8,128)(2,1)S(1)}, bf16[512,128]{1,0:T(8,128)(2,1)S(1)}, u32[]{:S(2)}, u32[]{:S(2)}) collective-permute-start(bf16[512,128]{1,0:T(8,128)(2,1)S(1)} %get-tuple-element.86.refs_0_), channel_id=1, source_target_pairs={{0,1},{1,2},{2,3},{3,0},{4,5},{5,6},{6,7},{7,4},{8,9},{9,10},{10,1... | collective-permute-start | bytes 393224 | tf_op jit(solution)/shard_map/ppermute | solution.py:599
  148.1 8.1 %collective-permute-start.5 = (bf16[512,128]{1,0:T(8,128)(2,1)S(1)}, bf16[512,128]{1,0:T(8,128)(2,1)S(1)}, u32[]{:S(2)}, u32[]{:S(2)}) collective-permute-start(bf16[512,128]{1,0:T(8,128)(2,1)S(1)} %get-tuple-element.86.refs_0_), channel_id=1, source_target_pairs={{0,2},{1,3},{2,0},{3,1},{4,6},{5,7},{6,4},{7,5},{8,10},{9,11},{10,... | collective-permute-start | bytes 393224 | tf_op jit(solution)/shard_map/ppermute | solution.py:599
  150.2 6.0 %collective-permute-start.6 = (bf16[512,128]{1,0:T(8,128)(2,1)S(1)}, bf16[512,128]{1,0:T(8,128)(2,1)S(1)}, u32[]{:S(2)}, u32[]{:S(2)}) collective-permute-start(bf16[512,128]{1,0:T(8,128)(2,1)S(1)} %get-tuple-element.86.refs_0_), channel_id=1, source_target_pairs={{0,3},{1,0},{2,1},{3,2},{4,7},{5,4},{6,5},{7,6},{8,11},{9,8},{10,9... | collective-permute-start | bytes 393224 | tf_op jit(solution)/shard_map/ppermute | solution.py:599
  156.2 2.3 %collective-permute-start.7 = (bf16[512,128]{1,0:T(8,128)(2,1)S(1)}, bf16[512,128]{1,0:T(8,128)(2,1)S(1)}, u32[]{:S(2)}, u32[]{:S(2)}) collective-permute-start(bf16[512,128]{1,0:T(8,128)(2,1)S(1)} %get-tuple-element.86.refs_0_), channel_id=1, source_target_pairs={{0,4},{4,0},{8,12},{12,8},{16,20},{20,16},{24,28},{28,24},{32,36},... | collective-permute-start | bytes 393224 | tf_op jit(solution)/shard_map/ppermute | solution.py:607
  157.5 1.3 collective-permute-start.8
  157.5 1.5 collective-permute-start.9
  158.0 1.3 collective-permute-start.10

commit v4 on v3

--- a/solution.py
+++ b/solution.py
@@ -21,6 +21,8 @@
 OWNERS = 8
 HUB_PER = 16
 TILES = 16
+PIECES = 7
+CHUNK = 448
 
 
 def nn(a, b):
@@ -352,22 +354,23 @@
     @pl.when(t == T1 - 1)
     def _():
         first = core[0] == 0
-        for k in range(4):
-            low = acc[k]
-            high = (mix0[...], acc[4], acc[5], jnp.zeros((C, C), F32))[k]
-            stay = jnp.where(first, low, high)
-            away = jnp.where(first, high, low)
-            for s in range(2):
-                at = (2 * k + s) * C
-                give[at : at + C, :] = away[:, s * BLK : (s + 1) * BLK]
-                keep[at : at + C, :] = stay[:, s * BLK : (s + 1) * BLK]
+        mats = (acc[0], acc[1], acc[2], acc[3], mix0[...], acc[4], acc[5])
+        pieces = [x[:, s * BLK : (s + 1) * BLK] for x in mats for s in range(2)]
+        for j in range(PIECES):
+            low, high = pieces[j], pieces[PIECES + j]
+            give[j * C : (j + 1) * C, :] = jnp.where(first, high, low)
+            keep[j * C : (j + 1) * C, :] = jnp.where(first, low, high)
 
 
 def pair_kernel(batch, keep, got, *outs):
     mine, other = keep, got
     for k in range(BATCH):
-        at = pl.ds(pl.multiple_of(((batch[0] + k) & (BATCH - 1)) * NODE, NODE), NODE)
+        at = pl.ds(pl.multiple_of(((batch[0] + k) & (BATCH - 1)) * CHUNK, DOM), CHUNK)
         outs[k][...] = (mine[at, :] + other[at, :]).astype(BF)
+
+
+def same_slot(n, m):
+    return (n == (m >> 3) * PIECES + (m & 7)) & ((m & 7) < PIECES)
 
 
 def second_hub_kernel(me, owners, recv, part0, part1, part2, part3, send):
@@ -377,7 +380,8 @@
     total += part2[...].astype(F32) + part3[...].astype(F32)
     at_owner = iota((DOM, 8, C), 0) == owner
     send[:, :, 0:C] = jnp.where(at_owner, backward[None], forward[None]).astype(BF)
-    send[:, :, C:] = total.astype(BF).reshape(DOM, 8, BLK)
+    place = hot(same_slot(iota((NODE, CHUNK), 1), iota((NODE, CHUNK), 0)))
+    send[:, :, C:] = nn(place, total.astype(BF)).astype(BF).reshape(DOM, 8, BLK)
 
 
 def spread_kernel(recv, send):
@@ -446,25 +450,28 @@
 
 def tie_kernel(chunk, kept, chunk_out, kept_out):
     del kept, kept_out
-    chunk_out[...] = chunk[...]
+    pack = hot(same_slot(iota((CHUNK, NODE), 0), iota((CHUNK, NODE), 1)))
+    chunk_out[...] = nn(pack, chunk[...]).astype(BF)
 
 
 def scale_kernel(core, batch, *refs):
     mine, other = refs[0:BATCH], refs[BATCH : 2 * BATCH]
-    conv_grad, mix_grad = refs[2 * BATCH :]
+    conv_grad, mix_grad, held = refs[2 * BATCH :]
     factor = 1.0 / math.sqrt(NODE * DOM * BATCH * T1)
     first = core[0] == 0
     for k in range(BATCH):
         block = (batch[0] + BATCH - k) & (BATCH - 1)
-        for s in range(2):
-            one = mine[k][s * C : (s + 1) * C, :].astype(F32) * factor
-            two = other[k][s * C : (s + 1) * C, :].astype(F32) * factor
-            lanes = slice(s * BLK, (s + 1) * BLK)
-            conv_grad[block, :, lanes] = jnp.where(first, one, two)
-
-            @pl.when(block < 3)
-            def _():
-                mix_grad[block, :, lanes] = jnp.where(first, two, one)
+        at = pl.ds(pl.multiple_of(block * CHUNK, DOM), CHUNK)
+        held[0, at, :] = jnp.where(first, mine[k][...], other[k][...])
+        held[1, at, :] = jnp.where(first, other[k][...], mine[k][...])
+    for p in range(2 * PIECES):
+        j = p % PIECES
+        piece = held[p // PIECES, j * C : (j + 1) * C, :].astype(F32) * factor
+        lanes = slice((p % 2) * BLK, (p % 2 + 1) * BLK)
+        if p < 8:
+            conv_grad[p // 2, :, lanes] = piece
+        else:
+            mix_grad[p // 2 - 4, :, lanes] = piece
 
 
 def swap(x, axis):
@@ -495,8 +502,8 @@
     field = (T1, NODE, C)
     edge = (T1, BLK, C)
     edge4 = (HIST, BLK, C)
-    half = (8 * C, BLK)
-    chunk = (NODE, BLK)
+    half = (PIECES * C, BLK)
+    chunk = (CHUNK, BLK)
     cols, rows, send1 = call(
         start_kernel,
         [((NODE, BLK), I32), ((8, NODE), I32), ((NODE, EXT), BF)],
@@ -577,7 +584,7 @@
     )
     recv4, mixed, two, gh, hop_hub = lax.optimization_barrier((recv4, mixed, two, gh, hop_hub))
     (send5,) = call(spread_kernel, [((DOM, 8, BLK), BF)], (recv4,), 6, flops=1 << 26)
-    recv5 = swap(send5, "dom").reshape(chunk)
+    recv5 = swap(send5, "dom").reshape(NODE, BLK)
     recv4 = recv4.reshape(NODE, C + BLK)
     (sgrad,) = call(
         signal_kernel,
@@ -590,7 +597,7 @@
     vmem, keep_place = (pl.BlockSpec(memory_space=m) for m in (pltpu.VMEM, pl.ANY))
     recv5, sgrad = pl.pallas_call(
         tie_kernel,
-        out_shape=[jax.ShapeDtypeStruct(x.shape, x.dtype) for x in (recv5, sgrad)],
+        out_shape=[jax.ShapeDtypeStruct(x, BF) for x in (chunk, sgrad.shape)],
         in_specs=[vmem, keep_place],
         out_specs=[vmem, keep_place],
         input_output_aliases={1: 1},
@@ -611,6 +618,7 @@
         (core, batch, *mine, *other),
         10,
         smem=2,
+        scratch=[pltpu.VMEM((2, PIECES * C, BLK), BF)],
         flops=1 << 20,
     )
     layer = jnp.transpose(layer, (1, 0, 2))[:, None]

time: 162 us -> 161 us (level)
  no operation moved by 1% of the time
where the time goes in v4:
time: 161 us; the launch traced here: 160 us
  Pallas kernels  59.2 us (37%)
  starting transfers between devices  52 us (32%)
  waiting for transfers between devices  40.8 us (25%)
  local copies, waits for them, and re-layouts  7.24 us (4%)
    pallas_call x11, Pallas kernels, call(): pl.pallas_call(kernel, out_shape=[jax.ShapeDtypeStruct(s, d) for s, d in...  42.6 us
    all_to_all x5, starting transfers between devices, swap(): return lax.all_to_all(x, axis, split_axis=0, concat_axis=0, tiled=True)  39.7 us
    all_to_all x5, waiting for transfers between devices, swap(): return lax.all_to_all(x, axis, split_axis=0, concat_axis=0, tiled=True)  33.1 us
    pallas_call x2, Pallas kernels, stepped(): pl.pallas_call(kernel, grid=(T1,), out_shape=[jax.ShapeDtypeStruct(s, d)...  16.3 us
    ppermute x3, starting transfers between devices, body(): lax.ppermute(parts[k], 'batch', rounds[k])  4.89 us
    ppermute x3, starting transfers between devices, body(): lax.ppermute(recv5, 'batch', rounds[k])  4.75 us
    unnamed x15, local copies, waits for them, and re-layouts  4.24 us
    ppermute x3, waiting for transfers between devices, body(): lax.ppermute(parts[k], 'batch', rounds[k])  4.19 us
  transfers between devices with their start and end apart: 16, of which 12 were waited for; matrix products, arithmetic and copies ran while one was open for 2% of the time, Pallas kernels for 25%

profile of v4, /device:TPU:1, one launch (start us, length us, event | category | flops | bytes accessed | tf_op | source)
XLA Modules:
  0.0 160.0 jit_solution(16094436478907956152)
XLA Ops:
  0.6 2.3 %copy.23 = bf16[512,1,4,256]{3,0,2,1:T(8,128)(2,1)} copy(bf16[512,1,4,256]{3,2,1,0:T(4,128)(2,1)} %param.12) | data formatting | bytes 2097152 | tf_op args[0]
  3.0 5.3 %shard_map.147 = (s32[512,128]{1,0:T(8,128)}, s32[8,512]{1,0:T(8,128)}, bf16[512,768]{1,0:T(8,128)(2,1)}) custom-call(s32[16]{0:T(128)} %trow.3, s32[16]{0:T(128)} %tcol.3, s32[16]{0:T(128)} %tmask.3, s32[1]{0:T(128)} %bitcast.me, s32[8]{0:T(128)} %owners.9, bf16[16,128,128]{2,1,0:T(8,128)(2,1)} %tiles.3, s32[2,64]{1,0:T(2,128)} %bitcast.55, ...), custom_call_target="tpu_custom_call" | custom-call | flops 2147483648 | bytes 8388608 | tf_op jit(solution)/shard_map/pallas_call | solution.py:66
  8.3 13.2 %all-to-all-start = ((bf16[64,8,768]{2,1,0:T(8,128)(2,1)}), bf16[64,8,768]{2,1,0:T(8,128)(2,1)S(1)}, u32[]{:S(2)}, u32[]{:S(2)}) async-start(bf16[64,8,768]{2,1,0:T(8,128)(2,1)} %bitcast.46), calls=%async_computation | async-start | bytes 1572864 | tf_op jit(solution)/shard_map/all_to_all | solution.py:478
  21.4 0.0 copy-start.4
  21.5 6.4 %shard_map.149 = (bf16[512,768]{1,0:T(8,128)(2,1)}, bf16[512,128]{1,0:T(8,128)(2,1)}, bf16[768,512]{1,0:T(8,128)(2,1)}, bf16[3,512,256]{2,1,0:T(8,128)(2,1)}, f3...) custom-call(s32[16]{0:T(128)} %trow.3, s32[16]{0:T(128)} %tcol.3, s32[16]{0:T(128)} %tmask.3, ...), custom_call_target="tpu_custom_call" | custom-call | flops 8589934592 | bytes 8388608 | tf_op jit(solution)/shard_map/pallas_call | solution.py:66
  27.9 16.3 %all-to-all-done = bf16[64,8,768]{2,1,0:T(8,128)(2,1)S(1)} async-done(((bf16[64,8,768]{2,1,0:T(8,128)(2,1)}), bf16[64,8,768]{2,1,0:T(8,128)(2,1)S(1)}, u32[]{:S(2)}, u32[]{:S(2)}) %all-to-all-start) | async-done | bytes 786464 | tf_op jit(solution)/shard_map/all_to_all | solution.py:478
  44.2 0.0 copy-start.1
  44.2 0.0 copy-done.4
  44.2 1.6 %shard_map.148 = bf16[64,8,256]{2,1,0:T(8,128)(2,1)} custom-call(s32[1]{0:T(128)} %bitcast.me, s32[8]{0:T(128)S(1)} %copy-done.4, bf16[512,768]{1,0:T(8,128)(2,1)S(1)} %bitcast.32), custom_call_target="tpu_custom_call" | custom-call | flops 268435456 | bytes 8388608 | tf_op jit(solution)/shard_map/pallas_call | solution.py:66
  45.8 6.2 %all-to-all-start.1 = ((bf16[64,8,256]{2,1,0:T(8,128)(2,1)}), bf16[64,8,256]{2,1,0:T(8,128)(2,1)S(1)}, u32[]{:S(2)}, u32[]{:S(2)}) async-start(bf16[64,8,256]{2,1,0:T(8,128)(2,1)} %shard_map.148), calls=%async_computation.1 | async-start | bytes 524288 | tf_op jit(solution)/shard_map/all_to_all | solution.py:478
  52.1 0.0 copy-done.1
  52.1 6.7 %shard_map.150 = (f32[3,512,256]{2,1,0:T(8,128)}, f32[3,512,256]{2,1,0:T(8,128)}, bf16[4,128,256]{2,1,0:T(8,128)(2,1)}, bf16[4,128,256]{2,1,0:T(8,128)(2,1)}) custom-call(bf16[512,768]{1,0:T(8,128)(2,1)} %bitcast.33, bf16[2,2,256,256]{3,2,1,0:T(8,128)(2,1)} %conv.9, s32[512,128]{1,0:T(8,128)} %get-tuple-element.49.cols, s32[8,512]{1,0:T(8,128)} %get-tuple-element.50.rows, ...), custom_call_target="tpu_custom_call" | custom-call | flops 8589934592 | bytes 8388608 | tf_op jit(solution)/shard_map/pallas_call | solution.py:66
  58.8 6.5 %all-to-all-done.1 = bf16[64,8,256]{2,1,0:T(8,128)(2,1)S(1)} async-done(((bf16[64,8,256]{2,1,0:T(8,128)(2,1)}), bf16[64,8,256]{2,1,0:T(8,128)(2,1)S(1)}, u32[]{:S(2)}, u32[]{:S(2)}) %all-to-all-start.1) | async-done | bytes 262176 | tf_op jit(solution)/shard_map/all_to_all | solution.py:478
  65.2 0.0 copy-start.6
  65.2 0.7 copy-done.6
  65.9 8.0 %shard_map.151 = (bf16[512,768]{1,0:T(8,128)(2,1)}, bf16[3,512,256]{2,1,0:T(8,128)(2,1)}, bf16[3,512,256]{2,1,0:T(8,128)(2,1)}, bf16[3,768,256]{2,1,0:T(8,128)(2...) custom-call(s32[1]{0:T(128)} %bitcast.me, s32[8]{0:T(128)} %owners.9, bf16[512,256]{1,0:T(8,128)(2,1)} %bitcast.47, ...), custom_call_target="tpu_custom_call" | custom-call | flops 4294967296 | bytes 8388608 | tf_op jit(solution)/shard_map/pallas_call | solution.py:86
  73.9 4.7 %all-to-all-start.2 = ((bf16[64,8,768]{2,1,0:T(8,128)(2,1)}), bf16[64,8,768]{2,1,0:T(8,128)(2,1)S(1)}, u32[]{:S(2)}, u32[]{:S(2)}) async-start(bf16[64,8,768]{2,1,0:T(8,128)(2,1)} %bitcast.45), calls=%async_computation.2 | async-start | bytes 1572864 | tf_op jit(solution)/shard_map/all_to_all | solution.py:478
  78.6 8.4 %shard_map.152 = (f32[1792,128]{1,0:T(8,128)}, f32[1792,128]{1,0:T(8,128)}) custom-call(s32[1]{0:T(128)} %bitcast.15.core, bf16[2,2,256,256]{3,2,1,0:T(8,128)(2,1)} %conv.9, bf16[3,256,256]{2,1,0:T(8,128)(2,1)} %mix.7, bf16[3,512,256]{2,1,0:T(8,128)(2,1)} %get-tuple-element.59.hop.hop_ref, bf16[3,512,256]{2,1,0:T(8,128)(2,1)} %bitcast.52, ...), custom_call_target="tpu_custom_call" | custom-call | flops 8589934592 | bytes 8388608 | tf_op jit(solution)/shard_map/pallas_call | solution.py:86
  87.0 0.0 copy-start.5
  87.0 0.7 collective-permute-start
  87.8 2.3 %collective-permute-done.got = f32[1792,128]{1,0:T(8,128)S(1)} collective-permute-done((f32[1792,128]{1,0:T(8,128)}, f32[1792,128]{1,0:T(8,128)S(1)}, u32[]{:S(2)}, u32[]{:S(2)}) %collective-permute-start) | collective-permute-done | bytes 917536 | tf_op jit(solution)/shard_map/ppermute | solution.py:563
  90.1 0.0 copy-start.3
  90.1 1.2 copy-done.3
  91.2 0.2 shard_map.153
  91.4 1.3 collective-permute-start.1
  92.7 2.5 %collective-permute-start.2 = (bf16[448,128]{1,0:T(8,128)(2,1)S(1)}, bf16[448,128]{1,0:T(8,128)(2,1)S(1)}, u32[]{:S(2)}, u32[]{:S(2)}) collective-permute-start(bf16[448,128]{1,0:T(8,128)(2,1)S(1)} %get-tuple-element.71), channel_id=1, source_target_pairs={{0,2},{1,3},{2,0},{3,1},{4,6},{5,7},{6,4},{7,5},{8,10},{9,11},{10,... | collective-permute-start | bytes 344072 | tf_op jit(solution)/shard_map/ppermute | solution.py:568
  95.1 1.2 collective-permute-start.3
  96.3 0.7 collective-permute-done.1.part1
  97.0 3.4 %collective-permute-done.2.part2 = bf16[448,128]{1,0:T(8,128)(2,1)S(1)} collective-permute-done((bf16[448,128]{1,0:T(8,128)(2,1)S(1)}, bf16[448,128]{1,0:T(8,128)(2,1)S(1)}, u32[]{:S(2)}, u32[]{:S(2)}) %collective-permute-start.2) | collective-permute-done | bytes 114720 | tf_op jit(solution)/shard_map/ppermute | solution.py:568
  100.5 0.0 collective-permute-done.3.part3
  100.5 0.9 all-to-all-done.2
  101.4 0.0 copy-start
  101.4 0.0 copy-done.5
  101.4 1.9 %shard_map.154 = bf16[64,8,384]{2,1,0:T(8,128)(2,1)} custom-call(s32[1]{0:T(128)} %bitcast.me, s32[8]{0:T(128)S(1)} %copy-done.5, bf16[512,768]{1,0:T(8,128)(2,1)S(1)} %bitcast.30, bf16[448,128]{1,0:T(8,128)(2,1)S(1)} %get-tuple-element.69.part0, bf16[448,128]{1,0:T(8,128)(2,1)S(1)} %collective-permute-done.1.part1, ...), custom_call_target="tpu_custom_call" | custom-call | flops 268435456 | bytes 8388608 | tf_op jit(solution)/shard_map/pallas_call | solution.py:66
  103.3 10.0 %all-to-all-start.3 = ((bf16[64,8,384]{2,1,0:T(8,128)(2,1)}), bf16[64,8,384]{2,1,0:T(8,128)(2,1)S(1)}, u32[]{:S(2)}, u32[]{:S(2)}) async-start(bf16[64,8,384]{2,1,0:T(8,128)(2,1)} %shard_map.154), calls=%async_computation.3 | async-start | bytes 786432 | tf_op jit(solution)/shard_map/all_to_all | solution.py:478
  113.3 0.0 copy-done
  113.3 8.1 %shard_map.155 = (f32[3,512,256]{2,1,0:T(8,128)}, f32[3,512,256]{2,1,0:T(8,128)}, f32[3,512,256]{2,1,0:T(8,128)}, bf16[3,128,256]{2,1,0:T(8,128)(2,1)}) custom-call(bf16[512,768]{1,0:T(8,128)(2,1)} %bitcast.31, s32[512,128]{1,0:T(8,128)} %get-tuple-element.49.cols, s32[8,512]{1,0:T(8,128)} %get-tuple-element.50.rows, ...), custom_call_target="tpu_custom_call" | custom-call | flops 8589934592 | bytes 8388608 | tf_op jit(solution)/shard_map/pallas_call | solution.py:66
  121.4 7.0 %all-to-all-done.3.recv = bf16[64,8,384]{2,1,0:T(8,128)(2,1)S(1)} async-done(((bf16[64,8,384]{2,1,0:T(8,128)(2,1)}), bf16[64,8,384]{2,1,0:T(8,128)(2,1)S(1)}, u32[]{:S(2)}, u32[]{:S(2)}) %all-to-all-start.3) | async-done | bytes 393248 | tf_op jit(solution)/shard_map/all_to_all | solution.py:478
  128.3 0.0 copy-start.2
  128.3 0.8 shard_map.156
  129.1 5.6 %all-to-all-start.4 = ((bf16[64,8,128]{2,1,0:T(8,128)(2,1)}), bf16[64,8,128]{2,1,0:T(8,128)(2,1)S(1)}, u32[]{:S(2)}, u32[]{:S(2)}) async-start(bf16[64,8,128]{2,1,0:T(8,128)(2,1)} %shard_map.156), calls=%async_computation.4 | async-start | bytes 262144 | tf_op jit(solution)/shard_map/all_to_all | solution.py:478
  134.7 0.0 copy-done.2
  134.7 5.7 %shard_map.157 = bf16[4,512,256]{2,1,0:T(8,128)(2,1)} custom-call(s32[1]{0:T(128)} %bitcast.me, s32[8]{0:T(128)} %owners.9, bf16[512,384]{1,0:T(8,128)(2,1)} %bitcast.34, s32[8,512]{1,0:T(8,128)} %get-tuple-element.50.rows, bf16[3,256,256]{2,1,0:T(8,128)(2,1)} %mix.7, bf16[2,2,256,256]{3,2,1,0:T(8,128)(2,1)} %conv.9, ...), custom_call_target="tpu_custom_call" | custom-call | flops 8589934592 | bytes 8388608 | tf_op jit(solution)/shard_map/pallas_call | solution.py:66
  140.4 3.0 %copy.22 = bf16[4,512,256]{2,0,1:T(4,128)(2,1)} copy(bf16[4,512,256]{2,1,0:T(8,128)(2,1)} %shard_map.157) | data formatting | bytes 2097152 | tf_op jit(solution)/shard_map/pallas_call | solution.py:66
  143.4 2.4 %all-to-all-done.4 = bf16[64,8,128]{2,1,0:T(8,128)(2,1)S(1)} async-done(((bf16[64,8,128]{2,1,0:T(8,128)(2,1)}), bf16[64,8,128]{2,1,0:T(8,128)(2,1)S(1)}, u32[]{:S(2)}, u32[]{:S(2)}) %all-to-all-start.4) | async-done | bytes 131104 | tf_op jit(solution)/shard_map/all_to_all | solution.py:478
  145.8 0.3 shard_map.158
  146.1 1.3 collective-permute-start.4
  147.4 2.1 %collective-permute-start.5 = (bf16[448,128]{1,0:T(8,128)(2,1)S(1)}, bf16[448,128]{1,0:T(8,128)(2,1)S(1)}, u32[]{:S(2)}, u32[]{:S(2)}) collective-permute-start(bf16[448,128]{1,0:T(8,128)(2,1)S(1)} %get-tuple-element.86.refs_0_), channel_id=1, source_target_pairs={{0,2},{1,3},{2,0},{3,1},{4,6},{5,7},{6,4},{7,5},{8,10},{9,11},{10,... | collective-permute-start | bytes 344072 | tf_op jit(solution)/shard_map/ppermute | solution.py:606
  149.5 1.3 collective-permute-start.6
  150.8 4.5 %shard_map.159 = bf16[3,512,256]{2,1,0:T(8,128)(2,1)} custom-call(bf16[512,384]{1,0:T(8,128)(2,1)} %bitcast.35, s32[512,128]{1,0:T(8,128)} %get-tuple-element.49.cols, bf16[512,128]{1,0:T(8,128)(2,1)} %get-tuple-element.55.a_hub, bf16[3,256,256]{2,1,0:T(8,128)(2,1)} %mix.7, bf16[3,128,256]{2,1,0:T(8,128)(2,1)} %get-tuple-element.81.hop_hub, ...), custom_call_target="tpu_custom_call" | custom-call | flops 4294967296 | bytes 8388608 | tf_op jit(solution)/shard_map/pallas_call | solution.py:66
  155.3 0.0 collective-permute-done.4.refs_1_
  155.3 0.0 collective-permute-done.5.refs_2_
  155.3 0.0 collective-permute-done.6.refs_3_
  155.3 1.3 collective-permute-start.7
  156.7 0.1 collective-permute-start.8
  156.8 0.4 collective-permute-start.9
  157.2 0.1 collective-permute-start.10
  157.3 0.4 collective-permute-done.7.refs_4_
  157.6 0.4 collective-permute-done.8.refs_5_
  158.0 0.2 collective-permute-done.9.refs_6_
  158.1 0.3 collective-permute-done.10.refs_7_
  158.5 1.5 shard_map.160
Async XLA Ops:
  8.3 35.9 %all-to-all-start = ((bf16[64,8,768]{2,1,0:T(8,128)(2,1)}), bf16[64,8,768]{2,1,0:T(8,128)(2,1)S(1)}, u32[]{:S(2)}, u32[]{:S(2)}) async-start(bf16[64,8,768]{2,1,0:T(8,128)(2,1)} %bitcast.46), calls=%async_computation | async-start | bytes 1572864 | tf_op jit(solution)/shard_map/all_to_all | solution.py:478
  21.4 22.8 %copy-start.4 = (s32[8]{0:T(128)S(1)}, s32[8]{0:T(128)}, u32[]{:S(2)}) copy-start(s32[8]{0:T(128)} %owners.9) | copy-start | bytes 100
  44.2 7.9 %copy-start.1 = (bf16[64,8,768]{2,1,0:T(8,128)(2,1)}, bf16[64,8,768]{2,1,0:T(8,128)(2,1)S(1)}, u32[]{:S(2)}) copy-start(bf16[64,8,768]{2,1,0:T(8,128)(2,1)S(1)} %all-to-all-done) | copy-start | bytes 2359300
  45.8 19.4 %all-to-all-start.1 = ((bf16[64,8,256]{2,1,0:T(8,128)(2,1)}), bf16[64,8,256]{2,1,0:T(8,128)(2,1)S(1)}, u32[]{:S(2)}, u32[]{:S(2)}) async-start(bf16[64,8,256]{2,1,0:T(8,128)(2,1)} %shard_map.148), calls=%async_computation.1 | async-start | bytes 524288 | tf_op jit(solution)/shard_map/all_to_all | solution.py:478
  65.2 0.7 copy-start.6
  73.9 27.5 %all-to-all-start.2 = ((bf16[64,8,768]{2,1,0:T(8,128)(2,1)}), bf16[64,8,768]{2,1,0:T(8,128)(2,1)S(1)}, u32[]{:S(2)}, u32[]{:S(2)}) async-start(bf16[64,8,768]{2,1,0:T(8,128)(2,1)} %bitcast.45), calls=%async_computation.2 | async-start | bytes 1572864 | tf_op jit(solution)/shard_map/all_to_all | solution.py:478
  87.0 14.4 %copy-start.5 = (s32[8]{0:T(128)S(1)}, s32[8]{0:T(128)}, u32[]{:S(2)}) copy-start(s32[8]{0:T(128)} %owners.9) | copy-start | bytes 100
  87.0 3.0 %collective-permute-start = (f32[1792,128]{1,0:T(8,128)}, f32[1792,128]{1,0:T(8,128)S(1)}, u32[]{:S(2)}, u32[]{:S(2)}) collective-permute-start(f32[1792,128]{1,0:T(8,128)} %get-tuple-element.68), channel_id=1, source_target_pairs={{0,4},{4,0},{8,12},{12,8},{16,20},{20,16},{24,28},{28,24},{32,36},... | collective-permute-start | bytes 2752520 | tf_op jit(solution)/shard_map/ppermute | solution.py:563
  90.1 1.2 copy-start.3
  91.4 5.6 %collective-permute-start.1 = (bf16[448,128]{1,0:T(8,128)(2,1)S(1)}, bf16[448,128]{1,0:T(8,128)(2,1)S(1)}, u32[]{:S(2)}, u32[]{:S(2)}) collective-permute-start(bf16[448,128]{1,0:T(8,128)(2,1)S(1)} %get-tuple-element.70), channel_id=1, source_target_pairs={{0,1},{1,2},{2,3},{3,0},{4,5},{5,6},{6,7},{7,4},{8,9},{9,10},{10,1... | collective-permute-start | bytes 344072 | tf_op jit(solution)/shard_map/ppermute | solution.py:568
  92.7 7.8 %collective-permute-start.2 = (bf16[448,128]{1,0:T(8,128)(2,1)S(1)}, bf16[448,128]{1,0:T(8,128)(2,1)S(1)}, u32[]{:S(2)}, u32[]{:S(2)}) collective-permute-start(bf16[448,128]{1,0:T(8,128)(2,1)S(1)} %get-tuple-element.71), channel_id=1, source_target_pairs={{0,2},{1,3},{2,0},{3,1},{4,6},{5,7},{6,4},{7,5},{8,10},{9,11},{10,... | collective-permute-start | bytes 344072 | tf_op jit(solution)/shard_map/ppermute | solution.py:568
  95.1 5.4 %collective-permute-start.3 = (bf16[448,128]{1,0:T(8,128)(2,1)S(1)}, bf16[448,128]{1,0:T(8,128)(2,1)S(1)}, u32[]{:S(2)}, u32[]{:S(2)}) collective-permute-start(bf16[448,128]{1,0:T(8,128)(2,1)S(1)} %get-tuple-element.72), channel_id=1, source_target_pairs={{0,3},{1,0},{2,1},{3,2},{4,7},{5,4},{6,5},{7,6},{8,11},{9,8},{10,9... | collective-permute-start | bytes 344072 | tf_op jit(solution)/shard_map/ppermute | solution.py:568
  101.4 11.9 %copy-start = (bf16[64,8,768]{2,1,0:T(8,128)(2,1)}, bf16[64,8,768]{2,1,0:T(8,128)(2,1)S(1)}, u32[]{:S(2)}) copy-start(bf16[64,8,768]{2,1,0:T(8,128)(2,1)S(1)} %all-to-all-done.2) | copy-start | bytes 2359300
  103.3 25.1 %all-to-all-start.3 = ((bf16[64,8,384]{2,1,0:T(8,128)(2,1)}), bf16[64,8,384]{2,1,0:T(8,128)(2,1)S(1)}, u32[]{:S(2)}, u32[]{:S(2)}) async-start(bf16[64,8,384]{2,1,0:T(8,128)(2,1)} %shard_map.154), calls=%async_computation.3 | async-start | bytes 786432 | tf_op jit(solution)/shard_map/all_to_all | solution.py:478
  128.3 6.4 %copy-start.2 = (bf16[64,8,384]{2,1,0:T(8,128)(2,1)}, bf16[64,8,384]{2,1,0:T(8,128)(2,1)S(1)}, u32[]{:S(2)}) copy-start(bf16[64,8,384]{2,1,0:T(8,128)(2,1)S(1)} %all-to-all-done.3.recv) | copy-start | bytes 1179652
  129.1 16.7 %all-to-all-start.4 = ((bf16[64,8,128]{2,1,0:T(8,128)(2,1)}), bf16[64,8,128]{2,1,0:T(8,128)(2,1)S(1)}, u32[]{:S(2)}, u32[]{:S(2)}) async-start(bf16[64,8,128]{2,1,0:T(8,128)(2,1)} %shard_map.156), calls=%async_computation.4 | async-start | bytes 262144 | tf_op jit(solution)/shard_map/all_to_all | solution.py:478
  146.1 9.2 %collective-permute-start.4 = (bf16[448,128]{1,0:T(8,128)(2,1)S(1)}, bf16[448,128]{1,0:T(8,128)(2,1)S(1)}, u32[]{:S(2)}, u32[]{:S(2)}) collective-permute-start(bf16[448,128]{1,0:T(8,128)(2,1)S(1)} %get-tuple-element.86.refs_0_), channel_id=1, source_target_pairs={{0,1},{1,2},{2,3},{3,0},{4,5},{5,6},{6,7},{7,4},{8,9},{9,10},{10,1... | collective-permute-start | bytes 344072 | tf_op jit(solution)/shard_map/ppermute | solution.py:606
  147.4 7.9 %collective-permute-start.5 = (bf16[448,128]{1,0:T(8,128)(2,1)S(1)}, bf16[448,128]{1,0:T(8,128)(2,1)S(1)}, u32[]{:S(2)}, u32[]{:S(2)}) collective-permute-start(bf16[448,128]{1,0:T(8,128)(2,1)S(1)} %get-tuple-element.86.refs_0_), channel_id=1, source_target_pairs={{0,2},{1,3},{2,0},{3,1},{4,6},{5,7},{6,4},{7,5},{8,10},{9,11},{10,... | collective-permute-start | bytes 344072 | tf_op jit(solution)/shard_map/ppermute | solution.py:606
  149.5 5.8 %collective-permute-start.6 = (bf16[448,128]{1,0:T(8,128)(2,1)S(1)}, bf16[448,128]{1,0:T(8,128)(2,1)S(1)}, u32[]{:S(2)}, u32[]{:S(2)}) collective-permute-start(bf16[448,128]{1,0:T(8,128)(2,1)S(1)} %get-tuple-element.86.refs_0_), channel_id=1, source_target_pairs={{0,3},{1,0},{2,1},{3,2},{4,7},{5,4},{6,5},{7,6},{8,11},{9,8},{10,9... | collective-permute-start | bytes 344072 | tf_op jit(solution)/shard_map/ppermute | solution.py:606
  155.3 2.3 %collective-permute-start.7 = (bf16[448,128]{1,0:T(8,128)(2,1)S(1)}, bf16[448,128]{1,0:T(8,128)(2,1)S(1)}, u32[]{:S(2)}, u32[]{:S(2)}) collective-permute-start(bf16[448,128]{1,0:T(8,128)(2,1)S(1)} %get-tuple-element.86.refs_0_), channel_id=1, source_target_pairs={{0,4},{4,0},{8,12},{12,8},{16,20},{20,16},{24,28},{28,24},{32,36},... | collective-permute-start | bytes 344072 | tf_op jit(solution)/shard_map/ppermute | solution.py:614
  156.7 1.3 collective-permute-start.8
  156.8 1.4 collective-permute-start.9
  157.2 1.3 collective-permute-start.10

commit v5 on v4

--- a/solution.py
+++ b/solution.py
@@ -417,22 +417,27 @@
 
 
 def signal_kernel(
-    me, owners, recv, rows, mix, conv, gh_ref, fac_f, fac_g, cot, sgrad
-):
+    me, owners, recv, rows, mix, conv, gh_ref, fac_f, fac_g, cot, sgrad, carried
+):
+    t = pl.program_id(0)
+
+    @pl.when(t == 0)
+    def _():
+        carried[...] = jnp.zeros_like(carried)
+
     mine, target = own_hub_block(me, owners, rows, recv)
-    for t in range(T1):
-        back = nn(put_step(target, t), mine).astype(BF)
-        gh = gh_ref[t] + nt(back, mix[2])
-        gf = (gh * fac_f[t]).astype(BF)
-        gg = (gh * fac_g[t]).astype(BF)
-        early = nt(gf, conv[0, 0]) + nt(gg, conv[1, 0])
-        late = nt(gf, conv[0, 1]) + nt(gg, conv[1, 1]) + cot[t].astype(F32)
-        if t == 0:
-            sgrad[0] = early.astype(BF)
-        else:
-            sgrad[t] = (early + carried).astype(BF)
-        carried = late
-    sgrad[T1] = carried.astype(BF)
+    back = nn(put_step(target, t), mine).astype(BF)
+    gh = gh_ref[0] + nt(back, mix[2])
+    gf = (gh * fac_f[0]).astype(BF)
+    gg = (gh * fac_g[0]).astype(BF)
+    early = nt(gf, conv[0, 0]) + nt(gg, conv[1, 0])
+    late = nt(gf, conv[0, 1]) + nt(gg, conv[1, 1]) + cot[0].astype(F32)
+    sgrad[t] = (early + carried[...]).astype(BF)
+    carried[...] = late
+
+    @pl.when(t == T1 - 1)
+    def _():
+        sgrad[T1] = late.astype(BF)
 
 
 def layer_kernel(recv, cols, a_hub, mix, hop_hub, mixed, two_ref, layer):
@@ -586,11 +591,14 @@
     (send5,) = call(spread_kernel, [((DOM, 8, BLK), BF)], (recv4,), 6, flops=1 << 26)
     recv5 = swap(send5, "dom").reshape(NODE, BLK)
     recv4 = recv4.reshape(NODE, C + BLK)
-    (sgrad,) = call(
+    (sgrad,) = stepped(
         signal_kernel,
         [((HIST, NODE, C), BF)],
         (me, hub_owner, recv4, rows, mix, conv, gh, fac_f, fac_g, cot),
+        ("all", "all", "all", "all", "this", "this", "this", "this"),
+        ("all",),
         smem=2,
+        scratch=[pltpu.VMEM((NODE, C), F32)],
         flops=8 << 30,
     )
     sgrad = jnp.transpose(sgrad, (1, 0, 2))
@@ -603,6 +611,7 @@
         input_output_aliases={1: 1},
         compiler_params=pltpu.CompilerParams(vmem_limit_bytes=4 << 20),
     )(recv5, sgrad)
+    first_swap = lax.ppermute(recv5, "dom", pairs)
     mine = [recv5] + [lax.ppermute(recv5, "batch", rounds[k]) for k in range(1, BATCH)]
     (layer,) = call(
         layer_kernel,
@@ -611,7 +620,7 @@
         flops=4 << 30,
     )
     mine, layer = lax.optimization_barrier((mine, layer))
-    other = [lax.ppermute(one, "dom", pairs) for one in mine]
+    other = [first_swap] + [lax.ppermute(one, "dom", pairs) for one in mine[1:]]
     conv_grad, mix_grad = call(
         scale_kernel,
         [((4, C, C), F32), ((3, C, C), F32)],

time: 161 us -> 161 us (level)
    pallas_call x2 -> x3, Pallas kernels: 16.3 us -> 22.3 us  [stepped(): pl.pallas_call(kernel, grid=(T1,), out_shape=[jax.ShapeDtypeStruct(s, d)...]
    pallas_call x11 -> x10, Pallas kernels: 42.6 us -> 36.9 us  [call(): pl.pallas_call(kernel, out_shape=[jax.ShapeDtypeStruct(s, d) for s, d in...]
where the time goes in v5:
time: 161 us; the launch traced here: 160 us
  Pallas kernels  59.5 us (37%)
  starting transfers between devices  51.7 us (32%)
  waiting for transfers between devices  40.6 us (25%)
  local copies, waits for them, and re-layouts  7.24 us (4%)
    all_to_all x5, starting transfers between devices, swap(): return lax.all_to_all(x, axis, split_axis=0, concat_axis=0, tiled=True)  39.7 us
    pallas_call x10, Pallas kernels, call(): pl.pallas_call(kernel, out_shape=[jax.ShapeDtypeStruct(s, d) for s, d in...  36.9 us
    all_to_all x5, waiting for transfers between devices, swap(): return lax.all_to_all(x, axis, split_axis=0, concat_axis=0, tiled=True)  32.8 us
    pallas_call x3, Pallas kernels, stepped(): pl.pallas_call(kernel, grid=(T1,), out_shape=[jax.ShapeDtypeStruct(s, d)...  22.3 us
    ppermute x3, starting transfers between devices, body(): lax.ppermute(parts[k], 'batch', rounds[k])  4.89 us
    ppermute x3, starting transfers between devices, body(): lax.ppermute(recv5, 'batch', rounds[k])  4.52 us
    unnamed x15, local copies, waits for them, and re-layouts  4.24 us
    ppermute x3, waiting for transfers between devices, body(): lax.ppermute(parts[k], 'batch', rounds[k])  4.2 us
  transfers between devices with their start and end apart: 16, of which 12 were waited for; matrix products, arithmetic and copies ran while one was open for 2% of the time, Pallas kernels for 25%

profile of v5, /device:TPU:1, one launch (start us, length us, event | category | flops | bytes accessed | tf_op | source)
XLA Modules:
  0.0 159.8 jit_solution(13781449197798455812)
XLA Ops:
  0.6 2.3 %copy.23 = bf16[512,1,4,256]{3,0,2,1:T(8,128)(2,1)} copy(bf16[512,1,4,256]{3,2,1,0:T(4,128)(2,1)} %param.12) | data formatting | bytes 2097152 | tf_op args[0]
  3.0 5.3 %shard_map.147 = (s32[512,128]{1,0:T(8,128)}, s32[8,512]{1,0:T(8,128)}, bf16[512,768]{1,0:T(8,128)(2,1)}) custom-call(s32[16]{0:T(128)} %trow.3, s32[16]{0:T(128)} %tcol.3, s32[16]{0:T(128)} %tmask.3, s32[1]{0:T(128)} %bitcast.me, s32[8]{0:T(128)} %owners.9, bf16[16,128,128]{2,1,0:T(8,128)(2,1)} %tiles.3, s32[2,64]{1,0:T(2,128)} %bitcast.55, ...), custom_call_target="tpu_custom_call" | custom-call | flops 2147483648 | bytes 8388608 | tf_op jit(solution)/shard_map/pallas_call | solution.py:66
  8.3 13.1 %all-to-all-start = ((bf16[64,8,768]{2,1,0:T(8,128)(2,1)}), bf16[64,8,768]{2,1,0:T(8,128)(2,1)S(1)}, u32[]{:S(2)}, u32[]{:S(2)}) async-start(bf16[64,8,768]{2,1,0:T(8,128)(2,1)} %bitcast.46), calls=%async_computation | async-start | bytes 1572864 | tf_op jit(solution)/shard_map/all_to_all | solution.py:483
  21.4 0.0 copy-start.4
  21.4 6.4 %shard_map.149 = (bf16[512,768]{1,0:T(8,128)(2,1)}, bf16[512,128]{1,0:T(8,128)(2,1)}, bf16[768,512]{1,0:T(8,128)(2,1)}, bf16[3,512,256]{2,1,0:T(8,128)(2,1)}, f3...) custom-call(s32[16]{0:T(128)} %trow.3, s32[16]{0:T(128)} %tcol.3, s32[16]{0:T(128)} %tmask.3, ...), custom_call_target="tpu_custom_call" | custom-call | flops 8589934592 | bytes 8388608 | tf_op jit(solution)/shard_map/pallas_call | solution.py:66
  27.8 16.3 %all-to-all-done = bf16[64,8,768]{2,1,0:T(8,128)(2,1)S(1)} async-done(((bf16[64,8,768]{2,1,0:T(8,128)(2,1)}), bf16[64,8,768]{2,1,0:T(8,128)(2,1)S(1)}, u32[]{:S(2)}, u32[]{:S(2)}) %all-to-all-start) | async-done | bytes 786464 | tf_op jit(solution)/shard_map/all_to_all | solution.py:483
  44.2 0.0 copy-start.1
  44.2 0.0 copy-done.4
  44.2 1.6 %shard_map.148 = bf16[64,8,256]{2,1,0:T(8,128)(2,1)} custom-call(s32[1]{0:T(128)} %bitcast.me, s32[8]{0:T(128)S(1)} %copy-done.4, bf16[512,768]{1,0:T(8,128)(2,1)S(1)} %bitcast.32), custom_call_target="tpu_custom_call" | custom-call | flops 268435456 | bytes 8388608 | tf_op jit(solution)/shard_map/pallas_call | solution.py:66
  45.8 6.2 %all-to-all-start.1 = ((bf16[64,8,256]{2,1,0:T(8,128)(2,1)}), bf16[64,8,256]{2,1,0:T(8,128)(2,1)S(1)}, u32[]{:S(2)}, u32[]{:S(2)}) async-start(bf16[64,8,256]{2,1,0:T(8,128)(2,1)} %shard_map.148), calls=%async_computation.1 | async-start | bytes 524288 | tf_op jit(solution)/shard_map/all_to_all | solution.py:483
  52.0 0.0 copy-done.1
  52.0 6.7 %shard_map.150 = (f32[3,512,256]{2,1,0:T(8,128)}, f32[3,512,256]{2,1,0:T(8,128)}, bf16[4,128,256]{2,1,0:T(8,128)(2,1)}, bf16[4,128,256]{2,1,0:T(8,128)(2,1)}) custom-call(bf16[512,768]{1,0:T(8,128)(2,1)} %bitcast.33, bf16[2,2,256,256]{3,2,1,0:T(8,128)(2,1)} %conv.9, s32[512,128]{1,0:T(8,128)} %get-tuple-element.49.cols, s32[8,512]{1,0:T(8,128)} %get-tuple-element.50.rows, ...), custom_call_target="tpu_custom_call" | custom-call | flops 8589934592 | bytes 8388608 | tf_op jit(solution)/shard_map/pallas_call | solution.py:66
  58.7 6.5 %all-to-all-done.1 = bf16[64,8,256]{2,1,0:T(8,128)(2,1)S(1)} async-done(((bf16[64,8,256]{2,1,0:T(8,128)(2,1)}), bf16[64,8,256]{2,1,0:T(8,128)(2,1)S(1)}, u32[]{:S(2)}, u32[]{:S(2)}) %all-to-all-start.1) | async-done | bytes 262176 | tf_op jit(solution)/shard_map/all_to_all | solution.py:483
  65.2 0.0 copy-start.6
  65.2 0.7 copy-done.6
  65.9 8.0 %shard_map.151 = (bf16[512,768]{1,0:T(8,128)(2,1)}, bf16[3,512,256]{2,1,0:T(8,128)(2,1)}, bf16[3,512,256]{2,1,0:T(8,128)(2,1)}, bf16[3,768,256]{2,1,0:T(8,128)(2...) custom-call(s32[1]{0:T(128)} %bitcast.me, s32[8]{0:T(128)} %owners.9, bf16[512,256]{1,0:T(8,128)(2,1)} %bitcast.47, ...), custom_call_target="tpu_custom_call" | custom-call | flops 4294967296 | bytes 8388608 | tf_op jit(solution)/shard_map/pallas_call | solution.py:86
  73.9 4.7 %all-to-all-start.2 = ((bf16[64,8,768]{2,1,0:T(8,128)(2,1)}), bf16[64,8,768]{2,1,0:T(8,128)(2,1)S(1)}, u32[]{:S(2)}, u32[]{:S(2)}) async-start(bf16[64,8,768]{2,1,0:T(8,128)(2,1)} %bitcast.45), calls=%async_computation.2 | async-start | bytes 1572864 | tf_op jit(solution)/shard_map/all_to_all | solution.py:483
  78.6 8.4 %shard_map.152 = (f32[1792,128]{1,0:T(8,128)}, f32[1792,128]{1,0:T(8,128)}) custom-call(s32[1]{0:T(128)} %bitcast.15.core, bf16[2,2,256,256]{3,2,1,0:T(8,128)(2,1)} %conv.9, bf16[3,256,256]{2,1,0:T(8,128)(2,1)} %mix.7, bf16[3,512,256]{2,1,0:T(8,128)(2,1)} %get-tuple-element.59.hop.hop_ref, bf16[3,512,256]{2,1,0:T(8,128)(2,1)} %bitcast.52, ...), custom_call_target="tpu_custom_call" | custom-call | flops 8589934592 | bytes 8388608 | tf_op jit(solution)/shard_map/pallas_call | solution.py:86
  87.0 0.0 copy-start.5
  87.0 0.7 collective-permute-start
  87.7 2.3 %collective-permute-done.got = f32[1792,128]{1,0:T(8,128)S(1)} collective-permute-done((f32[1792,128]{1,0:T(8,128)}, f32[1792,128]{1,0:T(8,128)S(1)}, u32[]{:S(2)}, u32[]{:S(2)}) %collective-permute-start) | collective-permute-done | bytes 917536 | tf_op jit(solution)/shard_map/ppermute | solution.py:568
  90.0 0.0 copy-start.3
  90.0 1.2 copy-done.3
  91.2 0.2 shard_map.153
  91.4 1.3 collective-permute-start.1
  92.7 2.4 %collective-permute-start.2 = (bf16[448,128]{1,0:T(8,128)(2,1)S(1)}, bf16[448,128]{1,0:T(8,128)(2,1)S(1)}, u32[]{:S(2)}, u32[]{:S(2)}) collective-permute-start(bf16[448,128]{1,0:T(8,128)(2,1)S(1)} %get-tuple-element.71), channel_id=1, source_target_pairs={{0,2},{1,3},{2,0},{3,1},{4,6},{5,7},{6,4},{7,5},{8,10},{9,11},{10,... | collective-permute-start | bytes 344072 | tf_op jit(solution)/shard_map/ppermute | solution.py:573
  95.1 1.2 collective-permute-start.3
  96.3 0.8 collective-permute-done.1.part1
  97.0 3.4 %collective-permute-done.2.part2 = bf16[448,128]{1,0:T(8,128)(2,1)S(1)} collective-permute-done((bf16[448,128]{1,0:T(8,128)(2,1)S(1)}, bf16[448,128]{1,0:T(8,128)(2,1)S(1)}, u32[]{:S(2)}, u32[]{:S(2)}) %collective-permute-start.2) | collective-permute-done | bytes 114720 | tf_op jit(solution)/shard_map/ppermute | solution.py:573
  100.5 0.0 collective-permute-done.3.part3
  100.5 0.9 all-to-all-done.2
  101.4 0.0 copy-start
  101.4 0.0 copy-done.5
  101.4 1.9 %shard_map.154 = bf16[64,8,384]{2,1,0:T(8,128)(2,1)} custom-call(s32[1]{0:T(128)} %bitcast.me, s32[8]{0:T(128)S(1)} %copy-done.5, bf16[512,768]{1,0:T(8,128)(2,1)S(1)} %bitcast.30, bf16[448,128]{1,0:T(8,128)(2,1)S(1)} %get-tuple-element.69.part0, bf16[448,128]{1,0:T(8,128)(2,1)S(1)} %collective-permute-done.1.part1, ...), custom_call_target="tpu_custom_call" | custom-call | flops 268435456 | bytes 8388608 | tf_op jit(solution)/shard_map/pallas_call | solution.py:66
  103.2 10.0 %all-to-all-start.3 = ((bf16[64,8,384]{2,1,0:T(8,128)(2,1)}), bf16[64,8,384]{2,1,0:T(8,128)(2,1)S(1)}, u32[]{:S(2)}, u32[]{:S(2)}) async-start(bf16[64,8,384]{2,1,0:T(8,128)(2,1)} %shard_map.154), calls=%async_computation.3 | async-start | bytes 786432 | tf_op jit(solution)/shard_map/all_to_all | solution.py:483
  113.2 0.0 copy-done
  113.3 8.1 %shard_map.155 = (f32[3,512,256]{2,1,0:T(8,128)}, f32[3,512,256]{2,1,0:T(8,128)}, f32[3,512,256]{2,1,0:T(8,128)}, bf16[3,128,256]{2,1,0:T(8,128)(2,1)}) custom-call(bf16[512,768]{1,0:T(8,128)(2,1)} %bitcast.31, s32[512,128]{1,0:T(8,128)} %get-tuple-element.49.cols, s32[8,512]{1,0:T(8,128)} %get-tuple-element.50.rows, ...), custom_call_target="tpu_custom_call" | custom-call | flops 8589934592 | bytes 8388608 | tf_op jit(solution)/shard_map/pallas_call | solution.py:66
  121.3 7.0 %all-to-all-done.3.recv = bf16[64,8,384]{2,1,0:T(8,128)(2,1)S(1)} async-done(((bf16[64,8,384]{2,1,0:T(8,128)(2,1)}), bf16[64,8,384]{2,1,0:T(8,128)(2,1)S(1)}, u32[]{:S(2)}, u32[]{:S(2)}) %all-to-all-start.3) | async-done | bytes 393248 | tf_op jit(solution)/shard_map/all_to_all | solution.py:483
  128.3 0.0 copy-start.2
  128.3 0.8 shard_map.156
  129.1 5.6 %all-to-all-start.4 = ((bf16[64,8,128]{2,1,0:T(8,128)(2,1)}), bf16[64,8,128]{2,1,0:T(8,128)(2,1)S(1)}, u32[]{:S(2)}, u32[]{:S(2)}) async-start(bf16[64,8,128]{2,1,0:T(8,128)(2,1)} %shard_map.156), calls=%async_computation.4 | async-start | bytes 262144 | tf_op jit(solution)/shard_map/all_to_all | solution.py:483
  134.7 0.0 copy-done.2
  134.7 5.9 %shard_map.157 = bf16[4,512,256]{2,1,0:T(8,128)(2,1)} custom-call(s32[1]{0:T(128)} %bitcast.me, s32[8]{0:T(128)} %owners.9, bf16[512,384]{1,0:T(8,128)(2,1)} %bitcast.34, s32[8,512]{1,0:T(8,128)} %get-tuple-element.50.rows, bf16[3,256,256]{2,1,0:T(8,128)(2,1)} %mix.7, bf16[2,2,256,256]{3,2,1,0:T(8,128)(2,1)} %conv.9, ...), custom_call_target="tpu_custom_call" | custom-call | flops 8589934592 | bytes 8388608 | tf_op jit(solution)/shard_map/pallas_call | solution.py:86
  140.6 3.0 %copy.22 = bf16[4,512,256]{2,0,1:T(4,128)(2,1)} copy(bf16[4,512,256]{2,1,0:T(8,128)(2,1)} %shard_map.157) | data formatting | bytes 2097152 | tf_op jit(solution)/shard_map/pallas_call | solution.py:86
  143.6 2.2 %all-to-all-done.4 = bf16[64,8,128]{2,1,0:T(8,128)(2,1)S(1)} async-done(((bf16[64,8,128]{2,1,0:T(8,128)(2,1)}), bf16[64,8,128]{2,1,0:T(8,128)(2,1)S(1)}, u32[]{:S(2)}, u32[]{:S(2)}) %all-to-all-start.4) | async-done | bytes 131104 | tf_op jit(solution)/shard_map/all_to_all | solution.py:483
  145.8 0.3 shard_map.158
  146.1 1.1 collective-permute-start.4
  147.2 2.1 %collective-permute-start.5 = (bf16[448,128]{1,0:T(8,128)(2,1)S(1)}, bf16[448,128]{1,0:T(8,128)(2,1)S(1)}, u32[]{:S(2)}, u32[]{:S(2)}) collective-permute-start(bf16[448,128]{1,0:T(8,128)(2,1)S(1)} %get-tuple-element.86.refs_0_), channel_id=1, source_target_pairs={{0,2},{1,3},{2,0},{3,1},{4,6},{5,7},{6,4},{7,5},{8,10},{9,11},{10,... | collective-permute-start | bytes 344072 | tf_op jit(solution)/shard_map/ppermute | solution.py:615
  149.3 1.3 collective-permute-start.6
  150.6 4.5 %shard_map.159 = bf16[3,512,256]{2,1,0:T(8,128)(2,1)} custom-call(bf16[512,384]{1,0:T(8,128)(2,1)} %bitcast.35, s32[512,128]{1,0:T(8,128)} %get-tuple-element.49.cols, bf16[512,128]{1,0:T(8,128)(2,1)} %get-tuple-element.55.a_hub, bf16[3,256,256]{2,1,0:T(8,128)(2,1)} %mix.7, bf16[3,128,256]{2,1,0:T(8,128)(2,1)} %get-tuple-element.81.hop_hub, ...), custom_call_target="tpu_custom_call" | custom-call | flops 4294967296 | bytes 8388608 | tf_op jit(solution)/shard_map/pallas_call | solution.py:66
  155.1 1.2 collective-permute-start.7
  156.3 0.0 collective-permute-done.4.refs_1_
  156.3 0.0 collective-permute-done.5.refs_2_
  156.3 0.0 collective-permute-done.6.refs_3_
  156.3 0.1 collective-permute-start.8
  156.4 0.5 collective-permute-start.9
  156.9 0.1 collective-permute-start.10
  157.0 0.3 collective-permute-done.7.refs_4_
  157.3 0.5 collective-permute-done.8.refs_5_
  157.7 0.2 collective-permute-done.9.refs_6_
  157.9 0.3 collective-permute-done.10.refs_7_
  158.2 1.5 shard_map.160
Async XLA Ops:
  8.3 35.9 %all-to-all-start = ((bf16[64,8,768]{2,1,0:T(8,128)(2,1)}), bf16[64,8,768]{2,1,0:T(8,128)(2,1)S(1)}, u32[]{:S(2)}, u32[]{:S(2)}) async-start(bf16[64,8,768]{2,1,0:T(8,128)(2,1)} %bitcast.46), calls=%async_computation | async-start | bytes 1572864 | tf_op jit(solution)/shard_map/all_to_all | solution.py:483
  21.4 22.8 %copy-start.4 = (s32[8]{0:T(128)S(1)}, s32[8]{0:T(128)}, u32[]{:S(2)}) copy-start(s32[8]{0:T(128)} %owners.9) | copy-start | bytes 100
  44.2 7.9 %copy-start.1 = (bf16[64,8,768]{2,1,0:T(8,128)(2,1)}, bf16[64,8,768]{2,1,0:T(8,128)(2,1)S(1)}, u32[]{:S(2)}) copy-start(bf16[64,8,768]{2,1,0:T(8,128)(2,1)S(1)} %all-to-all-done) | copy-start | bytes 2359300
  45.8 19.4 %all-to-all-start.1 = ((bf16[64,8,256]{2,1,0:T(8,128)(2,1)}), bf16[64,8,256]{2,1,0:T(8,128)(2,1)S(1)}, u32[]{:S(2)}, u32[]{:S(2)}) async-start(bf16[64,8,256]{2,1,0:T(8,128)(2,1)} %shard_map.148), calls=%async_computation.1 | async-start | bytes 524288 | tf_op jit(solution)/shard_map/all_to_all | solution.py:483
  65.2 0.7 copy-start.6
  73.9 27.5 %all-to-all-start.2 = ((bf16[64,8,768]{2,1,0:T(8,128)(2,1)}), bf16[64,8,768]{2,1,0:T(8,128)(2,1)S(1)}, u32[]{:S(2)}, u32[]{:S(2)}) async-start(bf16[64,8,768]{2,1,0:T(8,128)(2,1)} %bitcast.45), calls=%async_computation.2 | async-start | bytes 1572864 | tf_op jit(solution)/shard_map/all_to_all | solution.py:483
  87.0 14.4 %copy-start.5 = (s32[8]{0:T(128)S(1)}, s32[8]{0:T(128)}, u32[]{:S(2)}) copy-start(s32[8]{0:T(128)} %owners.9) | copy-start | bytes 100
  87.0 3.0 %collective-permute-start = (f32[1792,128]{1,0:T(8,128)}, f32[1792,128]{1,0:T(8,128)S(1)}, u32[]{:S(2)}, u32[]{:S(2)}) collective-permute-start(f32[1792,128]{1,0:T(8,128)} %get-tuple-element.68), channel_id=1, source_target_pairs={{0,4},{4,0},{8,12},{12,8},{16,20},{20,16},{24,28},{28,24},{32,36},... | collective-permute-start | bytes 2752520 | tf_op jit(solution)/shard_map/ppermute | solution.py:568
  90.0 1.2 copy-start.3
  91.4 5.6 %collective-permute-start.1 = (bf16[448,128]{1,0:T(8,128)(2,1)S(1)}, bf16[448,128]{1,0:T(8,128)(2,1)S(1)}, u32[]{:S(2)}, u32[]{:S(2)}) collective-permute-start(bf16[448,128]{1,0:T(8,128)(2,1)S(1)} %get-tuple-element.70), channel_id=1, source_target_pairs={{0,1},{1,2},{2,3},{3,0},{4,5},{5,6},{6,7},{7,4},{8,9},{9,10},{10,1... | collective-permute-start | bytes 344072 | tf_op jit(solution)/shard_map/ppermute | solution.py:573
  92.7 7.8 %collective-permute-start.2 = (bf16[448,128]{1,0:T(8,128)(2,1)S(1)}, bf16[448,128]{1,0:T(8,128)(2,1)S(1)}, u32[]{:S(2)}, u32[]{:S(2)}) collective-permute-start(bf16[448,128]{1,0:T(8,128)(2,1)S(1)} %get-tuple-element.71), channel_id=1, source_target_pairs={{0,2},{1,3},{2,0},{3,1},{4,6},{5,7},{6,4},{7,5},{8,10},{9,11},{10,... | collective-permute-start | bytes 344072 | tf_op jit(solution)/shard_map/ppermute | solution.py:573
  95.1 5.4 %collective-permute-start.3 = (bf16[448,128]{1,0:T(8,128)(2,1)S(1)}, bf16[448,128]{1,0:T(8,128)(2,1)S(1)}, u32[]{:S(2)}, u32[]{:S(2)}) collective-permute-start(bf16[448,128]{1,0:T(8,128)(2,1)S(1)} %get-tuple-element.72), channel_id=1, source_target_pairs={{0,3},{1,0},{2,1},{3,2},{4,7},{5,4},{6,5},{7,6},{8,11},{9,8},{10,9... | collective-permute-start | bytes 344072 | tf_op jit(solution)/shard_map/ppermute | solution.py:573
  101.4 11.9 %copy-start = (bf16[64,8,768]{2,1,0:T(8,128)(2,1)}, bf16[64,8,768]{2,1,0:T(8,128)(2,1)S(1)}, u32[]{:S(2)}) copy-start(bf16[64,8,768]{2,1,0:T(8,128)(2,1)S(1)} %all-to-all-done.2) | copy-start | bytes 2359300
  103.2 25.1 %all-to-all-start.3 = ((bf16[64,8,384]{2,1,0:T(8,128)(2,1)}), bf16[64,8,384]{2,1,0:T(8,128)(2,1)S(1)}, u32[]{:S(2)}, u32[]{:S(2)}) async-start(bf16[64,8,384]{2,1,0:T(8,128)(2,1)} %shard_map.154), calls=%async_computation.3 | async-start | bytes 786432 | tf_op jit(solution)/shard_map/all_to_all | solution.py:483
  128.3 6.4 %copy-start.2 = (bf16[64,8,384]{2,1,0:T(8,128)(2,1)}, bf16[64,8,384]{2,1,0:T(8,128)(2,1)S(1)}, u32[]{:S(2)}) copy-start(bf16[64,8,384]{2,1,0:T(8,128)(2,1)S(1)} %all-to-all-done.3.recv) | copy-start | bytes 1179652
  129.1 16.7 %all-to-all-start.4 = ((bf16[64,8,128]{2,1,0:T(8,128)(2,1)}), bf16[64,8,128]{2,1,0:T(8,128)(2,1)S(1)}, u32[]{:S(2)}, u32[]{:S(2)}) async-start(bf16[64,8,128]{2,1,0:T(8,128)(2,1)} %shard_map.156), calls=%async_computation.4 | async-start | bytes 262144 | tf_op jit(solution)/shard_map/all_to_all | solution.py:483
  146.1 10.2 %collective-permute-start.4 = (bf16[448,128]{1,0:T(8,128)(2,1)S(1)}, bf16[448,128]{1,0:T(8,128)(2,1)S(1)}, u32[]{:S(2)}, u32[]{:S(2)}) collective-permute-start(bf16[448,128]{1,0:T(8,128)(2,1)S(1)} %get-tuple-element.86.refs_0_), channel_id=1, source_target_pairs={{0,1},{1,2},{2,3},{3,0},{4,5},{5,6},{6,7},{7,4},{8,9},{9,10},{10,1... | collective-permute-start | bytes 344072 | tf_op jit(solution)/shard_map/ppermute | solution.py:615
  147.2 9.1 %collective-permute-start.5 = (bf16[448,128]{1,0:T(8,128)(2,1)S(1)}, bf16[448,128]{1,0:T(8,128)(2,1)S(1)}, u32[]{:S(2)}, u32[]{:S(2)}) collective-permute-start(bf16[448,128]{1,0:T(8,128)(2,1)S(1)} %get-tuple-element.86.refs_0_), channel_id=1, source_target_pairs={{0,2},{1,3},{2,0},{3,1},{4,6},{5,7},{6,4},{7,5},{8,10},{9,11},{10,... | collective-permute-start | bytes 344072 | tf_op jit(solution)/shard_map/ppermute | solution.py:615
  149.3 7.0 %collective-permute-start.6 = (bf16[448,128]{1,0:T(8,128)(2,1)S(1)}, bf16[448,128]{1,0:T(8,128)(2,1)S(1)}, u32[]{:S(2)}, u32[]{:S(2)}) collective-permute-start(bf16[448,128]{1,0:T(8,128)(2,1)S(1)} %get-tuple-element.86.refs_0_), channel_id=1, source_target_pairs={{0,3},{1,0},{2,1},{3,2},{4,7},{5,4},{6,5},{7,6},{8,11},{9,8},{10,9... | collective-permute-start | bytes 344072 | tf_op jit(solution)/shard_map/ppermute | solution.py:615
  155.1 2.2 %collective-permute-start.7 = (bf16[448,128]{1,0:T(8,128)(2,1)S(1)}, bf16[448,128]{1,0:T(8,128)(2,1)S(1)}, u32[]{:S(2)}, u32[]{:S(2)}) collective-permute-start(bf16[448,128]{1,0:T(8,128)(2,1)S(1)} %get-tuple-element.86.refs_0_), channel_id=1, source_target_pairs={{0,4},{4,0},{8,12},{12,8},{16,20},{20,16},{24,28},{28,24},{32,36},... | collective-permute-start | bytes 344072 | tf_op jit(solution)/shard_map/ppermute | solution.py:614
  156.3 1.4 collective-permute-start.8
  156.4 1.5 collective-permute-start.9
  156.9 1.3 collective-permute-start.10
